TPU v7x, 32 devices: a whole 2x2x4 slice. The times are simulated.
32 devices in a mesh: section: 2 (over core), dp: 8 (over z, y), mp: 2 (over x).
Axes of the slice: x: 2, y: 2, z: 4, core: 2. Of those that a mesh axis runs over, the one named last changes fastest.
Arguments:
- word_state: bfloat16 [2, 32, 20, 768], P(None, 'dp'), may hold values from -6 to 6
- region_state: bfloat16 [2, 32, 36, 768], P(None, 'dp'), may hold values from -6 to 6
- word_lengths: int32 [2, 32], P(None, 'dp'), may hold values from 5 to 20
- region_counts: int32 [2, 32], P(None, 'dp'), may hold values from 10 to 36
- word_cotangent: bfloat16 [2, 32, 20, 768], P(None, 'dp'), may hold values from -6 to 6
- region_cotangent: bfloat16 [2, 32, 36, 768], P(None, 'dp'), may hold values from -6 to 6
- cross_in: bfloat16 [768, 3, 768], P(None, None, 'mp'), may hold values from -0.21875 to 0.21875
- cross_bias: float32 [2, 768], P(None, 'mp'), may hold values from -1 to 1
- cross_out: bfloat16 [768, 768], P('mp'), may hold values from -0.875 to 0.875
- cross_post: float32 [3, 768], replicated
- attention_in: bfloat16 [2, 2, 768, 3, 768], P('section', None, None, None, 'mp'), may hold values from -0.21875 to 0.21875
- attention_bias: float32 [2, 2, 2, 768], P('section', None, None, 'mp'), may hold values from -1 to 1
- attention_out: bfloat16 [2, 2, 768, 768], P('section', None, 'mp'), may hold values from -0.875 to 0.875
- attention_post: float32 [2, 2, 3, 768], P('section')
- feed_in: bfloat16 [2, 2, 768, 3072], P('section', None, None, 'mp'), may hold values from -0.21875 to 0.21875
- feed_bias: float32 [2, 2, 3072], P('section', None, 'mp'), may hold values from -1 to 1
- feed_out: bfloat16 [2, 2, 3072, 768], P('section', None, 'mp'), may hold values from -0.109375 to 0.109375
- feed_post: float32 [2, 2, 3, 768], P('section')
Outputs:
- word_output: bfloat16 [2, 32, 20, 768], P('section', 'dp')
- region_output: bfloat16 [2, 32, 36, 768], P('section', 'dp')
- word_gradient: bfloat16 [2, 32, 20, 768], P('section', 'dp')
- region_gradient: bfloat16 [2, 32, 36, 768], P('section', 'dp')
- cross_in_gradient: float32 [768, 3, 768], P(('section', 'dp'), None, 'mp')
- cross_bias_gradient: float32 [2, 768], P(None, 'mp')
- cross_out_gradient: float32 [768, 768], P('mp', ('section', 'dp'))
- cross_post_gradient: float32 [3, 768], replicated
- attention_in_gradient: float32 [2, 2, 768, 3, 768], P('section', None, 'dp', None, 'mp')
- attention_bias_gradient: float32 [2, 2, 2, 768], P('section', None, None, 'mp')
- attention_out_gradient: float32 [2, 2, 768, 768], P('section', None, 'mp', 'dp')
- attention_post_gradient: float32 [2, 2, 3, 768], P('section')
- feed_in_gradient: float32 [2, 2, 768, 3072], P('section', None, 'dp', 'mp')
- feed_bias_gradient: float32 [2, 2, 3072], P('section', None, 'mp')
- feed_out_gradient: float32 [2, 2, 3072, 768], P('section', None, 'mp', 'dp')
- feed_post_gradient: float32 [2, 2, 3, 768], P('section')
- branch_scales: float32 [2, 8], P('section')
All inputs are finite; a program needn't handle non-finite values.
Results may differ from a plain program's by a relative error of at most 0.039.
Values may be sent and summed in bfloat16 or wider, within the bound.
No kernel may reach another device: no remote copies, remote signals or barrier semaphores. Data moves between devices by JAX's collectives and lax.ppermute only.
A program may use at most 256 MiB of HBM per device.

v0:
```python
from functools import partial

import jax
import jax.numpy as jnp
from jax import lax
from jax.experimental import pallas as pl
from jax.experimental.pallas import tpu as pltpu
from jax.sharding import PartitionSpec as P

D = 768
HALF = D // 2
HEAD_DIM = 64
PAIR = 2 * HEAD_DIM
WORDS = 20
REGIONS = 36
EPS = 1e-06
SCALE = HEAD_DIM**-0.5
COST_SCALE = 0.5
bf16 = jnp.bfloat16
f32 = jnp.float32

ROW_ATT_BIAS, ROW_ATT_POST, ROW_FEED_BIAS, ROW_FEED_POST, SMALL_ROWS = 0, 1, 4, 6, 16


def mm(a, b):
    return jnp.dot(a, b, preferred_element_type=f32)


def mm_nt(a, b):
    return lax.dot_general(a, b, (((1,), (1,)), ((), ())), preferred_element_type=f32)


def mm_tn(a, b):
    return lax.dot_general(a, b, (((0,), (0,)), ((), ())), preferred_element_type=f32)


def norm_of(value, gain, shift):
    centred = value - jnp.mean(value, axis=-1, keepdims=True)
    spread = jnp.mean(centred * centred, axis=-1, keepdims=True)
    rstd = lax.rsqrt(spread + EPS)
    unit = centred * rstd
    return unit, rstd, unit * gain + shift


def norm_back(unit, rstd, gain, incoming):
    scaled = incoming * gain
    mean = jnp.mean(scaled, axis=-1, keepdims=True)
    along = jnp.mean(scaled * unit, axis=-1, keepdims=True)
    return (scaled - mean - unit * along) * rstd


def summed(own, other):
    return own[...].astype(f32) + other[...].astype(f32)


def column_sum(value):
    return jnp.sum(value, axis=0, keepdims=True)


def square_sum(value, valid):
    rows = jnp.sum(value * value, axis=-1, keepdims=True) * valid
    return jnp.broadcast_to(jnp.sum(rows, axis=0, keepdims=True), (1, 128))


def lengths_of(meta, side, batch, item):
    result = jnp.zeros_like(item)
    for i in range(batch):
        result = jnp.where(item == i, meta[1 + side * batch + i], result)
    return result


def row_valid(meta, side, batch, rows):
    index = lax.broadcasted_iota(jnp.int32, (rows, 1), 0)
    length = lengths_of(meta, side, batch, lax.rem(index, batch))
    return (lax.div(index, batch) < length).astype(f32)


def pair_valid(meta, side, batch, rows, keys):
    index = lax.broadcasted_iota(jnp.int32, (1, keys), 1)
    item = lax.rem(index, batch)
    length = lengths_of(meta, side, batch, item)
    item = jnp.where(lax.div(index, batch) < length, item, -1)
    row_item = lax.rem(lax.broadcasted_iota(jnp.int32, (rows, 1), 0), batch)
    return jnp.broadcast_to(row_item, (rows, keys)) == jnp.broadcast_to(item, (rows, keys))


def head_lanes(head):
    lane = lax.broadcasted_iota(jnp.int32, (1, PAIR), 1)
    return (lane // HEAD_DIM) == head


def attend(query, keys, values, valid, probs_ref, context_ref):
    for pair in range(query.shape[1] // PAIR):
        lanes = slice(pair * PAIR, (pair + 1) * PAIR)
        contexts = []
        for head in range(2):
            chosen = query[:, lanes] * head_lanes(head).astype(bf16)
            scores = mm_nt(chosen, keys[:, lanes]) * SCALE
            scores = jnp.where(valid, scores, -1e9)
            shifted = jnp.exp(scores - jnp.max(scores, axis=-1, keepdims=True))
            total = jnp.sum(shifted, axis=-1, keepdims=True)
            probs = (shifted * (1.0 / total)).astype(bf16)
            probs_ref[2 * pair + head] = probs
            contexts.append(mm(probs, values[:, lanes]))
        context_ref[:, lanes] = jnp.where(head_lanes(0), contexts[0], contexts[1]).astype(bf16)


def attend_back(query, keys, values, probs_ref, grad_context, emit):
    first = head_lanes(0)
    for pair in range(query.shape[1] // PAIR):
        lanes = slice(pair * PAIR, (pair + 1) * PAIR)
        grads = ([], [], [])
        for head in range(2):
            probs = probs_ref[2 * pair + head]
            chosen = grad_context[:, lanes] * head_lanes(head).astype(bf16)
            grad_probs = mm_nt(chosen, values[:, lanes])
            wide = probs.astype(f32)
            product = wide * grad_probs
            grad_scores = product - wide * jnp.sum(product, axis=-1, keepdims=True)
            grad_scores = grad_scores.astype(bf16)
            grads[0].append(mm(grad_scores, keys[:, lanes]) * SCALE)
            grads[1].append(mm_tn(grad_scores, query[:, lanes]) * SCALE)
            grads[2].append(mm_tn(probs, grad_context[:, lanes]))
        for kind in range(3):
            emit(kind, lanes, jnp.where(first, grads[kind][0], grads[kind][1]).astype(bf16))


class Fetched:
    def __init__(self, copy, buffer):
        self.copy, self.buffer, self.waited = copy, buffer, False
        self.shape, self.dtype = buffer.shape, buffer.dtype

    def wait(self):
        if not self.waited:
            self.copy.wait()
            self.waited = True
        return self.buffer

    def __getitem__(self, index):
        return self.wait()[index]


class Weights:
    def __init__(self, meta, layer, pairs, buffers, sems):
        self.copies = []
        mine = meta[0] == layer
        at = 0
        for (own, other, pieces), buffer in zip(pairs, buffers):
            copies = []
            for piece in pieces:
                copy = pltpu.make_async_copy(own.at[piece], buffer.at[piece], sems.at[at])
                if other is None:
                    copy.start()
                else:
                    second = pltpu.make_async_copy(
                        other.at[piece], buffer.at[piece], sems.at[at]
                    )
                    pl.when(mine)(copy.start)
                    pl.when(jnp.logical_not(mine))(second.start)
                copies.append(Fetched(copy, buffer))
                at += 1
            self.copies.append(copies)

    def get(self, slot, piece=None):
        copies = self.copies[slot]
        for copy in copies if piece is None else (copies[piece],):
            copy.wait()
        return copies[0].buffer


def maps(own, other, side, pieces=((),)):
    if other is None:
        return own, None, pieces
    return own.at[0, side], other.at[0, side], pieces


ENTRY = ((0,), (1,), (2,))


def column_pieces(size, count):
    return tuple(
        (slice(None), slice(i * size // count, (i + 1) * size // count)) for i in range(count)
    )


def row_pieces(size, count):
    return tuple((slice(i * size // count, (i + 1) * size // count),) for i in range(count))


def call(body, ins, outs, scratch=(), cost=0.0, name=None, ties=(), mib=14):
    spaces = {
        "s": pltpu.SMEM, "v": pltpu.VMEM, "w": pltpu.HBM, "h": pltpu.HBM, "a": pl.ANY, "f": pl.ANY
    }
    ties = [tie if isinstance(tie, tuple) else (tie, "w") for tie in ties]
    extra = [(i, out[5]) for i, out in enumerate(outs) if len(out) > 3 and out[5] is not None]
    aliases = {len(ins) + at: i for at, (i, _) in enumerate(extra)}
    ins = list(ins) + [(array, "w") for _, array in extra]
    places = [out[3:5] if len(out) > 3 else None for out in outs]
    fetched = [i for i, (_, kind) in enumerate(ins) if kind in "hf"]
    written = [i for i, out in enumerate(outs) if out[2] == "h"]
    n_ins, n_ties, n_outs, n_scratch = len(ins), len(ties), len(outs), len(scratch)

    def whole(*refs):
        given = list(refs[:n_ins])
        results = list(refs[n_ins + n_ties : n_ins + n_ties + n_outs])
        rest = refs[n_ins + n_ties + n_outs :]
        own, rest = rest[:n_scratch], rest[n_scratch:]
        buffers, rest = rest[: len(fetched)], rest[len(fetched) :]
        staged, rest = rest[: len(written)], rest[len(written) :]
        sems = rest[0] if rest else None
        for slot, i in enumerate(fetched):
            copy = pltpu.make_async_copy(given[i], buffers[slot], sems.at[slot])
            copy.start()
            given[i] = Fetched(copy, buffers[slot])
        leaving = {}
        for slot, i in enumerate(written):
            target = results[i]
            if places[i] is not None:
                target = target.at[pl.ds(places[i][1], staged[slot].shape[0])]
            copy = pltpu.make_async_copy(staged[slot], target, sems.at[len(fetched) + slot])
            leaving[id(staged[slot])] = copy
            results[i] = staged[slot]
        started = []

        def flush(*done):
            for ref in done:
                copy = leaving.pop(id(ref), None)
                if copy is not None:
                    copy.start()
                    started.append(copy)

        body(flush, *given[: n_ins - len(extra)], *results, *own)
        flush(*[staged[slot] for slot in range(len(written))])
        for copy in started:
            copy.wait()
        for item in given:
            if isinstance(item, Fetched):
                item.wait()

    arrays = [
        pltpu.with_memory_space_constraint(array, spaces[kind]) if kind in "vwh" else array
        for array, kind in [*ins, *ties]
    ]
    own_scratch = list(scratch)
    own_scratch += [pltpu.VMEM(arrays[i].shape, arrays[i].dtype) for i in fetched]
    own_scratch += [pltpu.VMEM(outs[i][0], outs[i][1]) for i in written]
    if fetched or written:
        own_scratch.append(pltpu.SemaphoreType.DMA((len(fetched) + len(written),)))
    return pl.pallas_call(
        whole,
        out_shape=[
            spaces[out[2]]((out[3], *out[0][1:]) if len(out) > 3 else out[0], out[1]) for out in outs
        ],
        in_specs=[pl.BlockSpec(memory_space=spaces[kind]) for _, kind in [*ins, *ties]],
        out_specs=[pl.BlockSpec(memory_space=spaces[out[2]]) for out in outs],
        input_output_aliases=aliases,
        scratch_shapes=own_scratch,
        compiler_params=pltpu.CompilerParams(vmem_limit_bytes=mib * 1024 * 1024),
        cost_estimate=pl.CostEstimate(
            flops=int(cost * COST_SCALE * 1.15e9), bytes_accessed=0, transcendentals=0
        ),
        name=name,
    )(*arrays)


def spans_of(rows):
    return slice(0, rows[0]), slice(rows[0], rows[0] + rows[1])


def select_rows(value, chooser, own_ref, pack_ref):
    moved = mm(value, chooser[...]).astype(bf16)
    own_ref[...] = moved[:, :HALF]
    pack_ref[:, :HALF] = moved[:, HALF:]


def project(low, weights, bias_q, bias_v, qkv_ref):
    qkv_ref[0] = (mm(low, weights.get(0, 0)[0]) + bias_q).astype(bf16)
    qkv_ref[1] = mm(low, weights.get(0, 1)[1]).astype(bf16)
    qkv_ref[2] = (mm(low, weights.get(0, 2)[2]) + bias_v).astype(bf16)


def self_forward(
    side, layer, batch, meta, state, prior, small, chooser, att_in, att_out, place, ties=()
):
    rows = state.shape[0]
    width = att_in[0].shape[-1]
    first = prior is None

    def body(flush, meta, state, *refs):
        refs = list(refs)
        if not first:
            own, other, post = refs[:3]
            refs = refs[3:]
        small, chooser, in_own, in_other, out_own, out_other = refs[:6]
        qkv, probs, selected, pack, part, squares = refs[6:12]
        refs = refs[12:]
        if not first:
            mixed_ref, unit_ref, rstd_ref = refs[:3]
            refs = refs[3:]
        in_buffer, out_buffer, sems = refs
        weights = Weights(
            meta,
            layer,
            (maps(in_own, in_other, side, ENTRY), maps(out_own, out_other, side)),
            (in_buffer, out_buffer),
            sems,
        )
        valid = row_valid(meta, side, batch, rows)
        if first:
            low = state[...]
            squares[...] = square_sum(low.astype(f32), valid)
        else:
            branch = summed(own, other) + post[0:1]
            squares[...] = square_sum(branch, valid)
            unit, rstd, mixed = norm_of(state[...].astype(f32) + branch, post[1:2], post[2:3])
            unit_ref[...] = unit
            rstd_ref[...] = rstd
            mixed_ref[...] = mixed
            low = mixed.astype(bf16)
        select_rows(low, chooser, selected, pack)
        flush(selected)
        biases = small[ROW_ATT_BIAS : ROW_ATT_BIAS + 1]
        project(low, weights, biases[:, :width], biases[:, width : 2 * width], qkv)
        context = pack.at[:, HALF:]
        attend(
            qkv[0], qkv[1], qkv[2], pair_valid(meta, side, batch, rows, rows), probs, context
        )
        flush(qkv, probs, pack)
        part[...] = mm(context[...], weights.get(1)[...]).astype(bf16)

    ins = [(meta, "s"), (state, "v")]
    if not first:
        ins += list(zip(prior, "vvv"))
    ins += [(small, "v"), (chooser, "v")] + list(zip(att_in + att_out, "wawa"))
    outs = [
        ((3, rows, width), bf16, "h"),
        ((width // HEAD_DIM, rows, rows), bf16, "h"),
        ((rows, HALF), bf16, "h"),
        ((rows, HALF + width), bf16, "h", *place),
        ((rows, D), bf16, "v"),
        ((1, 128), f32, "h"),
    ]
    if not first:
        outs += [((rows, D), f32, "v"), ((rows, D), f32, "h"), ((rows, 1), f32, "h")]
    scratch = [
        pltpu.VMEM((3, D, width), bf16),
        pltpu.VMEM((width, D), bf16),
        pltpu.SemaphoreType.DMA((6,)),
    ]
    return call(body, ins, outs, scratch, 4.0, f"self_forward_{layer}_{side}", ties)


def feed_forward(
    side, layer, batch, meta, residual, own, other, small, chooser, feed_in, feed_out, place, ties=()
):
    rows = residual.shape[0]
    units = feed_in[0].shape[-1]
    step = units // 4

    def body(
        flush, meta, residual, own, other, small, chooser, in_own, in_other, out_own, out_other,
        settled_ref, unit_ref, rstd_ref, selected, pack, slope, part, squares,
        in_buffer, out_buffer, sems,
    ):
        weights = Weights(
            meta,
            layer,
            (
                maps(in_own, in_other, side, column_pieces(units, 4)),
                maps(out_own, out_other, side, row_pieces(units, 2)),
            ),
            (in_buffer, out_buffer),
            sems,
        )
        post = small[ROW_ATT_POST : ROW_ATT_POST + 3]
        branch = summed(own, other) + post[0:1]
        squares[...] = square_sum(branch, row_valid(meta, side, batch, rows))
        unit, rstd, settled = norm_of(residual[...].astype(f32) + branch, post[1:2], post[2:3])
        unit_ref[...] = unit
        rstd_ref[...] = rstd
        settled_ref[...] = settled
        low = settled.astype(bf16)
        select_rows(low, chooser, selected, pack)
        flush(unit_ref, rstd_ref, selected)
        for i in range(units // step):
            first = weights.get(0, i)
            columns = slice(i * step, (i + 1) * step)
            row = ROW_FEED_BIAS + (i * step) // D
            place = (i * step) % D
            hidden = mm(low, first[:, columns]) + small[row : row + 1, place : place + step]
            below = 0.5 + 0.5 * lax.erf(hidden * (0.5**0.5))
            density = jnp.exp(hidden * hidden * -0.5) * 0.3989422804014327
            pack[:, HALF + i * step : HALF + (i + 1) * step] = (hidden * below).astype(bf16)
            slope[:, columns] = (below + hidden * density).astype(bf16)
        flush(pack, slope)
        part[...] = mm(pack[:, HALF:], weights.get(1)[...]).astype(bf16)

    ins = [(meta, "s"), (residual, "v"), (own, "v"), (other, "v")]
    ins += [(small, "v"), (chooser, "v")] + list(zip(feed_in + feed_out, "wawa"))
    outs = [
        ((rows, D), f32, "h"),
        ((rows, D), f32, "h"),
        ((rows, 1), f32, "h"),
        ((rows, HALF), bf16, "h"),
        ((rows, HALF + units), bf16, "h", *place),
        ((rows, units), bf16, "h"),
        ((rows, D), bf16, "v"),
        ((1, 128), f32, "h"),
    ]
    scratch = [
        pltpu.VMEM((D, units), bf16),
        pltpu.VMEM((units, D), bf16),
        pltpu.SemaphoreType.DMA((6,)),
    ]
    return call(body, ins, outs, scratch, 4.3, f"feed_forward_{layer}_{side}", ties)


def cross_forward(
    batch, meta, streams, smalls, chooser, cross_in, cross_bias, cross_out, ties=()
):
    rows = [stream[0].shape[0] for stream in streams]
    spans = spans_of(rows)
    width = cross_out.shape[0]
    heads = width // HEAD_DIM

    def body(flush, meta, *refs):
        given = (refs[0:3], refs[3:6])
        small, chooser, in_ref, bias, out_ref = (refs[6:8], *refs[8:12])
        all_pack = refs[28]
        outs = [refs[12:20], refs[20:28]]
        for side in (0, 1):
            outs[side] = outs[side][:5] + (all_pack.at[spans[side]],) + outs[side][5:]
        in_buffer, out_buffer, sems = refs[29:]
        weights = Weights(
            meta,
            0,
            (maps(in_ref, None, 0, ENTRY), maps(out_ref, None, 0)),
            (in_buffer, out_buffer),
            sems,
        )
        lows = []
        for side in (0, 1):
            settled, own, other = given[side]
            state, unit_ref, rstd_ref, squares, selected, pack, qkv, probs, part = outs[side]
            post = small[side][ROW_FEED_POST : ROW_FEED_POST + 3]
            branch = summed(own, other) + post[0:1]
            unit, rstd, result = norm_of(settled[...] + branch, post[1:2], post[2:3])
            unit_ref[...] = unit
            rstd_ref[...] = rstd
            low = result.astype(bf16)
            state[...] = low
            valid = row_valid(meta, side, batch, rows[side])
            squares[0:1] = square_sum(branch, valid)
            squares[1:2] = square_sum(low.astype(f32), valid)
            select_rows(low, chooser, selected, pack)
            flush(unit_ref, rstd_ref, selected)
            lows.append(low)
        for side in (0, 1):
            project(lows[side], weights, bias[0:1], bias[1:2], outs[side][6])
        leave = weights.get(1)
        for side in (0, 1):
            pack, qkv, probs, part = outs[side][5:]
            there = outs[1 - side][6]
            valid = pair_valid(meta, 1 - side, batch, rows[side], rows[1 - side])
            context = pack.at[:, HALF:]
            attend(qkv[0], there[1], there[2], valid, probs, context)
            flush(qkv, probs)
            part[...] = mm(context[...], leave[...]).astype(bf16)

    ins = [(meta, "s")] + [pair for stream in streams for pair in zip(stream, "hvv")]
    ins += [(item, "v") for item in smalls]
    ins += [(chooser, "v"), (cross_in, "w"), (cross_bias, "v"), (cross_out, "w")]
    outs = []
    for side in (0, 1):
        here, there = rows[side], rows[1 - side]
        outs += [
            ((here, D), bf16, "v"),
            ((here, D), f32, "h"),
            ((here, 1), f32, "h"),
            ((2, 128), f32, "h"),
            ((here, HALF), bf16, "h"),
            ((3, here, width), bf16, "h"),
            ((heads, here, there), bf16, "h"),
            ((here, D), bf16, "v"),
        ]
    outs.append(((sum(rows), HALF + width), bf16, "h"))
    scratch = [
        pltpu.VMEM((3, D, width), bf16),
        pltpu.VMEM((width, D), bf16),
        pltpu.SemaphoreType.DMA((6,)),
    ]
    result = call(body, ins, outs, scratch, 6.8, "cross_forward", ties)
    return result[:8], result[8:16], result[16]


def feed_backward(
    layer, batch, meta, tops, joint, small, chooser, slopes, feed_in, feed_out, ties=()
):
    last = joint is None
    rows = [slope.shape[0] for slope in slopes]
    units = slopes[0].shape[1]
    spans, total = spans_of(rows), sum(rows)
    step = units // 4
    n_top = len(tops[0])

    def body(flush, meta, *refs):
        given = (refs[:n_top], refs[n_top : 2 * n_top])
        refs = refs[2 * n_top :]
        if not last:
            joint, refs = refs[:3], refs[3:]
        small, chooser, slopes = refs[:2], refs[2], refs[3:5]
        in_own, in_other, out_own, out_other = refs[5:9]
        grad_all, selected_all, pack_all, part_all, post_all, bias_all = refs[9:15]
        if last:
            results, squares_all = refs[15:17], refs[17]
        in_buffer, out_buffer, sems = refs[-3:]
        weights = [
            Weights(
                meta,
                layer,
                (
                    maps(out_own, out_other, side, row_pieces(units, 4)),
                    maps(in_own, in_other, side, column_pieces(units, 2)),
                ),
                (out_buffer.at[side], in_buffer.at[side]),
                sems.at[side],
            )
            for side in (1, 0)
        ][::-1]
        lows = [None, None]
        for side in (1, 0):
            here = spans[side]
            post = small[side][ROW_FEED_POST : ROW_FEED_POST + 3]
            if last:
                settled, own, other, cotangent = given[side]
                branch = summed(own, other) + post[0:1]
                unit, rstd, result = norm_of(settled[...] + branch, post[1:2], post[2:3])
                low = result.astype(bf16)
                results[side][...] = low
                valid = row_valid(meta, side, batch, rows[side])
                squares_all[side, 0:1] = square_sum(branch, valid)
                squares_all[side, 1:2] = square_sum(low.astype(f32), valid)
                incoming = cotangent[...].astype(f32) * valid
            else:
                unit_ref, rstd_ref = given[side]
                unit, rstd = unit_ref[...], rstd_ref[...]
                incoming = (joint[0][here] + summed_rows(joint[1], joint[2], here)).astype(bf16)
                incoming = incoming.astype(f32)
            grad = norm_back(unit, rstd, post[1:2], incoming)
            grad_all[here] = grad
            low = grad.astype(bf16)
            post_all[side, 0:1] = column_sum(low.astype(f32))
            post_all[side, 1:2] = column_sum(incoming * unit)
            post_all[side, 2:3] = column_sum(incoming)
            lows[side] = low
        for side in (1, 0):
            here = spans[side]
            select_rows(lows[side], chooser, selected_all.at[here], pack_all.at[here])
            for i in range(units // step):
                columns = slice(i * step, (i + 1) * step)
                active = mm_nt(lows[side], weights[side].get(0, i)[columns, :])
                hidden = (active * slopes[side][:, columns].astype(f32)).astype(bf16)
                pack_all[here, HALF + i * step : HALF + (i + 1) * step] = hidden
                bias_all[side, :, columns] = column_sum(hidden.astype(f32))
        flush(pack_all, selected_all)
        for side in (1, 0):
            here = spans[side]
            part_all[here] = mm_nt(pack_all[here, HALF:], weights[side].get(1)[...]).astype(bf16)

    ins = [(meta, "s")] + [pair for top in tops for pair in zip(top, "hfff" if last else "hh")]
    if not last:
        ins += list(zip(joint, "hhf"))
    ins += [(item, "f") for item in small] + [(chooser, "f")] + [(item, "h") for item in slopes]
    ins += list(zip(feed_in + feed_out, "wawa"))
    outs = [
        ((total, D), f32, "h"),
        ((total, HALF), bf16, "h"),
        ((total, HALF + units), bf16, "h"),
        ((total, D), bf16, "h"),
        ((2, 3, D), f32, "h"),
        ((2, 1, units), f32, "h"),
    ]
    if last:
        outs += [((here, D), bf16, "h") for here in rows] + [((2, 2, 128), f32, "h")]
    scratch = [
        pltpu.VMEM((2, D, units), bf16),
        pltpu.VMEM((2, units, D), bf16),
        pltpu.SemaphoreType.DMA((2, 6)),
    ]
    return call(body, ins, outs, scratch, 11.0, f"feed_backward_{layer}", ties, 24)


def summed_rows(own, other, here):
    return own[here].astype(f32) + other[here].astype(f32)


def back_through_norm(top, joint, here, gain, grad_all, post_ref):
    unit_ref, rstd_ref = top
    incoming = joint[0][here] + summed_rows(joint[1], joint[2], here)
    unit = unit_ref[...]
    grad = norm_back(unit, rstd_ref[...], gain, incoming)
    grad_all[here] = grad
    low = grad.astype(bf16)
    post_ref[0:1] = column_sum(low.astype(f32))
    post_ref[1:2] = column_sum(incoming * unit)
    post_ref[2:3] = column_sum(incoming)
    return low


def emit_into(pack, width):
    def emit(kind, lanes, value):
        start = HALF + kind * width + lanes.start
        pack[:, start : start + PAIR] = value

    return emit


def back_to_input(pack, weights, slot, width):
    grads = [pack[:, HALF + j * width : HALF + (j + 1) * width] for j in range(3)]
    total = mm_nt(grads[0], weights.get(slot, 0)[0])
    total += mm_nt(grads[1], weights.get(slot, 1)[1])
    total += mm_nt(grads[2], weights.get(slot, 2)[2])
    return total.astype(bf16)


def self_backward(
    layer, meta, tops, joint, small, chooser, qkvs, probs, att_in, att_out, ties=()
):
    rows = [qkv.shape[1] for qkv in qkvs]
    width = qkvs[0].shape[2]
    spans, total = spans_of(rows), sum(rows)

    def body(flush, meta, *refs):
        tops, joint = (refs[:2], refs[2:4]), refs[4:7]
        small, chooser, qkvs, probs = refs[7:9], refs[9], refs[10:12], refs[12:14]
        in_own, in_other, out_own, out_other = refs[14:18]
        grad_all, selected_all, pack_all, part_all, post_all, bias_all = refs[18:24]
        in_buffer, out_buffer, sems = refs[24:]
        weights = [
            Weights(
                meta,
                layer,
                (maps(out_own, out_other, side), maps(in_own, in_other, side, ENTRY)),
                (out_buffer.at[side], in_buffer.at[side]),
                sems.at[side],
            )
            for side in (1, 0)
        ][::-1]
        for side in (1, 0):
            here = spans[side]
            pack = pack_all.at[here]
            gain = small[side][ROW_ATT_POST + 1 : ROW_ATT_POST + 2]
            low = back_through_norm(tops[side], joint, here, gain, grad_all, post_all.at[side])
            select_rows(low, chooser, selected_all.at[here], pack)
            context = mm_nt(low, weights[side].get(0)[...]).astype(bf16)
            qkv = qkvs[side]
            attend_back(qkv[0], qkv[1], qkv[2], probs[side], context, emit_into(pack, width))
            bias_all[side, 0:1] = column_sum(pack[:, HALF : HALF + width].astype(f32))
            bias_all[side, 1:2] = column_sum(pack[:, HALF + 2 * width :].astype(f32))
        flush(pack_all, selected_all)
        for side in (1, 0):
            here = spans[side]
            part_all[here] = back_to_input(pack_all.at[here], weights[side], 1, width)

    ins = [(meta, "s")] + [(item, "h") for top in tops for item in top]
    ins += list(zip(joint, "hhf"))
    ins += [(item, "f") for item in small] + [(chooser, "f")]
    ins += [(item, "h") for item in (*qkvs, *probs)]
    ins += list(zip(att_in + att_out, "wawa"))
    outs = [
        ((total, D), f32, "h"),
        ((total, HALF), bf16, "h"),
        ((total, HALF + 3 * width), bf16, "h"),
        ((total, D), bf16, "h"),
        ((2, 3, D), f32, "h"),
        ((2, 2, width), f32, "h"),
    ]
    scratch = [
        pltpu.VMEM((2, 3, D, width), bf16),
        pltpu.VMEM((2, width, D), bf16),
        pltpu.SemaphoreType.DMA((2, 6)),
    ]
    return call(body, ins, outs, scratch, 12.0, f"self_backward_{layer}", ties, 18)


def cross_backward(meta, tops, joint, post, chooser, qkvs, probs, cross_in, cross_out, ties=()):
    rows = [qkv.shape[1] for qkv in qkvs]
    width = cross_out.shape[0]
    spans, total = spans_of(rows), sum(rows)

    def body(flush, meta, *refs):
        tops, joint = (refs[:2], refs[2:4]), refs[4:7]
        post, chooser, qkvs, probs = refs[7], refs[8], refs[9:11], refs[11:13]
        in_ref, out_ref = refs[13:15]
        grad_all, selected_all, pack_all, part_all, post_out, bias_out = refs[15:21]
        in_buffer, out_buffer, post_each, sems = refs[21:]
        weights = Weights(
            meta,
            0,
            (maps(out_ref, None, 0), maps(in_ref, None, 0, ENTRY)),
            (out_buffer, in_buffer),
            sems,
        )
        packs = [pack_all.at[here] for here in spans]
        lows = []
        for side in (0, 1):
            here = spans[side]
            low = back_through_norm(
                tops[side], joint, here, post[1:2], grad_all, post_each.at[side]
            )
            select_rows(low, chooser, selected_all.at[here], packs[side])
            lows.append(low)
        post_out[...] = post_each[0] + post_each[1]
        leave = weights.get(0)
        for side in (0, 1):
            context = mm_nt(lows[side], leave[...]).astype(bf16)
            to_here, to_there = emit_into(packs[side], width), emit_into(packs[1 - side], width)

            def emit(kind, lanes, value):
                (to_here if kind == 0 else to_there)(kind, lanes, value)

            attend_back(
                qkvs[side][0], qkvs[1 - side][1], qkvs[1 - side][2], probs[side], context, emit
            )
        bias_out[0:1] = column_sum(pack_all[:, HALF : HALF + width].astype(f32))
        bias_out[1:2] = column_sum(pack_all[:, HALF + 2 * width :].astype(f32))
        flush(pack_all, selected_all)
        part_all[...] = back_to_input(pack_all, weights, 1, width)

    ins = [(meta, "s")] + [(item, "h") for top in tops for item in top]
    ins += list(zip(joint, "hhf"))
    ins += [(post, "f"), (chooser, "f")] + [(a, "h") for a in (*qkvs, *probs)]
    ins += [(cross_in, "w"), (cross_out, "w")]
    outs = [
        ((total, D), f32, "h"),
        ((total, HALF), bf16, "h"),
        ((total, HALF + 3 * width), bf16, "h"),
        ((total, D), bf16, "h"),
        ((3, D), f32, "h"),
        ((2, width), f32, "h"),
    ]
    scratch = [
        pltpu.VMEM((3, D, width), bf16),
        pltpu.VMEM((width, D), bf16),
        pltpu.VMEM((2, 3, D), f32),
        pltpu.SemaphoreType.DMA((6,)),
    ]
    return call(body, ins, outs, scratch, 10.0, "cross_backward", ties, 16)


class Block:
    def __init__(self, in_selected, in_packs, in_gots, out_selected, out_pack, out_got):
        self.parts = [*in_selected, *in_packs, *in_gots, out_selected, out_pack, out_got]
        self.joined = len(in_packs) == 1
        self.kinds = "w" * len(self.parts)
        self.sizes = (out_pack.shape[1] - HALF, in_packs[0].shape[1] - HALF)
        self.rows = [array.shape[0] for array in in_selected]

    def buffers(self):
        return [
            pltpu.VMEM((2 * rows, HALF + size), bf16)
            for rows in self.rows
            for size in (self.sizes[1], self.sizes[0])
        ]

    def fetch(self, refs, buffers, sems, at):
        spans = spans_of(self.rows)
        in_selected, rest = refs[:2], refs[2:]
        if self.joined:
            pack, got, rest = [rest[0]] * 2, [rest[1]] * 2, rest[2:]
        else:
            pack, got, rest = rest[:2], rest[2:4], rest[4:]
        out_selected, out_pack, out_got = rest
        result = []
        for side in (0, 1):
            here, count = spans[side], self.rows[side]
            inner = here if self.joined else slice(0, count)
            per_side = []
            for kind, (selected, own, other, span) in enumerate(
                (
                    (in_selected[side], pack[side].at[inner], got[side].at[inner], None),
                    (out_selected.at[here], out_pack.at[here], out_got.at[here], here),
                )
            ):
                buffer = buffers[2 * side + kind]
                size = buffer.shape[1] - HALF
                mine = slice(0, count)
                copies = [
                    pltpu.make_async_copy(
                        selected, buffer.at[mine, pl.ds(0, HALF)], sems.at[at]
                    ),
                    pltpu.make_async_copy(
                        own.at[:, pl.ds(HALF, size)], buffer.at[mine, pl.ds(HALF, size)], sems.at[at + 1]
                    ),
                    pltpu.make_async_copy(
                        other, buffer.at[slice(count, 2 * count)], sems.at[at + 2]
                    ),
                ]
                at += 3
                for copy in copies:
                    copy.start()
                per_side.append((buffer, copies))
            result.append(per_side)
        return result, at


def chunk_order(groups):
    return [(s, z) for z in range(groups) for s in ((0, 1) if z % 2 == 0 else (1, 0))]


def gradients(blocks, cross, groups, name, ties=()):
    chunk = HALF // groups
    half = chunk // 2
    size = chunk + half if cross else chunk
    order = chunk_order(groups)
    aligned = half % 16 == 0
    width = sum(sum(block.sizes) for block in blocks)
    every = blocks + ([cross] if cross else [])
    n_in = sum(len(block.parts) for block in every)
    n_out = 1 if aligned else 3 if cross else 2
    n_sems = 12 * len(every) + 4 * len(every)

    def body(flush, *refs):
        inputs, outputs, rest = refs[:n_in], refs[n_in : n_in + n_out], list(refs[n_in + n_out :])
        if cross:
            cross_stage = rest.pop()
        stage, sems = rest.pop(), rest.pop()
        at = 0
        fetched = []
        for block in every:
            taken, inputs = inputs[: len(block.parts)], inputs[len(block.parts) :]
            own, rest = rest[:4], rest[4:]
            copies, at = block.fetch(taken, own, sems, at)
            fetched.append(copies)
        waited, leaving = set(), []

        def leave(source, side, columns, at):
            if not aligned:
                copies = [(source, outputs[side].at[:, columns])]
            elif side < 2:
                copies = [
                    (source.at[pl.ds(z * chunk, chunk)], outputs[0].at[pl.ds(k * size, chunk), columns])
                    for k, (s, z) in enumerate(order)
                    if s == side
                ]
            else:
                copies = [
                    (
                        source.at[pl.ds((s * groups + z) * half, half)],
                        outputs[0].at[pl.ds(k * size + chunk, half), columns],
                    )
                    for k, (s, z) in enumerate(order)
                ]
            for one, target in copies:
                copy = pltpu.make_async_copy(one, target, sems.at[at])
                copy.start()
                leaving.append(copy)

        def ready(item):
            buffer, copies = item
            if id(buffer) not in waited:
                waited.add(id(buffer))
                for copy in copies:
                    copy.wait()
            return buffer

        base = 0
        for block, copies in zip(blocks, fetched):
            for side in (0, 1):
                start = base
                for left, right in ((0, 1), (1, 0)):
                    left, right = ready(copies[side][left]), ready(copies[side][right])
                    turned = left[:, :HALF].T
                    span = right.shape[1] - HALF
                    for step in range(0, span, HALF):
                        value = mm(turned, right[:, HALF + step : HALF + step + HALF])
                        stage[side, :, start + step : start + step + HALF] = value.astype(bf16)
                    columns = pl.ds(start, span)
                    leave(stage.at[side, :, columns], side, columns, at)
                    at += 1
                    start += span
            base += sum(block.sizes)
        if cross:
            copies = fetched[-1]
            start = 0
            for left, right in ((0, 1), (1, 0)):
                lefts = [ready(copies[side][left])[:, :HALF].T for side in (0, 1)]
                rights = [ready(copies[side][right]) for side in (0, 1)]
                span = rights[0].shape[1] - HALF
                for step in range(0, span, HALF):
                    columns = slice(HALF + step, HALF + step + HALF)
                    value = mm(lefts[0], rights[0][:, columns]) + mm(lefts[1], rights[1][:, columns])
                    cross_stage[:, start + step : start + step + HALF] = value.astype(bf16)
                columns = pl.ds(start, span)
                leave(cross_stage.at[:, columns], 2, columns, at)
                at += 1
                start += span
        for copy in leaving:
            copy.wait()

    ins = [pair for block in every for pair in zip(block.parts, block.kinds)]
    if aligned:
        outs = [((2 * groups * size, width), bf16, "w")]
    else:
        outs = [((HALF, width), bf16, "w")] * n_out
    scratch = [buffer for block in every for buffer in block.buffers()]
    if cross:
        scratch += [
            pltpu.SemaphoreType.DMA((n_sems,)),
            pltpu.VMEM((2, HALF, width), bf16),
            pltpu.VMEM((HALF, sum(cross.sizes)), bf16),
        ]
    else:
        scratch += [pltpu.SemaphoreType.DMA((n_sems,)), pltpu.VMEM((2, HALF, width), bf16)]
    result = call(body, ins, outs, scratch, 6.0, name, ties, 20)
    if aligned:
        return result[0]
    chunks = [result[side].reshape(groups, chunk, width) for side in (0, 1)]
    pieces = [chunks[s][z] for s, z in order]
    if cross:
        extra = result[2].reshape(2, groups, half, width)
        pieces = [jnp.concatenate([one, extra[s, z]]) for one, (s, z) in zip(pieces, order)]
    return jnp.concatenate(pieces)


def placed_gradients(
    meta, feed1, late1, late_words, layer0, late_regions, chunk, width, units
):
    def body(flush, meta, feed1, late1, words_feed, words_late, layer0, regions, *outs):
        feed_in, feed_out, att_in, att_out, cross_in, cross_out = outs

        def store(side, feed, feed_base, late, late_base):
            feed_in[side] = feed[:, feed_base : feed_base + units].astype(f32)
            feed_out[side] = feed[:, feed_base + units : feed_base + 2 * units].astype(f32)
            for j in range(3):
                start = late_base + j * width
                att_in[side, j] = late[:chunk, start : start + width].astype(f32)
            att_out[side] = late[:chunk, late_base + 3 * width : late_base + 4 * width].astype(f32)

        items = [item.wait() for item in (feed1, late1, words_feed, words_late, layer0, regions)]
        feed1, late1, words_feed, words_late, layer0, regions = items

        @pl.when(meta[0] == 0)
        def _():
            store(0, layer0, 0, layer0, 2 * units)
            store(1, regions, 0, regions, 2 * units)

        @pl.when(meta[0] != 0)
        def _():
            store(0, words_feed, 0, words_late, 0)
            store(1, feed1, 0, late1, 0)

        for j in range(3):
            cross_in[j] = late1[chunk:, j * width : (j + 1) * width].astype(f32)
        cross_out[...] = late1[chunk:, 3 * width :].astype(f32)

    ins = [(meta, "s")]
    ins += [(item, "f") for item in (feed1, late1, *late_words, layer0, late_regions)]
    half = chunk // 2
    outs = [
        ((2, chunk, units), f32, "h"),
        ((2, chunk, units), f32, "h"),
        ((2, 3, chunk, width), f32, "h"),
        ((2, chunk, width), f32, "h"),
        ((3, half, width), f32, "h"),
        ((half, width), f32, "h"),
    ]
    return call(body, ins, outs, (), 4.0, "placed_gradients")


def swap(value, axis, distance=1):
    count = lax.axis_size(axis)
    return lax.ppermute(value, axis, [(i, i ^ distance) for i in range(count)])


def on_device(
    word_state,
    region_state,
    word_lengths,
    region_counts,
    word_cotangent,
    region_cotangent,
    cross_in,
    cross_bias,
    cross_out,
    cross_post,
    attention_in,
    attention_bias,
    attention_out,
    attention_post,
    feed_in,
    feed_bias,
    feed_out,
    feed_post,
):
    section = lax.axis_index("section")
    dp_count = lax.axis_size("dp")
    groups = dp_count // 2
    place = lax.axis_index("dp") % 2
    batch = word_state.shape[1]
    width = cross_out.shape[0]
    units = feed_in.shape[-1]
    both = (0, 1)
    chains = [[s * dp_count + 2 * z + y for s, z in chunk_order(groups)] for y in both]

    def flat(value):
        own = lax.dynamic_index_in_dim(value, section, 0, keepdims=False)
        return own.transpose(1, 0, 2).reshape(-1, D)

    def unflat(value):
        return value.reshape(-1, batch, D).transpose(1, 0, 2)[None]

    def chooser_of(pieces, per_section):
        column = jnp.arange(D)
        half = column // HALF
        inner = column % HALF
        side = jnp.where(half == 0, place, 1 - place)
        size = D // pieces
        if per_section:
            block = inner // (HALF // 2)
            inner = inner % (HALF // 2)
            feature = size * (dp_count * block + 2 * (inner // size) + side) + inner % size
        else:
            feature = size * (2 * (inner // size) + side) + inner % size
        return (jnp.arange(D)[:, None] == feature[None, :]).astype(bf16)

    chooser = chooser_of(dp_count, False)
    cross_chooser = chooser_of(2 * dp_count, True)

    small_own = jnp.concatenate(
        [
            attention_bias[0].reshape(2, 1, D),
            attention_post[0],
            feed_bias[0].reshape(2, -1, D),
            feed_post[0],
            jnp.zeros((2, SMALL_ROWS - 9, D), f32),
        ],
        axis=1,
    )
    small_other = swap(small_own, "section")
    smalls = [jnp.where(section == layer, small_own, small_other) for layer in both]
    small = [[smalls[layer][side] for side in both] for layer in both]
    att_in_own = attention_in.transpose(0, 1, 3, 2, 4)
    att_in = (att_in_own, swap(att_in_own, "section"))
    att_out = (attention_out, swap(attention_out, "section"))
    states = [flat(word_state), flat(region_state)]
    feed_in_later, feed_out_later, *_ = lax.optimization_barrier(
        (feed_in, feed_out, att_in[1], att_out[1], smalls[0], chooser, *states)
    )
    ff_in = (feed_in, swap(feed_in_later, "section"))
    ff_out = (feed_out, swap(feed_out_later, "section"))
    cross_entry = cross_in.transpose(1, 0, 2)

    lengths = [
        lax.dynamic_index_in_dim(value, section, 0, keepdims=False)
        for value in (word_lengths, region_counts)
    ]
    meta = jnp.concatenate([section[None].astype(jnp.int32), *lengths])
    cotangents = [flat(word_cotangent), flat(region_cotangent)]
    rows = [state.shape[0] for state in states]
    total_rows = sum(rows)

    def in_order(step, pack_index, tie=None, joined=True):
        results = [None, None]
        given = None
        for side in (1, 0):
            ties = () if tie is None else (tie,)
            place = (total_rows, rows[0] * side, given) if joined else ()
            results[side] = step(side, place, ties)
            tie, given = results[side][-1], results[side][pack_index]
        return results

    def over_mp(results, index):
        return [swap(results[side][index], "mp") for side in both]

    self0 = in_order(
        lambda side, place, ties: self_forward(
            side, 0, batch, meta, states[side], None, small[0][side], chooser, att_in, att_out,
            place, ties,
        ),
        3,
    )
    got = over_mp(self0, 4)
    feed0 = in_order(
        lambda side, place, ties: feed_forward(
            side, 0, batch, meta, states[side], self0[side][4], got[side], small[0][side], chooser,
            ff_in, ff_out, place, ties,
        ),
        4,
        self0[0][5],
    )
    got = over_mp(feed0, 6)
    self0_there = swap(self0[0][3], "dp")
    cross_w, cross_r, cross_pack = cross_forward(
        batch,
        meta,
        [(feed0[side][0], feed0[side][6], got[side]) for side in both],
        small[0],
        cross_chooser,
        cross_entry,
        cross_bias,
        cross_out,
        [(value, "a") for value in cotangents],
    )
    cross = (cross_w, cross_r)
    got = over_mp(cross, 7)
    feed0_there = swap(feed0[0][4], "dp")
    self1 = in_order(
        lambda side, place, ties: self_forward(
            side, 1, batch, meta, cross[side][0], (cross[side][7], got[side], cross_post),
            small[1][side], chooser, att_in, att_out, place, ties + (self0_there,),
        ),
        3,
    )
    got = over_mp(self1, 4)
    cross_there = swap(cross_pack, "dp")
    feed1 = in_order(
        lambda side, place, ties: feed_forward(
            side, 1, batch, meta, self1[side][6], self1[side][4], got[side], small[1][side], chooser,
            ff_in, ff_out, place, ties + (cross_there if side == 0 else feed0_there,),
        ),
        4,
        self1[0][5],
        False,
    )
    got = over_mp(feed1, 6)
    self1_there = swap(self1[0][3], "dp")
    feed1_there = [swap(feed1[side][4], "dp") for side in both]

    back_feed1 = feed_backward(
        1,
        batch,
        meta,
        [(feed1[side][0], feed1[side][6], got[side], cotangents[side]) for side in both],
        None,
        small[1],
        chooser,
        [feed1[side][5] for side in both],
        ff_in,
        ff_out,
        feed1_there[1:],
    )
    got = swap(back_feed1[3], "mp")
    back_feed1_there = swap(back_feed1[2], "dp")

    def scatter(value):
        return lax.psum_scatter(
            value, ("section", "dp"), scatter_dimension=0, axis_index_groups=chains, tiled=True
        )

    back_self1 = self_backward(
        1,
        meta,
        [feed1[side][1:3] for side in both],
        (back_feed1[0], back_feed1[3], got),
        small[1],
        chooser,
        [self1[side][0] for side in both],
        [self1[side][1] for side in both],
        att_in,
        att_out,
    )
    got = swap(back_self1[3], "mp")
    feed1_grads = gradients(
        [
            Block(
                [feed1[side][3] for side in both],
                [feed1[side][4] for side in both],
                feed1_there,
                *back_feed1[1:3],
                back_feed1_there,
            )
        ],
        None,
        groups,
        "feed_gradients_1",
        (back_self1[5],),
    )
    back_self1_there = swap(back_self1[2], "dp")
    back_cross = cross_backward(
        meta,
        [self1[side][7:9] for side in both],
        (back_self1[0], back_self1[3], got),
        cross_post,
        cross_chooser,
        [cross[side][5] for side in both],
        [cross[side][6] for side in both],
        cross_entry,
        cross_out,
        (feed1_grads, (self1_there, "w")),
    )
    cross_post_grad, cross_bias_grad = back_cross[4:6]
    got = swap(back_cross[3], "mp")
    back_cross_there = swap(back_cross[2], "dp")
    feed1_share = scatter(feed1_grads)

    back_feed0 = feed_backward(
        0,
        batch,
        meta,
        [cross[side][1:3] for side in both],
        (back_cross[0], back_cross[3], got),
        small[0],
        chooser,
        [feed0[side][5] for side in both],
        ff_in,
        ff_out,
        ((back_self1_there, "w"),),
    )
    got = swap(back_feed0[3], "mp")
    back_feed0_there = swap(back_feed0[2], "dp")
    late1_grads = gradients(
        [
            Block(
                [self1[side][2] for side in both],
                [self1[0][3]],
                [self1_there],
                *back_self1[1:3],
                back_self1_there,
            )
        ],
        Block(
            [cross[side][4] for side in both],
            [cross_pack],
            [cross_there],
            *back_cross[1:3],
            back_cross_there,
        ),
        groups,
        "late_gradients_1",
        (back_feed0[5],),
    )
    back_self0 = self_backward(
        0,
        meta,
        [feed0[side][1:3] for side in both],
        (back_feed0[0], back_feed0[3], got),
        small[0],
        chooser,
        [self0[side][0] for side in both],
        [self0[side][1] for side in both],
        att_in,
        att_out,
        (late1_grads,),
    )
    got = swap(back_self0[3], "mp")
    back_self0_there = swap(back_self0[2], "dp")
    late1_grads, feed1_share, back_feed0_there, _ = lax.optimization_barrier(
        (late1_grads, feed1_share, back_feed0_there, back_self0[5])
    )
    late1_share = scatter(late1_grads)
    layer0_grads = gradients(
        [
            Block(
                [feed0[side][3] for side in both],
                [feed0[0][4]],
                [feed0_there],
                *back_feed0[1:3],
                back_feed0_there,
            ),
            Block(
                [self0[side][2] for side in both],
                [self0[0][3]],
                [self0_there],
                *back_self0[1:3],
                back_self0_there,
            ),
        ],
        None,
        groups,
        "gradients_0",
        (back_self0[5],),
    )
    layer0_grads, late1_share = lax.optimization_barrier((layer0_grads, late1_share))
    layer0_share = scatter(layer0_grads)
    chunk = D // dp_count

    state_grad = (back_self0[0] + (back_self0[3].astype(f32) + got.astype(f32))).astype(bf16)
    spans = spans_of(rows)

    def packed(back_self, back_feed, squares):
        rows = [
            back_self[5].reshape(2, D),
            back_self[4].reshape(6, D),
            back_feed[5].reshape(-1, D),
            back_feed[4].reshape(6, D),
        ]
        row = jnp.concatenate([value.reshape(1, 128) for value in squares[:6]], axis=1)
        rest = jnp.concatenate([value.reshape(1, 128) for value in squares[6:]], axis=1)
        rest = jnp.concatenate([rest, jnp.zeros((1, D - rest.shape[1]), f32)], axis=1)
        return jnp.concatenate(rows + [row, rest], axis=0)

    def squares_of(lead, second, tail):
        result = []
        for side in both:
            result += [lead[side], second[side], tail[side][0:1], tail[side][1:2]]
        return result

    packs = [
        packed(
            back_self0,
            back_feed0,
            squares_of(
                [self0[side][5] for side in both],
                [feed0[side][7] for side in both],
                [cross[side][3] for side in both],
            ),
        ),
        packed(
            back_self1,
            back_feed1,
            squares_of(
                [self1[side][5] for side in both],
                [feed1[side][7] for side in both],
                [back_feed1[8][side] for side in both],
            ),
        ),
    ]
    counts = jnp.stack([jnp.sum(word_lengths), jnp.sum(region_counts)]).astype(f32)
    counts = jnp.pad(counts, (0, D - 2))[None] * 0.5
    mine = jnp.where(section == 0, packs[0], packs[1])
    theirs = jnp.where(section == 0, packs[1], packs[0])
    shared = [cross_post_grad, cross_bias_grad.reshape(1, D), counts]
    small_rows = packs[0].shape[0]
    total = jnp.concatenate([mine] + shared, axis=0) + swap(
        jnp.concatenate([theirs] + shared, axis=0), "section"
    )
    distance = 1
    while distance < dp_count:
        total = total + swap(total, "dp", distance)
        distance *= 2
    unit_rows = units // D
    at = 0
    att_bias_grad = total[0:2].reshape(1, 2, 2, width)
    at = 2
    att_post_grad = total[at : at + 6].reshape(1, 2, 3, D)
    at += 6
    feed_bias_grad = total[at : at + 2 * unit_rows].reshape(1, 2, units)
    at += 2 * unit_rows
    feed_post_grad = total[at : at + 6].reshape(1, 2, 3, D)
    at += 6
    squares = total[at : at + 2].reshape(-1, 128)[:8, 0]
    at = small_rows
    cross_post_total = total[at : at + 3]
    cross_bias_total = total[at + 3].reshape(2, width)
    valid_counts = total[at + 4, :2]
    scales = jnp.sqrt(squares / (jnp.repeat(valid_counts, 4) * D))[None]

    late_words = [
        lax.ppermute(value, "section", [(0, 1)]) for value in (feed1_share, late1_share[:chunk])
    ]
    outputs = (
        unflat(back_feed1[6]),
        unflat(back_feed1[7]),
        unflat(state_grad[spans[0]]),
        unflat(state_grad[spans[1]]),
        cross_bias_total,
        cross_post_total,
        att_bias_grad,
        att_post_grad,
        feed_bias_grad,
        feed_post_grad,
        scales,
    )
    layer0_share, late_words, outputs = lax.optimization_barrier((layer0_share, late_words, outputs))
    late_regions = lax.ppermute(layer0_share, "section", [(1, 0)])
    feed_in_grad, feed_out_grad, att_in_grad, att_out_grad, cross_in_grad, cross_out_grad = (
        placed_gradients(
            meta, feed1_share, late1_share, late_words, layer0_share, late_regions, chunk, width, units
        )
    )
    feed_in_grad = feed_in_grad[None]
    feed_out_grad = feed_out_grad.transpose(0, 2, 1)[None]
    att_in_grad = att_in_grad.transpose(0, 2, 1, 3)[None]
    att_out_grad = att_out_grad.transpose(0, 2, 1)[None]
    cross_in_grad = cross_in_grad.transpose(1, 0, 2)
    cross_out_grad = cross_out_grad.T
    return (
        *outputs[:4],
        cross_in_grad,
        outputs[4],
        cross_out_grad,
        outputs[5],
        att_in_grad,
        outputs[6],
        att_out_grad,
        outputs[7],
        feed_in_grad,
        outputs[8],
        feed_out_grad,
        outputs[9],
        outputs[10],
    )


def solution(mesh):
    placed = (
        P(None, "dp", None, None),
        P(None, "dp", None, None),
        P(None, "dp"),
        P(None, "dp"),
        P(None, "dp", None, None),
        P(None, "dp", None, None),
        P(None, None, "mp"),
        P(None, "mp"),
        P("mp", None),
        P(),
        P("section", None, None, None, "mp"),
        P("section", None, None, "mp"),
        P("section", None, "mp", None),
        P("section", None, None, None),
        P("section", None, None, "mp"),
        P("section", None, "mp"),
        P("section", None, "mp", None),
        P("section", None, None, None),
    )
    return jax.shard_map(
        on_device,
        mesh=mesh,
        in_specs=placed,
        out_specs=(
            P("section", "dp", None, None),
            P("section", "dp", None, None),
            P("section", "dp", None, None),
            P("section", "dp", None, None),
            P(("section", "dp"), None, "mp"),
            P(None, "mp"),
            P("mp", ("section", "dp")),
            P(),
            P("section", None, "dp", None, "mp"),
            P("section", None, None, "mp"),
            P("section", None, "mp", "dp"),
            P("section", None, None, None),
            P("section", None, "dp", "mp"),
            P("section", None, "mp"),
            P("section", None, "mp", "dp"),
            P("section", None, None, None),
            P("section", None),
        ),
        check_vma=False,
    )
```

profile of v0, /device:TPU:0, one launch (start us, length us, event | category | flops | bytes accessed | tf_op | source)
XLA Modules:
  0.0 353.0 jit_solution(4094038953189634825)
XLA Ops:
  11.5 2.9 collective-permute-done
  16.5 4.0 %self_forward_0_1.1 = (bf16[3,144,384]{2,1,0:T(8,128)(2,1)}, bf16[6,144,144]{2,1,0:T(8,128)(2,1)}, bf16[144,384]{1,0:T(8,128)(2,1)}, bf16[224,768]{1,0:T(8,128)(...) custom-call(s32[9]{0:T(128)S(1)} %pad_add_fusion.refs_0_, bf16[144,768]{1,0:T(8,128)(2,1)S(1)} %reshape.199.refs_1_, ...), custom_call_target="tpu_custom_call" | custom-call | flops 2300000000 | tf_op jit(solution)/shard_map/self_forward_0_1/pallas_call | solution.py:249
  20.5 2.9 collective-permute-start.6
  24.8 3.6 %self_forward_0_0.1 = (bf16[3,80,384]{2,1,0:T(8,128)(2,1)}, bf16[6,80,80]{2,1,0:T(8,128)(2,1)}, bf16[80,384]{1,0:T(8,128)(2,1)}, bf16[224,768]{1,0:T(8,128)(2,1)...) custom-call(s32[9]{0:T(128)S(1)} %pad_add_fusion.refs_0_, ...), custom_call_target="tpu_custom_call", output_to_operand_aliasing={{3}: (8, {})} | custom-call | flops 2300000000 | tf_op jit(solution)/shard_map/self_forward_0_0/pallas_call | solution.py:249
  29.1 1.5 collective-permute-done.5.refs_9_.refs_17_.refs_16_
  30.7 5.9 %feed_forward_0_1.1 = (f32[144,768]{1,0:T(8,128)}, f32[144,768]{1,0:T(8,128)}, f32[144,1]{1,0:T(8,128)}, bf16[144,384]{1,0:T(8,128)(2,1)}, bf16[224,1920]{1,0:T(...) custom-call(s32[9]{0:T(128)S(1)} %pad_add_fusion.refs_0_, ...), custom_call_target="tpu_custom_call" | custom-call | flops 2472499968 | tf_op jit(solution)/shard_map/feed_forward_0_1/pallas_call | solution.py:249
  36.7 4.5 %feed_forward_0_0.1 = (f32[80,768]{1,0:T(8,128)}, f32[80,768]{1,0:T(8,128)}, f32[80,1]{1,0:T(8,128)}, bf16[80,384]{1,0:T(8,128)(2,1)}, bf16[224,1920]{1,0:T(8,12...) custom-call(s32[9]{0:T(128)S(1)} %pad_add_fusion.refs_0_, ...), custom_call_target="tpu_custom_call", output_to_operand_aliasing={{4}: (10, {})} | custom-call | flops 2472499968 | tf_op jit(solution)/shard_map/feed_forward_0_0/pallas_call | solution.py:249
  41.2 3.0 collective-permute-start.8
  45.0 1.7 reshape.201.refs_14_.refs_8_
  46.7 1.6 dynamic-slice_bitcast_fusion.2
  48.3 1.6 reshape.200.refs_13_.refs_4_
  49.9 2.0 collective-permute-start.12
  56.6 8.9 %cross_forward.1 = (bf16[80,768]{1,0:T(8,128)(2,1)S(1)}, f32[80,768]{1,0:T(8,128)}, f32[80,1]{1,0:T(8,128)}, f32[2,128]{1,0:T(2,128)}, bf16[80,384]{1,0:T(8,128)...) custom-call(s32[9]{0:T(128)S(1)} %pad_add_fusion.refs_0_, ...), custom_call_target="tpu_custom_call" | custom-call | flops 3910000128 | tf_op jit(solution)/shard_map/cross_forward/pallas_call | solution.py:249
  65.5 1.8 collective-permute-start.11
  67.7 5.7 %collective-permute-done.11.refs_3_ = bf16[144,768]{1,0:T(8,128)(2,1)S(1)} collective-permute-done((bf16[144,768]{1,0:T(8,128)(2,1)S(1)}, bf16[144,768]{1,0:T(8,128)(2,1)S(1)}, u32[]{:S(2)}, u32[]{:S(2)}) %collective-permute-start.11) | collective-permute-done | bytes 221216 | tf_op jit(solution)/shard_map/ppermute | solution.py:973
  73.4 4.3 %self_forward_1_1.1 = (bf16[3,144,384]{2,1,0:T(8,128)(2,1)}, bf16[6,144,144]{2,1,0:T(8,128)(2,1)}, bf16[144,384]{1,0:T(8,128)(2,1)}, bf16[224,768]{1,0:T(8,128)(...) custom-call(s32[9]{0:T(128)S(1)} %pad_add_fusion.refs_0_, ...), custom_call_target="tpu_custom_call" | custom-call | flops 2300000000 | tf_op jit(solution)/shard_map/self_forward_1_1/pallas_call | solution.py:249
  79.1 1.5 collective-permute-start.15
  80.7 4.0 %self_forward_1_0.1 = (bf16[3,80,384]{2,1,0:T(8,128)(2,1)}, bf16[6,80,80]{2,1,0:T(8,128)(2,1)}, bf16[80,384]{1,0:T(8,128)(2,1)}, bf16[224,768]{1,0:T(8,128)(2,1)...) custom-call(s32[9]{0:T(128)S(1)} %pad_add_fusion.refs_0_, ...), custom_call_target="tpu_custom_call", output_to_operand_aliasing={{3}: (11, {})} | custom-call | flops 2300000000 | tf_op jit(solution)/shard_map/self_forward_1_0/pallas_call | solution.py:249
  85.6 5.0 %feed_forward_1_1.1 = (f32[144,768]{1,0:T(8,128)}, f32[144,768]{1,0:T(8,128)}, f32[144,1]{1,0:T(8,128)}, bf16[144,384]{1,0:T(8,128)(2,1)}, bf16[144,1920]{1,0:T(...) custom-call(s32[9]{0:T(128)S(1)} %pad_add_fusion.refs_0_, ...), custom_call_target="tpu_custom_call" | custom-call | flops 2472499968 | tf_op jit(solution)/shard_map/feed_forward_1_1/pallas_call | solution.py:249
  93.2 2.9 collective-permute-done.13.refs_3_
  96.8 4.0 %feed_forward_1_0.1 = (f32[80,768]{1,0:T(8,128)}, f32[80,768]{1,0:T(8,128)}, f32[80,1]{1,0:T(8,128)}, bf16[80,384]{1,0:T(8,128)(2,1)}, bf16[80,1920]{1,0:T(8,128...) custom-call(s32[9]{0:T(128)S(1)} %pad_add_fusion.refs_0_, ...), custom_call_target="tpu_custom_call" | custom-call | flops 2472499968 | tf_op jit(solution)/shard_map/feed_forward_1_0/pallas_call | solution.py:249
  100.7 1.5 collective-permute-start.16
  102.3 3.4 collective-permute-done.16.refs_3_
  106.5 12.0 %feed_backward_1.1 = (f32[224,768]{1,0:T(8,128)}, bf16[224,384]{1,0:T(8,128)(2,1)}, bf16[224,1920]{1,0:T(8,128)(2,1)}, bf16[224,768]{1,0:T(8,128)(2,1)}, f32[2,3...) custom-call(s32[9]{0:T(128)S(1)} %pad_add_fusion.refs_0_, ...), custom_call_target="tpu_custom_call" | custom-call | flops 6325000192 | tf_op jit(solution)/shard_map/feed_backward_1/pallas_call | solution.py:249
  118.5 1.5 collective-permute-start.19
  122.1 4.0 %collective-permute-done.19.refs_7_ = bf16[224,768]{1,0:T(8,128)(2,1)S(1)} collective-permute-done((bf16[224,768]{1,0:T(8,128)(2,1)}, bf16[224,768]{1,0:T(8,128)(2,1)S(1)}, u32[]{:S(2)}, u32[]{:S(2)}) %collective-permute-start.19) | collective-permute-done | bytes 344096 | tf_op jit(solution)/shard_map/ppermute | solution.py:973
  126.1 11.5 %self_backward_1.1 = (f32[224,768]{1,0:T(8,128)}, bf16[224,384]{1,0:T(8,128)(2,1)}, bf16[224,1536]{1,0:T(8,128)(2,1)}, bf16[224,768]{1,0:T(8,128)(2,1)}, f32[2,3,768]{2,1,0:T(4,128)}, /*index=5*/f32[2,2,384]{2,1,0:T(2,128)}) custom-call(s32[9]{0:T(128)S(1)} %pad_add_fusion.refs_0_, f32[80,768]{1,0:T(8,128)} %get-tuple-element.193.refs_1_, ...), custom_call_target="tpu_custom_call" | custom-call | flops 6899999744 | tf_op jit(solution)/shard_map/self_backward_1/pallas_call | solution.py:249
  137.6 2.7 collective-permute-done.21.refs_4_
  141.3 5.2 %feed_gradients_1.1.refs_16_ = bf16[768,3072]{1,0:T(8,128)(2,1)} custom-call(bf16[80,384]{1,0:T(8,128)(2,1)} %get-tuple-element.216.refs_0_, bf16[144,384]{1,0:T(8,128)(2,1)} %get-tuple-element.217.refs_1_, bf16[80,1920]{1,0:T(8,128)(2,1)} %get-tuple-element.218.refs_2_, bf16[144,1920]{1,0:T(8,128)(2,1)} %get-tuple-element.203.refs_3_, ...), custom_call_target="tpu_custom_call" | custom-call | flops 3449999872 | tf_op jit(solution)/shard_map/feed_gradients_1/pallas_call | solution.py:249
  149.6 6.2 %collective-permute-done.23.refs_17_.refs_3_ = bf16[224,768]{1,0:T(8,128)(2,1)S(1)} collective-permute-done((bf16[224,768]{1,0:T(8,128)(2,1)}, bf16[224,768]{1,0:T(8,128)(2,1)S(1)}, u32[]{:S(2)}, u32[]{:S(2)}) %collective-permute-start.23) | collective-permute-done | bytes 344096 | tf_op jit(solution)/shard_map/ppermute | solution.py:973
  156.5 9.8 %cross_backward.1 = (f32[224,768]{1,0:T(8,128)}, bf16[224,384]{1,0:T(8,128)(2,1)}, bf16[224,1536]{1,0:T(8,128)(2,1)}, bf16[224,768]{1,0:T(8,128)(2,1)}, f32[3,768]{1,0:T(4,128)}, /*index=5*/f32[2,384]{1,0:T(2,128)}) custom-call(s32[9]{0:T(128)S(1)} %pad_add_fusion.refs_0_, f32[80,768]{1,0:T(8,128)} %get-tuple-element.183.refs_1_, ...), custom_call_target="tpu_custom_call" | custom-call | flops 5750000128 | tf_op jit(solution)/shard_map/cross_backward/pallas_call | solution.py:249
  168.5 5.3 %collective-permute-done.24.refs_7_ = bf16[224,768]{1,0:T(8,128)(2,1)S(1)} collective-permute-done((bf16[224,768]{1,0:T(8,128)(2,1)}, bf16[224,768]{1,0:T(8,128)(2,1)S(1)}, u32[]{:S(2)}, u32[]{:S(2)}) %collective-permute-start.24) | collective-permute-done | bytes 344096 | tf_op jit(solution)/shard_map/ppermute | solution.py:973
  173.9 2.4 copy-done.3
  176.2 2.4 copy-done.5
  178.6 9.4 %feed_backward_0.1 = (f32[224,768]{1,0:T(8,128)}, bf16[224,384]{1,0:T(8,128)(2,1)}, bf16[224,1920]{1,0:T(8,128)(2,1)}, bf16[224,768]{1,0:T(8,128)(2,1)}, f32[2,3,768]{2,1,0:T(4,128)}, /*index=5*/f32[2,1,1536]{2,1,0:T(1,128)}) custom-call(s32[9]{0:T(128)S(1)} %pad_add_fusion.refs_0_, f32[80,768]{1,0:T(8,128)} %get-tuple-element.172.refs_1_, ...), custom_call_target="tpu_custom_call" | custom-call | flops 6325000192 | tf_op jit(solution)/shard_map/feed_backward_0/pallas_call | solution.py:249
  191.1 5.4 %late_gradients_1.1.refs_19_ = bf16[1152,1536]{1,0:T(8,128)(2,1)} custom-call(bf16[80,384]{1,0:T(8,128)(2,1)} %get-tuple-element.230.refs_0_, bf16[144,384]{1,0:T(8,128)(2,1)} %get-tuple-element.231.refs_1_, bf16[224,768]{1,0:T(8,128)(2,1)} %get-tuple-element.222.refs_2_, bf16[224,768]{1,0:T(8,128)(2,1)} %copy-done.63, ...), custom_call_target="tpu_custom_call" | custom-call | flops 3449999872 | tf_op jit(solution)/shard_map/late_gradients_1/pallas_call | solution.py:249
  196.5 11.6 %self_backward_0.1 = (f32[224,768]{1,0:T(8,128)}, bf16[224,384]{1,0:T(8,128)(2,1)}, bf16[224,1536]{1,0:T(8,128)(2,1)}, bf16[224,768]{1,0:T(8,128)(2,1)}, f32[2,3,768]{2,1,0:T(4,128)}, /*index=5*/f32[2,2,384]{2,1,0:T(2,128)}) custom-call(s32[9]{0:T(128)S(1)} %pad_add_fusion.refs_0_, f32[80,768]{1,0:T(8,128)} %get-tuple-element.238.refs_1_, ...), custom_call_target="tpu_custom_call" | custom-call | flops 6899999744 | tf_op jit(solution)/shard_map/self_backward_0/pallas_call | solution.py:249
  210.2 9.9 %collective-permute-done.29.refs_13_ = bf16[224,1536]{1,0:T(8,128)(2,1)S(1)} collective-permute-done((bf16[224,1536]{1,0:T(8,128)(2,1)S(1)}, bf16[224,1536]{1,0:T(8,128)(2,1)S(1)}, u32[]{:S(2)}, u32[]{:S(2)}) %collective-permute-start.29) | collective-permute-done | bytes 688160 | tf_op jit(solution)/shard_map/ppermute | solution.py:973
  221.0 6.7 %gradients_0.1 = bf16[768,4608]{1,0:T(8,128)(2,1)} custom-call(bf16[80,384]{1,0:T(8,128)(2,1)} %get-tuple-element.165.refs_0_, bf16[144,384]{1,0:T(8,128)(2,1)} %get-tuple-element.166.refs_1_, bf16[224,1920]{1,0:T(8,128)(2,1)} %get-tuple-element.167.refs_2_, bf16[224,1920]{1,0:T(8,128)(2,1)} %copy-done.26, bf16[224,384]{1,0:T(8,128)(2,1)} %get-tuple-element.228.refs_4_, ...), custom_call_target="tpu_custom_call" | custom-call | flops 3449999872 | tf_op jit(solution)/shard_map/gradients_0/pallas_call | solution.py:249
  228.0 24.6 %reduce-scatter.6.cloned.1.call-done.refs_2_ = bf16[144,1536]{1,0:T(8,128)(2,1)} async-done(((bf16[1152,1536]{1,0:T(8,128)(2,1)}), bf16[144,1536]{1,0:T(8,128)(2,1)}) %reduce-scatter.6.cloned.1.call-update) | async-done | bytes 442384 | tf_op jit(solution)/shard_map/reduce_scatter | solution.py:1147
  257.7 1.7 collective-permute-start.34
  259.4 3.2 collective-permute-done.34
  262.7 7.1 %collective-permute-done.35 = f32[25,768]{1,0:T(8,128)S(1)} collective-permute-done((f32[25,768]{1,0:T(8,128)S(1)}, f32[25,768]{1,0:T(8,128)S(1)}, u32[]{:S(2)}, u32[]{:S(2)}) %collective-permute-start.35) | collective-permute-done | bytes 76832 | tf_op jit(solution)/shard_map/ppermute | solution.py:973
  272.0 1.8 collective-permute-start.32
  273.7 7.4 %collective-permute-done.36 = f32[25,768]{1,0:T(8,128)S(1)} collective-permute-done((f32[25,768]{1,0:T(8,128)S(1)}, f32[25,768]{1,0:T(8,128)S(1)}, u32[]{:S(2)}, u32[]{:S(2)}) %collective-permute-start.36) | collective-permute-done | bytes 76832 | tf_op jit(solution)/shard_map/ppermute | solution.py:973
  290.5 46.1 %reduce-scatter.8.cloned.1.call-done.refs_5_ = bf16[96,4608]{1,0:T(8,128)(2,1)} async-done(((bf16[768,4608]{1,0:T(8,128)(2,1)}), bf16[96,4608]{1,0:T(8,128)(2,1)}) %reduce-scatter.8.cloned.1.call-update) | async-done | bytes 884752 | tf_op jit(solution)/shard_map/reduce_scatter | solution.py:1147
  339.2 2.0 collective-permute-done.37.refs_6_
  342.3 3.7 %placed_gradients.1 = (f32[2,96,1536]{2,1,0:T(8,128)}, f32[2,96,1536]{2,1,0:T(8,128)}, f32[2,3,96,384]{3,2,1,0:T(8,128)}, f32[2,96,384]{2,1,0:T(8,128)}, f32[3,48,384]{2,1,0:T(8,128)}, /*index=5*/f32[48,384]{1,0:T(8,128)}) custom-call(s32[9]{0:T(128)S(1)} %pad_add_fusion.refs_0_, bf16[96,3072]{1,0:T(8,128)(2,1)S(1)} %copy-done.24, ...), custom_call_target="tpu_custom_call" | custom-call | flops 2300000000 | tf_op jit(solution)/shard_map/placed_gradients/pallas_call | solution.py:249
  (295 shorter events, 56.1 us)
Async XLA Ops:
  7.2 200.9 %reduce-scatter.4.cloned.1.call-start = ((), (), s32[]{:S(2)}) async-start(), calls=%async_computation.3 | async-start | bytes 5308416 | tf_op jit(solution)/shard_map/reduce_scatter | solution.py:1147
  7.3 8.5 %collective-permute-start.1 = (bf16[1,2,3,768,384]{4,3,2,1,0:T(8,128)(2,1)}, bf16[1,2,3,768,384]{4,3,2,1,0:T(8,128)(2,1)}, u32[]{:S(2)}, u32[]{:S(2)}) collective-permute-start(bf16[1,2,3,768,384]{4,3,2,1,0:T(8,128)(2,1)} %bitcast.86), channel_id=1, source_target_pairs={{0,16},{16,0},{1,17},{17,1},{2,18},{18,2},{3,19},{19,3},{4,20},{20... | collective-permute-start | bytes 10616840 | tf_op jit(solution)/shard_map/ppermute | solution.py:973
  7.8 7.8 %collective-permute-start.2 = (bf16[1,2,384,768]{3,2,1,0:T(8,128)(2,1)}, bf16[1,2,384,768]{3,2,1,0:T(8,128)(2,1)S(1)}, u32[]{:S(2)}, u32[]{:S(2)}) collective-permute-start(bf16[1,2,384,768]{3,2,1,0:T(8,128)(2,1)} %refs_17_.3), channel_id=1, source_target_pairs={{0,16},{16,0},{1,17},{17,1},{2,18},{18,2},{3,19},{19,3},{4,20},{20... | collective-permute-start | bytes 3538952 | tf_op jit(solution)/shard_map/ppermute | solution.py:973
  10.3 4.1 %collective-permute-start = (f32[2,16,768]{2,1,0:T(8,128)S(1)}, f32[2,16,768]{2,1,0:T(8,128)S(1)}, u32[]{:S(2)}, u32[]{:S(2)}) collective-permute-start(f32[2,16,768]{2,1,0:T(8,128)S(1)} %concatenate.31), channel_id=1, source_target_pairs={{0,16},{16,0},{1,17},{17,1},{2,18},{18,2},{3,19},{19,3},{4,20},{20... | collective-permute-start | bytes 294920 | tf_op jit(solution)/shard_map/ppermute | solution.py:973
  15.8 13.3 %collective-permute-start.4 = (bf16[1,2,768,1536]{3,2,1,0:T(8,128)(2,1)}, bf16[1,2,768,1536]{3,2,1,0:T(8,128)(2,1)S(1)}, u32[]{:S(2)}, u32[]{:S(2)}) collective-permute-start(bf16[1,2,768,1536]{3,2,1,0:T(8,128)(2,1)} %refs_13_.1), channel_id=1, source_target_pairs={{0,16},{16,0},{1,17},{17,1},{2,18},{18,2},{3,19},{19,3},{4,20},{20... | collective-permute-start | bytes 14155784 | tf_op jit(solution)/shard_map/ppermute | solution.py:973
  16.2 14.5 %collective-permute-start.5 = (bf16[1,2,1536,768]{3,2,1,0:T(8,128)(2,1)}, bf16[1,2,1536,768]{3,2,1,0:T(8,128)(2,1)S(1)}, u32[]{:S(2)}, u32[]{:S(2)}) collective-permute-start(bf16[1,2,1536,768]{3,2,1,0:T(8,128)(2,1)} %refs_15_.3), channel_id=1, source_target_pairs={{0,16},{16,0},{1,17},{17,1},{2,18},{18,2},{3,19},{19,3},{4,20},{20... | collective-permute-start | bytes 14155784 | tf_op jit(solution)/shard_map/ppermute | solution.py:973
  20.5 8.6 %collective-permute-start.6 = (bf16[144,768]{1,0:T(8,128)(2,1)S(1)}, bf16[144,768]{1,0:T(8,128)(2,1)S(1)}, u32[]{:S(2)}, u32[]{:S(2)}) collective-permute-start(bf16[144,768]{1,0:T(8,128)(2,1)S(1)} %get-tuple-element.161.refs_2_), channel_id=1, source_target_pairs={{0,1},{1,0},{2,3},{3,2},{4,5},{5,4},{6,7},{7,6},{8,9},{9,8},{10,11... | collective-permute-start | bytes 663560 | tf_op jit(solution)/shard_map/ppermute | solution.py:973
  28.4 8.1 %collective-permute-start.3 = (bf16[80,768]{1,0:T(8,128)(2,1)S(1)}, bf16[80,768]{1,0:T(8,128)(2,1)S(1)}, u32[]{:S(2)}, u32[]{:S(2)}) collective-permute-start(bf16[80,768]{1,0:T(8,128)(2,1)S(1)} %get-tuple-element.158.refs_2_), channel_id=1, source_target_pairs={{0,1},{1,0},{2,3},{3,2},{4,5},{5,4},{6,7},{7,6},{8,9},{9,8},{10,11... | collective-permute-start | bytes 368648 | tf_op jit(solution)/shard_map/ppermute | solution.py:973
  41.2 10.7 %collective-permute-start.8 = (bf16[80,768]{1,0:T(8,128)(2,1)}, bf16[80,768]{1,0:T(8,128)(2,1)}, u32[]{:S(2)}, u32[]{:S(2)}) collective-permute-start(bf16[80,768]{1,0:T(8,128)(2,1)} %get-tuple-element.169.refs_2_), channel_id=1, source_target_pairs={{0,1},{1,0},{2,3},{3,2},{4,5},{5,4},{6,7},{7,6},{8,9},{9,8},{10,11... | collective-permute-start | bytes 368648 | tf_op jit(solution)/shard_map/ppermute | solution.py:973
  44.2 8.3 %collective-permute-start.9 = (bf16[144,768]{1,0:T(8,128)(2,1)}, bf16[144,768]{1,0:T(8,128)(2,1)}, u32[]{:S(2)}, u32[]{:S(2)}) collective-permute-start(bf16[144,768]{1,0:T(8,128)(2,1)} %get-tuple-element.171.refs_5_), channel_id=1, source_target_pairs={{0,1},{1,0},{2,3},{3,2},{4,5},{5,4},{6,7},{7,6},{8,9},{9,8},{10,11... | collective-permute-start | bytes 663560 | tf_op jit(solution)/shard_map/ppermute | solution.py:973
  49.9 17.8 %collective-permute-start.12 = (bf16[224,768]{1,0:T(8,128)(2,1)}, bf16[224,768]{1,0:T(8,128)(2,1)S(1)}, u32[]{:S(2)}, u32[]{:S(2)}) collective-permute-start(bf16[224,768]{1,0:T(8,128)(2,1)} %get-tuple-element.180.refs_9_), channel_id=1, source_target_pairs={{0,2},{2,0},{4,6},{6,4},{8,10},{10,8},{12,14},{14,12},{1,3},{3,1},... | collective-permute-start | bytes 1032200 | tf_op jit(solution)/shard_map/ppermute | solution.py:973
  51.9 32.8 %collective-permute-start.7 = (bf16[224,1920]{1,0:T(8,128)(2,1)}, bf16[224,1920]{1,0:T(8,128)(2,1)S(1)}, u32[]{:S(2)}, u32[]{:S(2)}) collective-permute-start(bf16[224,1920]{1,0:T(8,128)(2,1)} %get-tuple-element.167.refs_2_), channel_id=1, source_target_pairs={{0,2},{2,0},{4,6},{6,4},{8,10},{10,8},{12,14},{14,12},{1,3},{3,1},... | collective-permute-start | bytes 2580488 | tf_op jit(solution)/shard_map/ppermute | solution.py:973
  56.6 29.0 %slice-start.2 = ((s8[4718592]{0:T(1024)(128)(4,1)}), s8[4194304]{0:T(1024)(128)(4,1)S(1)}, s32[]{:S(2)}) async-start(s8[4718592]{0:T(1024)(128)(4,1)} %bitcast.84), calls=%async_computation.8 | async-start | bytes 8388608
  65.5 7.9 %collective-permute-start.11 = (bf16[144,768]{1,0:T(8,128)(2,1)S(1)}, bf16[144,768]{1,0:T(8,128)(2,1)S(1)}, u32[]{:S(2)}, u32[]{:S(2)}) collective-permute-start(bf16[144,768]{1,0:T(8,128)(2,1)S(1)} %get-tuple-element.179.refs_2_), channel_id=1, source_target_pairs={{0,1},{1,0},{2,3},{3,2},{4,5},{5,4},{6,7},{7,6},{8,9},{9,8},{10,11... | collective-permute-start | bytes 663560 | tf_op jit(solution)/shard_map/ppermute | solution.py:973
  67.3 13.3 %collective-permute-start.10 = (bf16[80,768]{1,0:T(8,128)(2,1)S(1)}, bf16[80,768]{1,0:T(8,128)(2,1)S(1)}, u32[]{:S(2)}, u32[]{:S(2)}) collective-permute-start(bf16[80,768]{1,0:T(8,128)(2,1)S(1)} %get-tuple-element.177.refs_2_), channel_id=1, source_target_pairs={{0,1},{1,0},{2,3},{3,2},{4,5},{5,4},{6,7},{7,6},{8,9},{9,8},{10,11... | collective-permute-start | bytes 368648 | tf_op jit(solution)/shard_map/ppermute | solution.py:973
  77.6 7.0 %collective-permute-start.14 = (bf16[144,768]{1,0:T(8,128)(2,1)S(1)}, bf16[144,768]{1,0:T(8,128)(2,1)S(1)}, u32[]{:S(2)}, u32[]{:S(2)}) collective-permute-start(bf16[144,768]{1,0:T(8,128)(2,1)S(1)} %get-tuple-element.189.refs_2_), channel_id=1, source_target_pairs={{0,1},{1,0},{2,3},{3,2},{4,5},{5,4},{6,7},{7,6},{8,9},{9,8},{10,11... | collective-permute-start | bytes 663560 | tf_op jit(solution)/shard_map/ppermute | solution.py:973
  79.1 16.9 %collective-permute-start.15 = (bf16[224,768]{1,0:T(8,128)(2,1)S(1)}, bf16[224,768]{1,0:T(8,128)(2,1)S(1)}, u32[]{:S(2)}, u32[]{:S(2)}) collective-permute-start(bf16[224,768]{1,0:T(8,128)(2,1)S(1)} %copy-done.62), channel_id=1, source_target_pairs={{0,2},{2,0},{4,6},{6,4},{8,10},{10,8},{12,14},{14,12},{1,3},{3,1},... | collective-permute-start | bytes 1032200 | tf_op jit(solution)/shard_map/ppermute | solution.py:973
  90.6 15.1 %collective-permute-start.18 = (bf16[144,1920]{1,0:T(8,128)(2,1)}, bf16[144,1920]{1,0:T(8,128)(2,1)S(1)}, u32[]{:S(2)}, u32[]{:S(2)}) collective-permute-start(bf16[144,1920]{1,0:T(8,128)(2,1)} %get-tuple-element.203.refs_3_), channel_id=1, source_target_pairs={{0,2},{2,0},{4,6},{6,4},{8,10},{10,8},{12,14},{14,12},{1,3},{3,1},... | collective-permute-start | bytes 1658888 | tf_op jit(solution)/shard_map/ppermute | solution.py:973
  91.1 4.9 %collective-permute-start.13 = (bf16[80,768]{1,0:T(8,128)(2,1)S(1)}, bf16[80,768]{1,0:T(8,128)(2,1)S(1)}, u32[]{:S(2)}, u32[]{:S(2)}) collective-permute-start(bf16[80,768]{1,0:T(8,128)(2,1)S(1)} %get-tuple-element.187.refs_2_), channel_id=1, source_target_pairs={{0,1},{1,0},{2,3},{3,2},{4,5},{5,4},{6,7},{7,6},{8,9},{9,8},{10,11... | collective-permute-start | bytes 368648 | tf_op jit(solution)/shard_map/ppermute | solution.py:973
  92.6 13.1 %collective-permute-start.17 = (bf16[144,768]{1,0:T(8,128)(2,1)S(1)}, bf16[144,768]{1,0:T(8,128)(2,1)S(1)}, u32[]{:S(2)}, u32[]{:S(2)}) collective-permute-start(bf16[144,768]{1,0:T(8,128)(2,1)S(1)} %get-tuple-element.200.refs_6_), channel_id=1, source_target_pairs={{0,1},{1,0},{2,3},{3,2},{4,5},{5,4},{6,7},{7,6},{8,9},{9,8},{10,11... | collective-permute-start | bytes 663560 | tf_op jit(solution)/shard_map/ppermute | solution.py:973
  100.7 4.9 %collective-permute-start.16 = (bf16[80,768]{1,0:T(8,128)(2,1)S(1)}, bf16[80,768]{1,0:T(8,128)(2,1)S(1)}, u32[]{:S(2)}, u32[]{:S(2)}) collective-permute-start(bf16[80,768]{1,0:T(8,128)(2,1)S(1)} %get-tuple-element.198.refs_2_), channel_id=1, source_target_pairs={{0,1},{1,0},{2,3},{3,2},{4,5},{5,4},{6,7},{7,6},{8,9},{9,8},{10,11... | collective-permute-start | bytes 368648 | tf_op jit(solution)/shard_map/ppermute | solution.py:973
  118.5 7.5 %collective-permute-start.19 = (bf16[224,768]{1,0:T(8,128)(2,1)}, bf16[224,768]{1,0:T(8,128)(2,1)S(1)}, u32[]{:S(2)}, u32[]{:S(2)}) collective-permute-start(bf16[224,768]{1,0:T(8,128)(2,1)} %get-tuple-element.205.refs_6_), channel_id=1, source_target_pairs={{0,1},{1,0},{2,3},{3,2},{4,5},{5,4},{6,7},{7,6},{8,9},{9,8},{10,11... | collective-permute-start | bytes 1032200 | tf_op jit(solution)/shard_map/ppermute | solution.py:973
  120.1 20.3 %collective-permute-start.22 = (bf16[224,1920]{1,0:T(8,128)(2,1)}, bf16[224,1920]{1,0:T(8,128)(2,1)S(1)}, u32[]{:S(2)}, u32[]{:S(2)}) collective-permute-start(bf16[224,1920]{1,0:T(8,128)(2,1)} %get-tuple-element.220.refs_7_), channel_id=1, source_target_pairs={{0,2},{2,0},{4,6},{6,4},{8,10},{10,8},{12,14},{14,12},{1,3},{3,1},... | collective-permute-start | bytes 2580488 | tf_op jit(solution)/shard_map/ppermute | solution.py:973
  120.7 19.7 %collective-permute-start.21 = (bf16[80,1920]{1,0:T(8,128)(2,1)S(1)}, bf16[80,1920]{1,0:T(8,128)(2,1)S(1)}, u32[]{:S(2)}, u32[]{:S(2)}) collective-permute-start(bf16[80,1920]{1,0:T(8,128)(2,1)S(1)} %copy-done.64), channel_id=1, source_target_pairs={{0,2},{2,0},{4,6},{6,4},{8,10},{10,8},{12,14},{14,12},{1,3},{3,1},... | collective-permute-start | bytes 921608 | tf_op jit(solution)/shard_map/ppermute | solution.py:973
  146.6 106.0 %reduce-scatter.6.cloned.1.call-start = ((), (), s32[]{:S(2)}) async-start(), calls=%async_computation.4 | async-start | bytes 3981312 | tf_op jit(solution)/shard_map/reduce_scatter | solution.py:1147
  146.6 9.1 %collective-permute-start.23 = (bf16[224,768]{1,0:T(8,128)(2,1)}, bf16[224,768]{1,0:T(8,128)(2,1)S(1)}, u32[]{:S(2)}, u32[]{:S(2)}) collective-permute-start(bf16[224,768]{1,0:T(8,128)(2,1)} %get-tuple-element.222.refs_2_), channel_id=1, source_target_pairs={{0,2},{2,0},{4,6},{6,4},{8,10},{10,8},{12,14},{14,12},{1,3},{3,1},... | collective-permute-start | bytes 1032200 | tf_op jit(solution)/shard_map/ppermute | solution.py:973
  147.6 8.2 %collective-permute-start.20 = (bf16[224,768]{1,0:T(8,128)(2,1)}, bf16[224,768]{1,0:T(8,128)(2,1)S(1)}, u32[]{:S(2)}, u32[]{:S(2)}) collective-permute-start(bf16[224,768]{1,0:T(8,128)(2,1)} %get-tuple-element.211.refs_6_), channel_id=1, source_target_pairs={{0,1},{1,0},{2,3},{3,2},{4,5},{5,4},{6,7},{7,6},{8,9},{9,8},{10,11... | collective-permute-start | bytes 1032200 | tf_op jit(solution)/shard_map/ppermute | solution.py:973
  148.8 19.7 %collective-permute-start.25 = (bf16[224,1536]{1,0:T(8,128)(2,1)}, bf16[224,1536]{1,0:T(8,128)(2,1)S(1)}, u32[]{:S(2)}, u32[]{:S(2)}) collective-permute-start(bf16[224,1536]{1,0:T(8,128)(2,1)} %get-tuple-element.227.refs_5_), channel_id=1, source_target_pairs={{0,2},{2,0},{4,6},{6,4},{8,10},{10,8},{12,14},{14,12},{1,3},{3,1},... | collective-permute-start | bytes 2064392 | tf_op jit(solution)/shard_map/ppermute | solution.py:973
  166.3 7.5 %collective-permute-start.24 = (bf16[224,768]{1,0:T(8,128)(2,1)}, bf16[224,768]{1,0:T(8,128)(2,1)S(1)}, u32[]{:S(2)}, u32[]{:S(2)}) collective-permute-start(bf16[224,768]{1,0:T(8,128)(2,1)} %get-tuple-element.224.refs_6_), channel_id=1, source_target_pairs={{0,1},{1,0},{2,3},{3,2},{4,5},{5,4},{6,7},{7,6},{8,9},{9,8},{10,11... | collective-permute-start | bytes 1032200 | tf_op jit(solution)/shard_map/ppermute | solution.py:973
  167.5 22.7 %collective-permute-start.26 = (bf16[224,1536]{1,0:T(8,128)(2,1)}, bf16[224,1536]{1,0:T(8,128)(2,1)S(1)}, u32[]{:S(2)}, u32[]{:S(2)}) collective-permute-start(bf16[224,1536]{1,0:T(8,128)(2,1)} %get-tuple-element.236.refs_12_), channel_id=1, source_target_pairs={{0,2},{2,0},{4,6},{6,4},{8,10},{10,8},{12,14},{14,12},{1,3},{3,1},... | collective-permute-start | bytes 2064392 | tf_op jit(solution)/shard_map/ppermute | solution.py:973
  188.0 8.5 %collective-permute-start.28 = (bf16[224,768]{1,0:T(8,128)(2,1)}, bf16[224,768]{1,0:T(8,128)(2,1)S(1)}, u32[]{:S(2)}, u32[]{:S(2)}) collective-permute-start(bf16[224,768]{1,0:T(8,128)(2,1)} %get-tuple-element.243.refs_6_), channel_id=1, source_target_pairs={{0,1},{1,0},{2,3},{3,2},{4,5},{5,4},{6,7},{7,6},{8,9},{9,8},{10,11... | collective-permute-start | bytes 1032200 | tf_op jit(solution)/shard_map/ppermute | solution.py:973
  189.3 18.9 %collective-permute-start.27 = (bf16[224,1920]{1,0:T(8,128)(2,1)}, bf16[224,1920]{1,0:T(8,128)(2,1)}, u32[]{:S(2)}, u32[]{:S(2)}) collective-permute-start(bf16[224,1920]{1,0:T(8,128)(2,1)} %get-tuple-element.229.refs_5_), channel_id=1, source_target_pairs={{0,2},{2,0},{4,6},{6,4},{8,10},{10,8},{12,14},{14,12},{1,3},{3,1},... | collective-permute-start | bytes 2580488 | tf_op jit(solution)/shard_map/ppermute | solution.py:973
  208.2 128.4 %reduce-scatter.8.cloned.1.call-start = ((), (), s32[]{:S(2)}) async-start(), calls=%async_computation.5 | async-start | bytes 7962624 | tf_op jit(solution)/shard_map/reduce_scatter | solution.py:1147
  209.2 10.9 %collective-permute-start.29 = (bf16[224,1536]{1,0:T(8,128)(2,1)S(1)}, bf16[224,1536]{1,0:T(8,128)(2,1)S(1)}, u32[]{:S(2)}, u32[]{:S(2)}) collective-permute-start(bf16[224,1536]{1,0:T(8,128)(2,1)S(1)} %copy-done.29), channel_id=1, source_target_pairs={{0,2},{2,0},{4,6},{6,4},{8,10},{10,8},{12,14},{14,12},{1,3},{3,1},... | collective-permute-start | bytes 2064392 | tf_op jit(solution)/shard_map/ppermute | solution.py:973
  227.9 28.1 %copy-start.42 = (f32[2,3,768]{2,1,0:T(4,128)S(1)}, f32[2,3,768]{2,1,0:T(4,128)}, u32[]{:S(2)}) copy-start(f32[2,3,768]{2,1,0:T(4,128)} %get-tuple-element.262) | copy-start | bytes 55300
  227.9 28.2 %copy-start.43 = (f32[2,2,384]{2,1,0:T(2,128)S(1)}, f32[2,2,384]{2,1,0:T(2,128)}, u32[]{:S(2)}) copy-start(f32[2,2,384]{2,1,0:T(2,128)} %get-tuple-element.248.refs_14_) | copy-start | bytes 18436
  227.9 28.4 %copy-start.38 = (f32[3,768]{1,0:T(4,128)S(1)}, f32[3,768]{1,0:T(4,128)}, u32[]{:S(2)}) copy-start(f32[3,768]{1,0:T(4,128)} %get-tuple-element.273) | copy-start | bytes 27652
  227.9 42.6 %copy-start.34 = (bf16[144,768]{1,0:T(8,128)(2,1)S(1)}, bf16[144,768]{1,0:T(8,128)(2,1)}, u32[]{:S(2)}) copy-start(bf16[144,768]{1,0:T(8,128)(2,1)} %get-tuple-element.259) | copy-start | bytes 663556
  252.6 28.9 %copy-start.24 = (bf16[96,3072]{1,0:T(8,128)(2,1)S(1)}, bf16[96,3072]{1,0:T(8,128)(2,1)}, u32[]{:S(2)}) copy-start(bf16[96,3072]{1,0:T(8,128)(2,1)} %reduce-scatter.4.cloned.1.call-done.refs_1_) | copy-start | bytes 1769476
  252.6 30.7 %copy-start.19 = (bf16[144,1536]{1,0:T(8,128)(2,1)S(1)}, bf16[144,1536]{1,0:T(8,128)(2,1)}, u32[]{:S(2)}) copy-start(bf16[144,1536]{1,0:T(8,128)(2,1)} %reduce-scatter.6.cloned.1.call-done.refs_2_) | copy-start | bytes 1327108
  256.3 1.4 collective-permute-start.33
  257.7 4.9 %collective-permute-start.34 = (f32[25,768]{1,0:T(8,128)S(1)}, f32[25,768]{1,0:T(8,128)S(1)}, u32[]{:S(2)}, u32[]{:S(2)}) collective-permute-start(f32[25,768]{1,0:T(8,128)S(1)} %fusion.2), channel_id=1, source_target_pairs={{0,2},{2,0},{4,6},{6,4},{8,10},{10,8},{12,14},{14,12},{1,3},{3,1},... | collective-permute-start | bytes 230408 | tf_op jit(solution)/shard_map/ppermute | solution.py:973
  262.6 7.2 %collective-permute-start.35 = (f32[25,768]{1,0:T(8,128)S(1)}, f32[25,768]{1,0:T(8,128)S(1)}, u32[]{:S(2)}, u32[]{:S(2)}) collective-permute-start(f32[25,768]{1,0:T(8,128)S(1)} %add.160), channel_id=1, source_target_pairs={{0,4},{2,6},{4,0},{6,2},{8,12},{10,14},{12,8},{14,10},{1,5},{3,7},... | collective-permute-start | bytes 230408 | tf_op jit(solution)/shard_map/ppermute | solution.py:973
  269.8 11.3 %collective-permute-start.36 = (f32[25,768]{1,0:T(8,128)S(1)}, f32[25,768]{1,0:T(8,128)S(1)}, u32[]{:S(2)}, u32[]{:S(2)}) collective-permute-start(f32[25,768]{1,0:T(8,128)S(1)} %add.161), channel_id=1, source_target_pairs={{0,8},{2,10},{4,12},{6,14},{8,0},{10,2},{12,4},{14,6},{1,9},{3,11}... | collective-permute-start | bytes 230408 | tf_op jit(solution)/shard_map/ppermute | solution.py:973
  272.0 15.9 %collective-permute-start.32 = (bf16[224,768]{1,0:T(8,128)(2,1)S(1)}, bf16[224,768]{1,0:T(8,128)(2,1)S(1)}, u32[]{:S(2)}, u32[]{:S(2)}) collective-permute-start(bf16[224,768]{1,0:T(8,128)(2,1)S(1)} %copy-done.32), channel_id=1, source_target_pairs={{0,1},{1,0},{2,3},{3,2},{4,5},{5,4},{6,7},{7,6},{8,9},{9,8},{10,11... | collective-permute-start | bytes 1032200 | tf_op jit(solution)/shard_map/ppermute | solution.py:973
  281.5 9.0 %collective-permute-start.30 = (bf16[96,3072]{1,0:T(8,128)(2,1)S(1)}, bf16[96,3072]{1,0:T(8,128)(2,1)S(1)}, u32[]{:S(2)}, u32[]{:S(2)}) collective-permute-start(bf16[96,3072]{1,0:T(8,128)(2,1)S(1)} %copy-done.24), channel_id=1, source_target_pairs={{0,16},{1,17},{2,18},{3,19},{4,20},{5,21},{6,22},{7,23},{8,24},{9,... | collective-permute-start | bytes 1769480 | tf_op jit(solution)/shard_map/ppermute | solution.py:1350
  284.1 6.5 %collective-permute-start.31 = (bf16[96,1536]{1,0:T(8,128)(2,1)}, bf16[96,1536]{1,0:T(8,128)(2,1)S(1)}, u32[]{:S(2)}, u32[]{:S(2)}) collective-permute-start(bf16[96,1536]{1,0:T(8,128)(2,1)} %slice.94), channel_id=1, source_target_pairs={{0,16},{1,17},{2,18},{3,19},{4,20},{5,21},{6,22},{7,23},{8,24},{9,... | collective-permute-start | bytes 884744 | tf_op jit(solution)/shard_map/ppermute | solution.py:1350
  336.6 4.5 %collective-permute-start.37 = (bf16[96,4608]{1,0:T(8,128)(2,1)}, bf16[96,4608]{1,0:T(8,128)(2,1)S(1)}, u32[]{:S(2)}, u32[]{:S(2)}) collective-permute-start(bf16[96,4608]{1,0:T(8,128)(2,1)} %reduce-scatter.8.cloned.1.call-done.refs_5_), channel_id=1, source_target_pairs={{16,0},{17,1},{18,2},{19,3},{20,4},{21,5},{22,6},{23,7},{24,8},{25... | collective-permute-start | bytes 2654216 | tf_op jit(solution)/shard_map/ppermute | solution.py:1366
  (67 other events, 875.7 us)
Sparse Core Ops, SparseCore 0:
  146.7 55.6 reduce-scatter.3
  208.3 44.2 reduce-scatter.5
  255.0 81.5 reduce-scatter.7
where the time goes:
time: 360 us; the launch traced here: 353 us
  waiting for transfers between devices  138 us (38%)
  Pallas kernels  119 us (33%)
  starting transfers between devices  39.6 us (11%)
  local copies, waits for them, and re-layouts  33.3 us (9%)
  between operations  15.4 us (4%)
  other arithmetic  7.21 us (2%)
    pallas_call x18, Pallas kernels, call(): pl.pallas_call(whole, out_shape=[spaces[out[2]]((out[3], *out[0][1:]) if...  119 us
    reduce_scatter x3, waiting for transfers between devices, scatter(): lax.psum_scatter(value, ('section', 'dp'), scatter_dimension=0, axis_inde...  70.7 us
    ppermute x35, waiting for transfers between devices, swap(): return lax.ppermute(value, axis, [(i, i ^ distance) for i in range(count)])  65.4 us
    ppermute x35, starting transfers between devices, swap(): return lax.ppermute(value, axis, [(i, i ^ distance) for i in range(count)])  35.3 us
    unnamed x164, local copies, waits for them, and re-layouts  18.4 us
  transfers between devices with their start and end apart: 41, of which 21 were waited for; matrix products, arithmetic and copies ran while one was open for 7% of the time, Pallas kernels for 27%

commit v1 on v0

--- a/solution.py
+++ b/solution.py
@@ -331,7 +331,8 @@
     ins = [(meta, "s"), (state, "v")]
     if not first:
         ins += list(zip(prior, "vvv"))
-    ins += [(small, "v"), (chooser, "v")] + list(zip(att_in + att_out, "wawa"))
+    ins += [(small, "v"), (chooser, "v")]
+    ins += list(zip(att_in + att_out, "wawa" if layer == 0 else "wwww"))
     outs = [
         ((3, rows, width), bf16, "h"),
         ((width // HEAD_DIM, rows, rows), bf16, "h"),
@@ -396,9 +397,10 @@
         part[...] = mm(pack[:, HALF:], weights.get(1)[...]).astype(bf16)
 
     ins = [(meta, "s"), (residual, "v"), (own, "v"), (other, "v")]
-    ins += [(small, "v"), (chooser, "v")] + list(zip(feed_in + feed_out, "wawa"))
+    ins += [(small, "v"), (chooser, "v")]
+    ins += list(zip(feed_in + feed_out, "wawa" if layer == 0 else "wwww"))
     outs = [
-        ((rows, D), f32, "h"),
+        ((rows, D), f32, "v"),
         ((rows, D), f32, "h"),
         ((rows, 1), f32, "h"),
         ((rows, HALF), bf16, "h"),
@@ -467,7 +469,7 @@
             flush(qkv, probs)
             part[...] = mm(context[...], leave[...]).astype(bf16)
 
-    ins = [(meta, "s")] + [pair for stream in streams for pair in zip(stream, "hvv")]
+    ins = [(meta, "s")] + [pair for stream in streams for pair in zip(stream, "vvv")]
     ins += [(item, "v") for item in smalls]
     ins += [(chooser, "v"), (cross_in, "w"), (cross_bias, "v"), (cross_out, "w")]
     outs = []
@@ -493,113 +495,145 @@
     return result[:8], result[8:16], result[16]
 
 
+class Layout:
+    def __init__(self, sides, rows, given):
+        self.sides, self.total, self.spans = sides, sum(rows), spans_of(rows)
+        self.single = len(sides) == 1
+        self.side = sides[0]
+        self.count = rows[self.side] if self.single else self.total
+        self.given = given
+
+    def here(self, side):
+        return slice(0, self.count) if self.single else self.spans[side]
+
+    def index(self, side):
+        return 0 if self.single else side
+
+    def rows(self, width, dtype, at):
+        if not self.single:
+            return (self.total, width), dtype, "h"
+        given = self.given[at] if self.given else None
+        return (self.count, width), dtype, "h", self.total, self.spans[self.side].start, given
+
+    def each(self, shape, at):
+        if not self.single:
+            return (2, *shape), f32, "h"
+        given = self.given[at] if self.given else None
+        return (1, *shape), f32, "h", 2, self.side, given
+
+
 def feed_backward(
-    layer, batch, meta, tops, joint, small, chooser, slopes, feed_in, feed_out, ties=()
+    layer, sides, rows, batch, meta, tops, joint, small, chooser, slopes, feed_in, feed_out, ties=(),
+    given=None,
 ):
     last = joint is None
-    rows = [slope.shape[0] for slope in slopes]
+    layout = Layout(sides, rows, given)
     units = slopes[0].shape[1]
-    spans, total = spans_of(rows), sum(rows)
     step = units // 4
     n_top = len(tops[0])
+    n = len(sides)
 
     def body(flush, meta, *refs):
-        given = (refs[:n_top], refs[n_top : 2 * n_top])
-        refs = refs[2 * n_top :]
+        tops = {}
+        for side in sides:
+            tops[side], refs = refs[:n_top], refs[n_top:]
         if not last:
             joint, refs = refs[:3], refs[3:]
-        small, chooser, slopes = refs[:2], refs[2], refs[3:5]
-        in_own, in_other, out_own, out_other = refs[5:9]
-        grad_all, selected_all, pack_all, part_all, post_all, bias_all = refs[9:15]
+        small, refs = dict(zip(sides, refs[:n])), refs[n:]
+        chooser, slopes, refs = refs[0], dict(zip(sides, refs[1 : 1 + n])), refs[1 + n :]
+        in_own, in_other, out_own, out_other = refs[:4]
+        grad_all, selected_all, pack_all, part_all, post_all, bias_all = refs[4:10]
         if last:
-            results, squares_all = refs[15:17], refs[17]
+            squares_all, results = refs[10], dict(zip(sides, refs[11 : 11 + n]))
         in_buffer, out_buffer, sems = refs[-3:]
-        weights = [
-            Weights(
+        weights = {}
+        for i, side in enumerate(sides):
+            weights[side] = Weights(
                 meta,
                 layer,
                 (
                     maps(out_own, out_other, side, row_pieces(units, 4)),
                     maps(in_own, in_other, side, column_pieces(units, 2)),
                 ),
-                (out_buffer.at[side], in_buffer.at[side]),
-                sems.at[side],
+                (out_buffer.at[i], in_buffer.at[i]),
+                sems.at[i],
             )
-            for side in (1, 0)
-        ][::-1]
-        lows = [None, None]
-        for side in (1, 0):
-            here = spans[side]
+        lows = {}
+        for side in sides:
+            here, at = layout.here(side), layout.index(side)
             post = small[side][ROW_FEED_POST : ROW_FEED_POST + 3]
             if last:
-                settled, own, other, cotangent = given[side]
+                settled, own, other, cotangent = tops[side]
                 branch = summed(own, other) + post[0:1]
                 unit, rstd, result = norm_of(settled[...] + branch, post[1:2], post[2:3])
                 low = result.astype(bf16)
                 results[side][...] = low
                 valid = row_valid(meta, side, batch, rows[side])
-                squares_all[side, 0:1] = square_sum(branch, valid)
-                squares_all[side, 1:2] = square_sum(low.astype(f32), valid)
+                squares_all[at, 0:1] = square_sum(branch, valid)
+                squares_all[at, 1:2] = square_sum(low.astype(f32), valid)
                 incoming = cotangent[...].astype(f32) * valid
             else:
-                unit_ref, rstd_ref = given[side]
+                unit_ref, rstd_ref = tops[side]
                 unit, rstd = unit_ref[...], rstd_ref[...]
                 incoming = (joint[0][here] + summed_rows(joint[1], joint[2], here)).astype(bf16)
                 incoming = incoming.astype(f32)
             grad = norm_back(unit, rstd, post[1:2], incoming)
             grad_all[here] = grad
             low = grad.astype(bf16)
-            post_all[side, 0:1] = column_sum(low.astype(f32))
-            post_all[side, 1:2] = column_sum(incoming * unit)
-            post_all[side, 2:3] = column_sum(incoming)
+            post_all[at, 0:1] = column_sum(low.astype(f32))
+            post_all[at, 1:2] = column_sum(incoming * unit)
+            post_all[at, 2:3] = column_sum(incoming)
             lows[side] = low
-        for side in (1, 0):
-            here = spans[side]
-            select_rows(lows[side], chooser, selected_all.at[here], pack_all.at[here])
+        flush(grad_all, post_all)
+        for side in sides:
+            here, at = layout.here(side), layout.index(side)
             for i in range(units // step):
                 columns = slice(i * step, (i + 1) * step)
                 active = mm_nt(lows[side], weights[side].get(0, i)[columns, :])
                 hidden = (active * slopes[side][:, columns].astype(f32)).astype(bf16)
                 pack_all[here, HALF + i * step : HALF + (i + 1) * step] = hidden
-                bias_all[side, :, columns] = column_sum(hidden.astype(f32))
+                bias_all[at, :, columns] = column_sum(hidden.astype(f32))
+            select_rows(lows[side], chooser, selected_all.at[here], pack_all.at[here])
         flush(pack_all, selected_all)
-        for side in (1, 0):
-            here = spans[side]
+        for side in sides:
+            here = layout.here(side)
             part_all[here] = mm_nt(pack_all[here, HALF:], weights[side].get(1)[...]).astype(bf16)
 
-    ins = [(meta, "s")] + [pair for top in tops for pair in zip(top, "hfff" if last else "hh")]
+    ins = [(meta, "s")] + [pair for top in tops for pair in zip(top, "vvvv" if last else "vv")]
     if not last:
-        ins += list(zip(joint, "hhf"))
-    ins += [(item, "f") for item in small] + [(chooser, "f")] + [(item, "h") for item in slopes]
-    ins += list(zip(feed_in + feed_out, "wawa"))
+        ins += [(item, "v") for item in joint]
+    ins += [(item, "v") for item in (*small, chooser, *slopes)]
+    ins += list(zip(feed_in + feed_out, "wwww"))
+    count = layout.count
     outs = [
-        ((total, D), f32, "h"),
-        ((total, HALF), bf16, "h"),
-        ((total, HALF + units), bf16, "h"),
-        ((total, D), bf16, "h"),
-        ((2, 3, D), f32, "h"),
-        ((2, 1, units), f32, "h"),
+        ((count, D), f32, "v" if last else "h"),
+        layout.rows(HALF, bf16, 1),
+        ((count, HALF + units), bf16, "h"),
+        ((count, D), bf16, "v" if last else "h"),
+        layout.each((3, D), 4),
+        layout.each((1, units), 5),
     ]
     if last:
-        outs += [((here, D), bf16, "h") for here in rows] + [((2, 2, 128), f32, "h")]
+        outs += [layout.each((2, 128), 6)] + [((rows[side], D), bf16, "h") for side in sides]
     scratch = [
-        pltpu.VMEM((2, D, units), bf16),
-        pltpu.VMEM((2, units, D), bf16),
-        pltpu.SemaphoreType.DMA((2, 6)),
+        pltpu.VMEM((n, D, units), bf16),
+        pltpu.VMEM((n, units, D), bf16),
+        pltpu.SemaphoreType.DMA((n, 6)),
     ]
-    return call(body, ins, outs, scratch, 11.0, f"feed_backward_{layer}", ties, 24)
+    name = f"feed_backward_{layer}_" + "".join(map(str, sides))
+    return call(body, ins, outs, scratch, 11.0 * count / layout.total, name, ties, 24)
 
 
 def summed_rows(own, other, here):
     return own[here].astype(f32) + other[here].astype(f32)
 
 
-def back_through_norm(top, joint, here, gain, grad_all, post_ref):
+def back_through_norm(top, grad_in, branch, gain, grad_ref, post_ref):
     unit_ref, rstd_ref = top
-    incoming = joint[0][here] + summed_rows(joint[1], joint[2], here)
+    incoming = grad_in + branch
     unit = unit_ref[...]
     grad = norm_back(unit, rstd_ref[...], gain, incoming)
-    grad_all[here] = grad
+    grad_ref[...] = grad
     low = grad.astype(bf16)
     post_ref[0:1] = column_sum(low.astype(f32))
     post_ref[1:2] = column_sum(incoming * unit)
@@ -624,76 +658,86 @@
 
 
 def self_backward(
-    layer, meta, tops, joint, small, chooser, qkvs, probs, att_in, att_out, ties=()
+    layer, sides, rows, meta, tops, joint, small, chooser, qkvs, probs, att_in, att_out, ties=(),
+    given=None,
 ):
-    rows = [qkv.shape[1] for qkv in qkvs]
+    layout = Layout(sides, rows, given)
     width = qkvs[0].shape[2]
-    spans, total = spans_of(rows), sum(rows)
+    n = len(sides)
 
     def body(flush, meta, *refs):
-        tops, joint = (refs[:2], refs[2:4]), refs[4:7]
-        small, chooser, qkvs, probs = refs[7:9], refs[9], refs[10:12], refs[12:14]
-        in_own, in_other, out_own, out_other = refs[14:18]
-        grad_all, selected_all, pack_all, part_all, post_all, bias_all = refs[18:24]
-        in_buffer, out_buffer, sems = refs[24:]
-        weights = [
-            Weights(
+        tops = {side: refs[2 * i : 2 * i + 2] for i, side in enumerate(sides)}
+        joint, refs = refs[2 * n : 2 * n + 3], refs[2 * n + 3 :]
+        small, chooser, refs = dict(zip(sides, refs[:n])), refs[n], refs[n + 1 :]
+        qkvs, probs, refs = dict(zip(sides, refs[:n])), dict(zip(sides, refs[n : 2 * n])), refs[2 * n :]
+        in_own, in_other, out_own, out_other = refs[:4]
+        grad_all, selected_all, pack_all, part_all, post_all, bias_all = refs[4:10]
+        in_buffer, out_buffer, sems = refs[10:]
+        weights = {}
+        for i, side in enumerate(sides):
+            weights[side] = Weights(
                 meta,
                 layer,
                 (maps(out_own, out_other, side), maps(in_own, in_other, side, ENTRY)),
-                (out_buffer.at[side], in_buffer.at[side]),
-                sems.at[side],
+                (out_buffer.at[i], in_buffer.at[i]),
+                sems.at[i],
             )
-            for side in (1, 0)
-        ][::-1]
-        for side in (1, 0):
-            here = spans[side]
+        for side in sides:
+            here, at = layout.here(side), layout.index(side)
             pack = pack_all.at[here]
             gain = small[side][ROW_ATT_POST + 1 : ROW_ATT_POST + 2]
-            low = back_through_norm(tops[side], joint, here, gain, grad_all, post_all.at[side])
-            select_rows(low, chooser, selected_all.at[here], pack)
+            low = back_through_norm(
+                tops[side],
+                joint[0][here],
+                summed_rows(joint[1], joint[2], here),
+                gain,
+                grad_all.at[here],
+                post_all.at[at],
+            )
             context = mm_nt(low, weights[side].get(0)[...]).astype(bf16)
             qkv = qkvs[side]
             attend_back(qkv[0], qkv[1], qkv[2], probs[side], context, emit_into(pack, width))
-            bias_all[side, 0:1] = column_sum(pack[:, HALF : HALF + width].astype(f32))
-            bias_all[side, 1:2] = column_sum(pack[:, HALF + 2 * width :].astype(f32))
-        flush(pack_all, selected_all)
-        for side in (1, 0):
-            here = spans[side]
+            bias_all[at, 0:1] = column_sum(pack[:, HALF : HALF + width].astype(f32))
+            bias_all[at, 1:2] = column_sum(pack[:, HALF + 2 * width :].astype(f32))
+            select_rows(low, chooser, selected_all.at[here], pack)
+        flush(pack_all, selected_all, grad_all, post_all, bias_all)
+        for side in sides:
+            here = layout.here(side)
             part_all[here] = back_to_input(pack_all.at[here], weights[side], 1, width)
 
-    ins = [(meta, "s")] + [(item, "h") for top in tops for item in top]
-    ins += list(zip(joint, "hhf"))
-    ins += [(item, "f") for item in small] + [(chooser, "f")]
-    ins += [(item, "h") for item in (*qkvs, *probs)]
-    ins += list(zip(att_in + att_out, "wawa"))
+    near = "v" if layer == 1 else "h"
+    ins = [(meta, "s")] + [(item, near) for top in tops for item in top]
+    ins += [*zip(joint, "vvv" if layer == 1 else "hhf")] + [(item, near) for item in small]
+    ins += [(item, near) for item in (chooser, *qkvs, *probs)]
+    ins += list(zip(att_in + att_out, "wwww"))
     outs = [
-        ((total, D), f32, "h"),
-        ((total, HALF), bf16, "h"),
-        ((total, HALF + 3 * width), bf16, "h"),
-        ((total, D), bf16, "h"),
-        ((2, 3, D), f32, "h"),
-        ((2, 2, width), f32, "h"),
+        ((layout.count, D), f32, "h"),
+        layout.rows(HALF, bf16, 1),
+        layout.rows(HALF + 3 * width, bf16, 2),
+        ((layout.count, D), bf16, "h"),
+        layout.each((3, D), 4),
+        layout.each((2, width), 5),
     ]
     scratch = [
-        pltpu.VMEM((2, 3, D, width), bf16),
-        pltpu.VMEM((2, width, D), bf16),
-        pltpu.SemaphoreType.DMA((2, 6)),
+        pltpu.VMEM((n, 3, D, width), bf16),
+        pltpu.VMEM((n, width, D), bf16),
+        pltpu.SemaphoreType.DMA((n, 6)),
     ]
-    return call(body, ins, outs, scratch, 12.0, f"self_backward_{layer}", ties, 18)
-
-
-def cross_backward(meta, tops, joint, post, chooser, qkvs, probs, cross_in, cross_out, ties=()):
+    name = f"self_backward_{layer}_" + "".join(map(str, sides))
+    return call(body, ins, outs, scratch, 12.0 * layout.count / layout.total, name, ties, 18)
+
+
+def cross_backward(meta, tops, grads, owns, others, post, chooser, qkvs, probs, cross_in, cross_out, ties=()):
     rows = [qkv.shape[1] for qkv in qkvs]
     width = cross_out.shape[0]
     spans, total = spans_of(rows), sum(rows)
 
     def body(flush, meta, *refs):
-        tops, joint = (refs[:2], refs[2:4]), refs[4:7]
-        post, chooser, qkvs, probs = refs[7], refs[8], refs[9:11], refs[11:13]
-        in_ref, out_ref = refs[13:15]
-        grad_all, selected_all, pack_all, part_all, post_out, bias_out = refs[15:21]
-        in_buffer, out_buffer, post_each, sems = refs[21:]
+        tops, grads, owns, others = (refs[:2], refs[2:4]), refs[4:6], refs[6:8], refs[8:10]
+        post, chooser, qkvs, probs = refs[10], refs[11], refs[12:14], refs[14:16]
+        in_ref, out_ref = refs[16:18]
+        grad_all, selected_all, pack_all, part_all, post_out, bias_out = refs[18:24]
+        in_buffer, out_buffer, post_each, sems = refs[24:]
         weights = Weights(
             meta,
             0,
@@ -706,9 +750,13 @@
         for side in (0, 1):
             here = spans[side]
             low = back_through_norm(
-                tops[side], joint, here, post[1:2], grad_all, post_each.at[side]
+                tops[side],
+                grads[side][...],
+                summed(owns[side], others[side]),
+                post[1:2],
+                grad_all.at[here],
+                post_each.at[side],
             )
-            select_rows(low, chooser, selected_all.at[here], packs[side])
             lows.append(low)
         post_out[...] = post_each[0] + post_each[1]
         leave = weights.get(0)
@@ -722,20 +770,22 @@
             attend_back(
                 qkvs[side][0], qkvs[1 - side][1], qkvs[1 - side][2], probs[side], context, emit
             )
+        for side in (0, 1):
+            select_rows(lows[side], chooser, selected_all.at[spans[side]], packs[side])
         bias_out[0:1] = column_sum(pack_all[:, HALF : HALF + width].astype(f32))
         bias_out[1:2] = column_sum(pack_all[:, HALF + 2 * width :].astype(f32))
         flush(pack_all, selected_all)
         part_all[...] = back_to_input(pack_all, weights, 1, width)
 
     ins = [(meta, "s")] + [(item, "h") for top in tops for item in top]
-    ins += list(zip(joint, "hhf"))
-    ins += [(post, "f"), (chooser, "f")] + [(a, "h") for a in (*qkvs, *probs)]
+    ins += [(item, "h") for item in (*grads, *owns)] + [(item, "f") for item in others]
+    ins += [(item, "h") for item in (post, chooser, *qkvs, *probs)]
     ins += [(cross_in, "w"), (cross_out, "w")]
     outs = [
-        ((total, D), f32, "h"),
+        ((total, D), f32, "v"),
         ((total, HALF), bf16, "h"),
         ((total, HALF + 3 * width), bf16, "h"),
-        ((total, D), bf16, "h"),
+        ((total, D), bf16, "v"),
         ((3, D), f32, "h"),
         ((2, width), f32, "h"),
     ]
@@ -749,11 +799,11 @@
 
 
 class Block:
-    def __init__(self, in_selected, in_packs, in_gots, out_selected, out_pack, out_got):
-        self.parts = [*in_selected, *in_packs, *in_gots, out_selected, out_pack, out_got]
-        self.joined = len(in_packs) == 1
+    def __init__(self, in_selected, in_packs, in_gots, out_selected, out_packs, out_gots):
+        self.parts = [*in_selected, *in_packs, *in_gots, out_selected, *out_packs, *out_gots]
+        self.counts = (len(in_packs), len(out_packs))
         self.kinds = "w" * len(self.parts)
-        self.sizes = (out_pack.shape[1] - HALF, in_packs[0].shape[1] - HALF)
+        self.sizes = (out_packs[0].shape[1] - HALF, in_packs[0].shape[1] - HALF)
         self.rows = [array.shape[0] for array in in_selected]
 
     def buffers(self):
@@ -766,20 +816,21 @@
     def fetch(self, refs, buffers, sems, at):
         spans = spans_of(self.rows)
         in_selected, rest = refs[:2], refs[2:]
-        if self.joined:
-            pack, got, rest = [rest[0]] * 2, [rest[1]] * 2, rest[2:]
-        else:
-            pack, got, rest = rest[:2], rest[2:4], rest[4:]
-        out_selected, out_pack, out_got = rest
+        n_in, n_out = self.counts
+        pack, got, rest = rest[:n_in], rest[n_in : 2 * n_in], rest[2 * n_in :]
+        out_selected, out_pack, out_got = rest[0], rest[1 : 1 + n_out], rest[1 + n_out :]
+
+        def rows_of(items, side):
+            return items[0].at[spans[side]] if len(items) == 1 else items[side]
+
         result = []
         for side in (0, 1):
-            here, count = spans[side], self.rows[side]
-            inner = here if self.joined else slice(0, count)
+            count = self.rows[side]
             per_side = []
-            for kind, (selected, own, other, span) in enumerate(
+            for kind, (selected, own, other) in enumerate(
                 (
-                    (in_selected[side], pack[side].at[inner], got[side].at[inner], None),
-                    (out_selected.at[here], out_pack.at[here], out_got.at[here], here),
+                    (in_selected[side], rows_of(pack, side), rows_of(got, side)),
+                    (out_selected.at[spans[side]], rows_of(out_pack, side), rows_of(out_got, side)),
                 )
             ):
                 buffer = buffers[2 * side + kind]
@@ -808,7 +859,7 @@
     return [(s, z) for z in range(groups) for s in ((0, 1) if z % 2 == 0 else (1, 0))]
 
 
-def gradients(blocks, cross, groups, name, ties=()):
+def gradients(meta, blocks, cross, groups, name, ties=(), split=False):
     chunk = HALF // groups
     half = chunk // 2
     size = chunk + half if cross else chunk
@@ -817,10 +868,10 @@
     width = sum(sum(block.sizes) for block in blocks)
     every = blocks + ([cross] if cross else [])
     n_in = sum(len(block.parts) for block in every)
-    n_out = 1 if aligned else 3 if cross else 2
+    n_out = 2 if split else 1 if aligned else 3 if cross else 2
     n_sems = 12 * len(every) + 4 * len(every)
 
-    def body(flush, *refs):
+    def body(flush, meta, *refs):
         inputs, outputs, rest = refs[:n_in], refs[n_in : n_in + n_out], list(refs[n_in + n_out :])
         if cross:
             cross_stage = rest.pop()
@@ -835,6 +886,13 @@
         waited, leaving = set(), []
 
         def leave(source, side, columns, at):
+            if split:
+                kept = pltpu.make_async_copy(source, outputs[0].at[:, columns], sems.at[at])
+                sent = pltpu.make_async_copy(source, outputs[1].at[:, columns], sems.at[at])
+                pl.when(meta[0] == side)(kept.start)
+                pl.when(meta[0] != side)(sent.start)
+                leaving.append(kept)
+                return
             if not aligned:
                 copies = [(source, outputs[side].at[:, columns])]
             elif side < 2:
@@ -898,8 +956,8 @@
         for copy in leaving:
             copy.wait()
 
-    ins = [pair for block in every for pair in zip(block.parts, block.kinds)]
-    if aligned:
+    ins = [(meta, "s")] + [pair for block in every for pair in zip(block.parts, block.kinds)]
+    if aligned and not split:
         outs = [((2 * groups * size, width), bf16, "w")]
     else:
         outs = [((HALF, width), bf16, "w")] * n_out
@@ -913,6 +971,8 @@
     else:
         scratch += [pltpu.SemaphoreType.DMA((n_sems,)), pltpu.VMEM((2, HALF, width), bf16)]
     result = call(body, ins, outs, scratch, 6.0, name, ties, 20)
+    if split:
+        return result
     if aligned:
         return result[0]
     chunks = [result[side].reshape(groups, chunk, width) for side in (0, 1)]
@@ -1045,7 +1105,7 @@
     att_out = (attention_out, swap(attention_out, "section"))
     states = [flat(word_state), flat(region_state)]
     feed_in_later, feed_out_later, *_ = lax.optimization_barrier(
-        (feed_in, feed_out, att_in[1], att_out[1], smalls[0], chooser, *states)
+        (feed_in, feed_out, att_in[1], att_out[1], smalls[0], chooser, cross_chooser, *states)
     )
     ff_in = (feed_in, swap(feed_in_later, "section"))
     ff_out = (feed_out, swap(feed_out_later, "section"))
@@ -1100,7 +1160,6 @@
         cross_entry,
         cross_bias,
         cross_out,
-        [(value, "a") for value in cotangents],
     )
     cross = (cross_w, cross_r)
     got = over_mp(cross, 7)
@@ -1108,7 +1167,7 @@
     self1 = in_order(
         lambda side, place, ties: self_forward(
             side, 1, batch, meta, cross[side][0], (cross[side][7], got[side], cross_post),
-            small[1][side], chooser, att_in, att_out, place, ties + (self0_there,),
+            small[1][side], chooser, att_in, att_out, place, ties + ((self0_there, "a"), (cotangents[side], "w")),
         ),
         3,
     )
@@ -1117,7 +1176,7 @@
     feed1 = in_order(
         lambda side, place, ties: feed_forward(
             side, 1, batch, meta, self1[side][6], self1[side][4], got[side], small[1][side], chooser,
-            ff_in, ff_out, place, ties + (cross_there if side == 0 else feed0_there,),
+            ff_in, ff_out, place, ties + ((cross_there if side == 0 else feed0_there, "a"),),
         ),
         4,
         self1[0][5],
@@ -1127,67 +1186,84 @@
     self1_there = swap(self1[0][3], "dp")
     feed1_there = [swap(feed1[side][4], "dp") for side in both]
 
-    back_feed1 = feed_backward(
-        1,
-        batch,
-        meta,
-        [(feed1[side][0], feed1[side][6], got[side], cotangents[side]) for side in both],
-        None,
-        small[1],
-        chooser,
-        [feed1[side][5] for side in both],
-        ff_in,
-        ff_out,
-        feed1_there[1:],
-    )
-    got = swap(back_feed1[3], "mp")
-    back_feed1_there = swap(back_feed1[2], "dp")
+    given, back_feed1 = None, [None, None]
+    for side in (1, 0):
+        given = feed_backward(
+            1,
+            (side,),
+            rows,
+            batch,
+            meta,
+            [(feed1[side][0], feed1[side][6], got[side], cotangents[side])],
+            None,
+            [small[1][side]],
+            chooser,
+            [feed1[side][5]],
+            ff_in,
+            ff_out,
+            ((feed1_there[side], "a"),),
+            given,
+        )
+        back_feed1[side] = given
+    got = over_mp(back_feed1, 3)
+    back_feed1_there = [swap(back_feed1[side][2], "dp") for side in both]
 
     def scatter(value):
         return lax.psum_scatter(
             value, ("section", "dp"), scatter_dimension=0, axis_index_groups=chains, tiled=True
         )
 
-    back_self1 = self_backward(
-        1,
+    given, back_self1 = None, [None, None]
+    for side in (1, 0):
+        given = self_backward(
+            1,
+            (side,),
+            rows,
+            meta,
+            [feed1[side][1:3]],
+            (back_feed1[side][0], back_feed1[side][3], got[side]),
+            [small[1][side]],
+            chooser,
+            [self1[side][0]],
+            [self1[side][1]],
+            att_in,
+            att_out,
+            (),
+            given,
+        )
+        back_self1[side] = given
+    got = over_mp(back_self1, 3)
+    feed1_grads = gradients(
         meta,
-        [feed1[side][1:3] for side in both],
-        (back_feed1[0], back_feed1[3], got),
-        small[1],
-        chooser,
-        [self1[side][0] for side in both],
-        [self1[side][1] for side in both],
-        att_in,
-        att_out,
-    )
-    got = swap(back_self1[3], "mp")
-    feed1_grads = gradients(
         [
             Block(
                 [feed1[side][3] for side in both],
                 [feed1[side][4] for side in both],
                 feed1_there,
-                *back_feed1[1:3],
+                back_feed1[0][1],
+                [back_feed1[side][2] for side in both],
                 back_feed1_there,
             )
         ],
         None,
         groups,
         "feed_gradients_1",
-        (back_self1[5],),
-    )
-    back_self1_there = swap(back_self1[2], "dp")
+        (back_self1[0][5],),
+    )
+    back_self1_there = swap(back_self1[0][2], "dp")
     back_cross = cross_backward(
         meta,
         [self1[side][7:9] for side in both],
-        (back_self1[0], back_self1[3], got),
+        [back_self1[side][0] for side in both],
+        [back_self1[side][3] for side in both],
+        got,
         cross_post,
         cross_chooser,
         [cross[side][5] for side in both],
         [cross[side][6] for side in both],
         cross_entry,
         cross_out,
-        (feed1_grads, (self1_there, "w")),
+        (feed1_grads, (self1_there, "a")),
     )
     cross_post_grad, cross_bias_grad = back_cross[4:6]
     got = swap(back_cross[3], "mp")
@@ -1196,35 +1272,40 @@
 
     back_feed0 = feed_backward(
         0,
+        (1, 0),
+        rows,
         batch,
         meta,
-        [cross[side][1:3] for side in both],
+        [cross[side][1:3] for side in (1, 0)],
         (back_cross[0], back_cross[3], got),
-        small[0],
+        small[0][::-1],
         chooser,
-        [feed0[side][5] for side in both],
+        [feed0[side][5] for side in (1, 0)],
         ff_in,
         ff_out,
-        ((back_self1_there, "w"),),
+        ((back_self1_there, "a"),),
     )
     got = swap(back_feed0[3], "mp")
     back_feed0_there = swap(back_feed0[2], "dp")
     late1_grads = gradients(
+        meta,
         [
             Block(
                 [self1[side][2] for side in both],
                 [self1[0][3]],
                 [self1_there],
-                *back_self1[1:3],
-                back_self1_there,
+                back_self1[0][1],
+                [back_self1[0][2]],
+                [back_self1_there],
             )
         ],
         Block(
             [cross[side][4] for side in both],
             [cross_pack],
             [cross_there],
-            *back_cross[1:3],
-            back_cross_there,
+            back_cross[1],
+            [back_cross[2]],
+            [back_cross_there],
         ),
         groups,
         "late_gradients_1",
@@ -1232,47 +1313,58 @@
     )
     back_self0 = self_backward(
         0,
+        (1, 0),
+        rows,
         meta,
-        [feed0[side][1:3] for side in both],
+        [feed0[side][1:3] for side in (1, 0)],
         (back_feed0[0], back_feed0[3], got),
-        small[0],
+        small[0][::-1],
         chooser,
-        [self0[side][0] for side in both],
-        [self0[side][1] for side in both],
+        [self0[side][0] for side in (1, 0)],
+        [self0[side][1] for side in (1, 0)],
         att_in,
         att_out,
         (late1_grads,),
     )
     got = swap(back_self0[3], "mp")
     back_self0_there = swap(back_self0[2], "dp")
-    late1_grads, feed1_share, back_feed0_there, _ = lax.optimization_barrier(
-        (late1_grads, feed1_share, back_feed0_there, back_self0[5])
-    )
     late1_share = scatter(late1_grads)
     layer0_grads = gradients(
+        meta,
         [
             Block(
                 [feed0[side][3] for side in both],
                 [feed0[0][4]],
                 [feed0_there],
-                *back_feed0[1:3],
-                back_feed0_there,
+                back_feed0[1],
+                [back_feed0[2]],
+                [back_feed0_there],
             ),
             Block(
                 [self0[side][2] for side in both],
                 [self0[0][3]],
                 [self0_there],
-                *back_self0[1:3],
-                back_self0_there,
+                back_self0[1],
+                [back_self0[2]],
+                [back_self0_there],
             ),
         ],
         None,
         groups,
         "gradients_0",
-        (back_self0[5],),
-    )
-    layer0_grads, late1_share = lax.optimization_barrier((layer0_grads, late1_share))
-    layer0_share = scatter(layer0_grads)
+        (back_self0[5], feed1_share),
+        True,
+    )
+    layer0_kept, layer0_sent = layer0_grads
+    layer0_total = layer0_kept.astype(f32) + swap(layer0_sent, "section").astype(f32)
+    layer0_total, late1_share = lax.optimization_barrier((layer0_total.astype(bf16), late1_share))
+    layer0_share = lax.psum_scatter(
+        layer0_total,
+        "dp",
+        scatter_dimension=0,
+        axis_index_groups=[[2 * z + y for z in range(groups)] for y in both],
+        tiled=True,
+    )
     chunk = D // dp_count
 
     state_grad = (back_self0[0] + (back_self0[3].astype(f32) + got.astype(f32))).astype(bf16)
@@ -1307,12 +1399,12 @@
             ),
         ),
         packed(
-            back_self1,
-            back_feed1,
+            back_self1[0],
+            back_feed1[0],
             squares_of(
                 [self1[side][5] for side in both],
                 [feed1[side][7] for side in both],
-                [back_feed1[8][side] for side in both],
+                [back_feed1[0][6][side] for side in both],
             ),
         ),
     ]
@@ -1350,8 +1442,8 @@
         lax.ppermute(value, "section", [(0, 1)]) for value in (feed1_share, late1_share[:chunk])
     ]
     outputs = (
-        unflat(back_feed1[6]),
-        unflat(back_feed1[7]),
+        unflat(back_feed1[0][7]),
+        unflat(back_feed1[1][7]),
         unflat(state_grad[spans[0]]),
         unflat(state_grad[spans[1]]),
         cross_bias_total,

time: 360 us -> 327 us (0.908)
  waiting for transfers between devices: 138 us -> 116 us
  local copies, waits for them, and re-layouts: 33.3 us -> 23.1 us
  other arithmetic: 7.21 us -> 11.9 us
    reduce_scatter x3 -> x2, waiting for transfers between devices: 70.7 us -> 6.45 us  [scatter(): lax.psum_scatter(value, ('section', 'dp'), scatter_dimension=0, axis_inde...]
    reduce_scatter x0 -> x1, waiting for transfers between devices: none -> 30.2 us  [on_device(): lax.psum_scatter(layer0_total, 'dp', scatter_dimension=0, axis_index_grou...]
    ppermute x35 -> x39, waiting for transfers between devices: 65.4 us -> 76.9 us  [swap(): return lax.ppermute(value, axis, [(i, i ^ distance) for i in range(count)])]
    unnamed x164 -> x188, local copies, waits for them, and re-layouts: 18.4 us -> 10.6 us
    convert_element_type x0 -> x1, other arithmetic: none -> 4.65 us  [on_device(): layer0_total.astype(bf16)]
    pallas_call x18 -> x20, Pallas kernels: 119 us -> 116 us  [call(): pl.pallas_call(whole, out_shape=[spaces[out[2]]((out[3], *out[0][1:]) if...]
    ppermute x35 -> x39, starting transfers between devices: 35.3 us -> 34.4 us  [swap(): return lax.ppermute(value, axis, [(i, i ^ distance) for i in range(count)])]
  transfers between devices with their start and end apart: 41 -> 45, of which waited for: 21 -> 21; matrix products, arithmetic and copies ran while one was open for 7% -> 8% of each run, Pallas kernels for 27% -> 33%
where the time goes in v1:
time: 327 us; the launch traced here: 321 us
  waiting for transfers between devices  116 us (35%)
  Pallas kernels  116 us (35%)
  starting transfers between devices  38.9 us (12%)
  local copies, waits for them, and re-layouts  23.1 us (7%)
  between operations  15.7 us (5%)
  other arithmetic  11.9 us (4%)
    pallas_call x20, Pallas kernels, call(): pl.pallas_call(whole, out_shape=[spaces[out[2]]((out[3], *out[0][1:]) if...  116 us
    ppermute x39, waiting for transfers between devices, swap(): return lax.ppermute(value, axis, [(i, i ^ distance) for i in range(count)])  76.9 us
    ppermute x39, starting transfers between devices, swap(): return lax.ppermute(value, axis, [(i, i ^ distance) for i in range(count)])  34.4 us
    reduce_scatter x1, waiting for transfers between devices, on_device(): lax.psum_scatter(layer0_total, 'dp', scatter_dimension=0, axis_index_grou...  30.2 us
    unnamed x188, local copies, waits for them, and re-layouts  10.6 us
  transfers between devices with their start and end apart: 45, of which 21 were waited for; matrix products, arithmetic and copies ran while one was open for 8% of the time, Pallas kernels for 33%

profile of v1, /device:TPU:0, one launch (start us, length us, event | category | flops | bytes accessed | tf_op | source)
XLA Modules:
  0.0 321.0 jit_solution(13558271293613970969)
XLA Ops:
  11.4 1.4 fusion.1.refs_9_.refs_12_
  16.3 4.0 %self_forward_0_1.1 = (bf16[3,144,384]{2,1,0:T(8,128)(2,1)}, bf16[6,144,144]{2,1,0:T(8,128)(2,1)}, bf16[144,384]{1,0:T(8,128)(2,1)}, bf16[224,768]{1,0:T(8,128)(...) custom-call(s32[9]{0:T(128)S(1)} %pad_add_fusion.refs_0_, bf16[144,768]{1,0:T(8,128)(2,1)S(1)} %reshape.199.refs_1_, ...), custom_call_target="tpu_custom_call" | custom-call | flops 2300000000 | tf_op jit(solution)/shard_map/self_forward_0_1/pallas_call | solution.py:249
  20.3 2.9 collective-permute-start.6
  23.3 3.6 %self_forward_0_0.1 = (bf16[3,80,384]{2,1,0:T(8,128)(2,1)}, bf16[6,80,80]{2,1,0:T(8,128)(2,1)}, bf16[80,384]{1,0:T(8,128)(2,1)}, bf16[224,768]{1,0:T(8,128)(2,1)...) custom-call(s32[9]{0:T(128)S(1)} %pad_add_fusion.refs_0_, ...), custom_call_target="tpu_custom_call", output_to_operand_aliasing={{3}: (8, {})} | custom-call | flops 2300000000 | tf_op jit(solution)/shard_map/self_forward_0_0/pallas_call | solution.py:249
  26.9 2.1 collective-permute-done.6.refs_3_
  29.1 1.5 collective-permute-done.5.refs_9_.refs_11_.refs_16_
  30.6 5.0 %feed_forward_0_1.1 = (f32[144,768]{1,0:T(8,128)S(1)}, f32[144,768]{1,0:T(8,128)}, f32[144,1]{1,0:T(8,128)}, bf16[144,384]{1,0:T(8,128)(2,1)}, bf16[224,1920]{1,...) custom-call(s32[9]{0:T(128)S(1)} %pad_add_fusion.refs_0_, ...), custom_call_target="tpu_custom_call" | custom-call | flops 2472499968 | tf_op jit(solution)/shard_map/feed_forward_0_1/pallas_call | solution.py:249
  36.4 2.8 collective-permute-start.9
  39.2 3.8 %feed_forward_0_0.1 = (f32[80,768]{1,0:T(8,128)S(1)}, f32[80,768]{1,0:T(8,128)}, f32[80,1]{1,0:T(8,128)}, bf16[80,384]{1,0:T(8,128)(2,1)}, bf16[224,1920]{1,0:T(...) custom-call(s32[9]{0:T(128)S(1)} %pad_add_fusion.refs_0_, ...), custom_call_target="tpu_custom_call", output_to_operand_aliasing={{4}: (10, {})} | custom-call | flops 2472499968 | tf_op jit(solution)/shard_map/feed_forward_0_0/pallas_call | solution.py:249
  43.9 1.7 reshape.200.refs_12_.refs_4_
  45.6 2.2 collective-permute-start.12
  51.1 7.3 %cross_forward.1 = (bf16[80,768]{1,0:T(8,128)(2,1)S(1)}, f32[80,768]{1,0:T(8,128)}, f32[80,1]{1,0:T(8,128)}, f32[2,128]{1,0:T(2,128)}, bf16[80,384]{1,0:T(8,128)...) custom-call(s32[9]{0:T(128)S(1)} %pad_add_fusion.refs_0_, ...), custom_call_target="tpu_custom_call" | custom-call | flops 3910000128 | tf_op jit(solution)/shard_map/cross_forward/pallas_call | solution.py:249
  58.4 1.5 collective-permute-start.11
  60.5 5.6 %collective-permute-done.11.refs_3_ = bf16[144,768]{1,0:T(8,128)(2,1)S(1)} collective-permute-done((bf16[144,768]{1,0:T(8,128)(2,1)S(1)}, bf16[144,768]{1,0:T(8,128)(2,1)S(1)}, u32[]{:S(2)}, u32[]{:S(2)}) %collective-permute-start.11) | collective-permute-done | bytes 221216 | tf_op jit(solution)/shard_map/ppermute | solution.py:1033
  66.1 4.8 %self_forward_1_1.1 = (bf16[3,144,384]{2,1,0:T(8,128)(2,1)}, bf16[6,144,144]{2,1,0:T(8,128)(2,1)}, bf16[144,384]{1,0:T(8,128)(2,1)}, bf16[224,768]{1,0:T(8,128)(...) custom-call(s32[9]{0:T(128)S(1)} %pad_add_fusion.refs_0_, ...), custom_call_target="tpu_custom_call" | custom-call | flops 2300000000 | tf_op jit(solution)/shard_map/self_forward_1_1/pallas_call | solution.py:249
  70.9 1.5 collective-permute-start.14
  73.1 1.5 collective-permute-start.15
  74.6 4.0 %self_forward_1_0.1 = (bf16[3,80,384]{2,1,0:T(8,128)(2,1)}, bf16[6,80,80]{2,1,0:T(8,128)(2,1)}, bf16[80,384]{1,0:T(8,128)(2,1)}, bf16[224,768]{1,0:T(8,128)(2,1)...) custom-call(s32[9]{0:T(128)S(1)} %pad_add_fusion.refs_0_, ...), custom_call_target="tpu_custom_call", output_to_operand_aliasing={{3}: (11, {})} | custom-call | flops 2300000000 | tf_op jit(solution)/shard_map/self_forward_1_0/pallas_call | solution.py:249
  78.7 4.9 %feed_forward_1_1.1 = (f32[144,768]{1,0:T(8,128)S(1)}, f32[144,768]{1,0:T(8,128)}, f32[144,1]{1,0:T(8,128)}, bf16[144,384]{1,0:T(8,128)(2,1)}, bf16[144,1920]{1,...) custom-call(s32[9]{0:T(128)S(1)} %pad_add_fusion.refs_0_, ...), custom_call_target="tpu_custom_call" | custom-call | flops 2472499968 | tf_op jit(solution)/shard_map/feed_forward_1_1/pallas_call | solution.py:249
  86.1 2.9 collective-permute-done.13.refs_3_
  89.0 4.4 %feed_forward_1_0.1 = (f32[80,768]{1,0:T(8,128)S(1)}, f32[80,768]{1,0:T(8,128)}, f32[80,1]{1,0:T(8,128)}, bf16[80,384]{1,0:T(8,128)(2,1)}, bf16[80,1920]{1,0:T(8...) custom-call(s32[9]{0:T(128)S(1)} %pad_add_fusion.refs_0_, ...), custom_call_target="tpu_custom_call" | custom-call | flops 2472499968 | tf_op jit(solution)/shard_map/feed_forward_1_0/pallas_call | solution.py:249
  93.4 1.6 collective-permute-start.19
  96.6 4.9 %feed_backward_1_1.1 = (f32[144,768]{1,0:T(8,128)S(1)}, bf16[224,384]{1,0:T(8,128)(2,1)}, bf16[144,1920]{1,0:T(8,128)(2,1)}, bf16[144,768]{1,0:T(8,128)(2,1)S(1)...) custom-call(s32[9]{0:T(128)S(1)} %pad_add_fusion.refs_0_, ...), custom_call_target="tpu_custom_call" | custom-call | flops 4066071552 | tf_op jit(solution)/shard_map/feed_backward_1_1/pallas_call | solution.py:249
  101.6 1.7 collective-permute-start.21
  103.4 4.5 %feed_backward_1_0.1 = (f32[80,768]{1,0:T(8,128)S(1)}, bf16[224,384]{1,0:T(8,128)(2,1)}, bf16[80,1920]{1,0:T(8,128)(2,1)}, bf16[80,768]{1,0:T(8,128)(2,1)S(1)}, ...) custom-call(s32[9]{0:T(128)S(1)} %pad_add_fusion.refs_0_, ...), custom_call_target="tpu_custom_call", output_to_operand_aliasing={{1}: (12, {}), {4}: (13, {}), {5}: (14, {}), {6}: (15, {})} | custom-call | flops 2258928640 | tf_op jit(solution)/shard_map/feed_backward_1_0/pallas_call | solution.py:249
  108.4 1.7 collective-permute-start.24
  110.5 6.2 %self_backward_1_1.1 = (f32[144,768]{1,0:T(8,128)}, bf16[224,384]{1,0:T(8,128)(2,1)}, bf16[224,1536]{1,0:T(8,128)(2,1)}, bf16[144,768]{1,0:T(8,128)(2,1)}, f32[2,3,768]{2,1,0:T(4,128)}, /*index=5*/f32[2,2,384]{2,1,0:T(2,128)}) custom-call(s32[9]{0:T(128)S(1)} %pad_add_fusion.refs_0_, f32[144,768]{1,0:T(8,128)S(1)} %copy-done.33, f32[144,1]{1,0:T(8,128)S(1)} %copy-done.42, ...), custom_call_target="tpu_custom_call" | custom-call | flops 4435714048 | tf_op jit(solution)/shard_map/self_backward_1_1/pallas_call | solution.py:249
  116.8 5.7 %self_backward_1_0.1 = (f32[80,768]{1,0:T(8,128)}, bf16[224,384]{1,0:T(8,128)(2,1)}, bf16[224,1536]{1,0:T(8,128)(2,1)}, bf16[80,768]{1,0:T(8,128)(2,1)}, f32[2,3,768]{2,1,0:T(4,128)}, /*index=5*/f32[2,2,384]{2,1,0:T(2,128)}) custom-call(s32[9]{0:T(128)S(1)} %pad_add_fusion.refs_0_, ...), custom_call_target="tpu_custom_call", output_to_operand_aliasing={{1}: (14, {}), {2}: (15, {}), {4}: (16, {}), {5}: (17, {})} | custom-call | flops 2464285696 | tf_op jit(solution)/shard_map/self_backward_1_0/pallas_call | solution.py:249
  124.5 5.7 %feed_gradients_1.1.refs_19_ = bf16[768,3072]{1,0:T(8,128)(2,1)} custom-call(s32[9]{0:T(128)S(1)} %pad_add_fusion.refs_0_, bf16[80,384]{1,0:T(8,128)(2,1)} %get-tuple-element.241.refs_1_, bf16[144,384]{1,0:T(8,128)(2,1)} %get-tuple-element.242.refs_2_, bf16[80,1920]{1,0:T(8,128)(2,1)} %get-tuple-element.218.refs_3_, ...), custom_call_target="tpu_custom_call" | custom-call | flops 3449999872 | tf_op jit(solution)/shard_map/feed_gradients_1/pallas_call | solution.py:249
  135.3 6.5 %collective-permute-done.26.refs_20_.refs_4_ = bf16[224,768]{1,0:T(8,128)(2,1)S(1)} collective-permute-done((bf16[224,768]{1,0:T(8,128)(2,1)S(1)}, bf16[224,768]{1,0:T(8,128)(2,1)S(1)}, u32[]{:S(2)}, u32[]{:S(2)}) %collective-permute-start.26) | collective-permute-done | bytes 344096 | tf_op jit(solution)/shard_map/ppermute | solution.py:1033
  141.8 9.3 %cross_backward.1 = (f32[224,768]{1,0:T(8,128)S(1)}, bf16[224,384]{1,0:T(8,128)(2,1)}, bf16[224,1536]{1,0:T(8,128)(2,1)}, bf16[224,768]{1,0:T(8,128)(2,1)S(1)}, f32[3,768]{1,0:T(4,128)}, /*index=5*/f32[2,384]{1,0:T(2,128)}) custom-call(s32[9]{0:T(128)S(1)} %pad_add_fusion.refs_0_, f32[80,768]{1,0:T(8,128)} %get-tuple-element.195.refs_1_, ...), custom_call_target="tpu_custom_call" | custom-call | flops 5750000128 | tf_op jit(solution)/shard_map/cross_backward/pallas_call | solution.py:249
  152.5 6.0 %collective-permute-done.27.refs_7_ = bf16[224,768]{1,0:T(8,128)(2,1)S(1)} collective-permute-done((bf16[224,768]{1,0:T(8,128)(2,1)S(1)}, bf16[224,768]{1,0:T(8,128)(2,1)S(1)}, u32[]{:S(2)}, u32[]{:S(2)}) %collective-permute-start.27) | collective-permute-done | bytes 344096 | tf_op jit(solution)/shard_map/ppermute | solution.py:1033
  158.6 8.4 %feed_backward_0_10.1 = (f32[224,768]{1,0:T(8,128)}, bf16[224,384]{1,0:T(8,128)(2,1)}, bf16[224,1920]{1,0:T(8,128)(2,1)}, bf16[224,768]{1,0:T(8,128)(2,1)}, f32[2,3,768]{2,1,0:T(4,128)}, /*index=5*/f32[2,1,1536]{2,1,0:T(1,128)}) custom-call(s32[9]{0:T(128)S(1)} %pad_add_fusion.refs_0_, f32[144,768]{1,0:T(8,128)S(1)} %copy-done.16, f32[144,1]{1,0:T(8,128)S(1)} %copy-done.26, ...), custom_call_target="tpu_custom_call" | custom-call | flops 6325000192 | tf_op jit(solution)/shard_map/feed_backward_0_10/pallas_call | solution.py:249
  167.8 5.9 %late_gradients_1.1.refs_19_ = bf16[1152,1536]{1,0:T(8,128)(2,1)} custom-call(s32[9]{0:T(128)S(1)} %pad_add_fusion.refs_0_, bf16[80,384]{1,0:T(8,128)(2,1)} %get-tuple-element.267.refs_1_, bf16[144,384]{1,0:T(8,128)(2,1)} %get-tuple-element.268.refs_2_, bf16[224,768]{1,0:T(8,128)(2,1)} %get-tuple-element.247.refs_3_, bf16[224,768]{1,0:T(8,128)(2,1)} %copy-done.36, ...), custom_call_target="tpu_custom_call" | custom-call | flops 3449999872 | tf_op jit(solution)/shard_map/late_gradients_1/pallas_call | solution.py:249
  176.0 6.0 %collective-permute-done.30.refs_7_ = bf16[224,768]{1,0:T(8,128)(2,1)S(1)} collective-permute-done((bf16[224,768]{1,0:T(8,128)(2,1)S(1)}, bf16[224,768]{1,0:T(8,128)(2,1)S(1)}, u32[]{:S(2)}, u32[]{:S(2)}) %collective-permute-start.30) | collective-permute-done | bytes 344096 | tf_op jit(solution)/shard_map/ppermute | solution.py:1033
  182.0 12.6 %self_backward_0_10.1 = (f32[224,768]{1,0:T(8,128)}, bf16[224,384]{1,0:T(8,128)(2,1)}, bf16[224,1536]{1,0:T(8,128)(2,1)}, bf16[224,768]{1,0:T(8,128)(2,1)}, f32[2,3,768]{2,1,0:T(4,128)}, /*index=5*/f32[2,2,384]{2,1,0:T(2,128)}) custom-call(s32[9]{0:T(128)S(1)} %pad_add_fusion.refs_0_, f32[144,768]{1,0:T(8,128)} %get-tuple-element.257.refs_1_, ...), custom_call_target="tpu_custom_call" | custom-call | flops 6899999744 | tf_op jit(solution)/shard_map/self_backward_0_10/pallas_call | solution.py:249
  195.0 10.8 %collective-permute-done.32.refs_14_ = bf16[224,1536]{1,0:T(8,128)(2,1)S(1)} collective-permute-done((bf16[224,1536]{1,0:T(8,128)(2,1)}, bf16[224,1536]{1,0:T(8,128)(2,1)S(1)}, u32[]{:S(2)}, u32[]{:S(2)}) %collective-permute-start.32) | collective-permute-done | bytes 688160 | tf_op jit(solution)/shard_map/ppermute | solution.py:1033
  206.6 7.3 %gradients_0.1 = (bf16[384,4608]{1,0:T(8,128)(2,1)}, bf16[384,4608]{1,0:T(8,128)(2,1)}) custom-call(s32[9]{0:T(128)S(1)} %pad_add_fusion.refs_0_, bf16[80,384]{1,0:T(8,128)(2,1)} %get-tuple-element.177.refs_1_, bf16[144,384]{1,0:T(8,128)(2,1)} %get-tuple-element.178.refs_2_, bf16[224,1920]{1,0:T(8,128)(2,1)} %get-tuple-element.179.refs_3_, ...), custom_call_target="tpu_custom_call" | custom-call | flops 3449999872 | tf_op jit(solution)/shard_map/gradients_0/pallas_call | solution.py:249
  214.0 6.4 %collective-permute-done.33 = bf16[384,4608]{1,0:T(8,128)(2,1)S(1)} collective-permute-done((bf16[384,4608]{1,0:T(8,128)(2,1)}, bf16[384,4608]{1,0:T(8,128)(2,1)S(1)}, u32[]{:S(2)}, u32[]{:S(2)}) %collective-permute-start.33) | collective-permute-done | bytes 3538976 | tf_op jit(solution)/shard_map/ppermute | solution.py:1033
  220.4 4.7 %add_convert_fusion = bf16[384,4608]{1,0:T(8,128)(2,1)} fusion(bf16[384,4608]{1,0:T(8,128)(2,1)S(1)} %collective-permute-done.33, bf16[384,4608]{1,0:T(8,128)(2,1)} %get-tuple-element.278), kind=kLoop, calls=%fused_computation | loop fusion | flops 7077888 | bytes 10616832 | tf_op jit(solution)/shard_map/convert_element_type | solution.py:1360
  225.3 6.5 %reduce-scatter.6.cloned.1.call-done.refs_2_ = bf16[144,1536]{1,0:T(8,128)(2,1)} async-done(((bf16[1152,1536]{1,0:T(8,128)(2,1)}), bf16[144,1536]{1,0:T(8,128)(2,1)}) %reduce-scatter.6.cloned.1.call-update) | async-done | bytes 442384 | tf_op jit(solution)/shard_map/reduce_scatter | solution.py:1212
  238.2 3.5 %collective-permute-done.38 = f32[25,768]{1,0:T(8,128)S(1)} collective-permute-done((f32[25,768]{1,0:T(8,128)S(1)}, f32[25,768]{1,0:T(8,128)S(1)}, u32[]{:S(2)}, u32[]{:S(2)}) %collective-permute-start.38) | collective-permute-done | bytes 76832 | tf_op jit(solution)/shard_map/ppermute | solution.py:1033
  241.9 9.0 %collective-permute-done.39 = f32[25,768]{1,0:T(8,128)S(1)} collective-permute-done((f32[25,768]{1,0:T(8,128)S(1)}, f32[25,768]{1,0:T(8,128)S(1)}, u32[]{:S(2)}, u32[]{:S(2)}) %collective-permute-start.39) | collective-permute-done | bytes 76832 | tf_op jit(solution)/shard_map/ppermute | solution.py:1033
  252.7 1.8 collective-permute-start.36
  254.5 10.5 %collective-permute-done.40 = f32[25,768]{1,0:T(8,128)S(1)} collective-permute-done((f32[25,768]{1,0:T(8,128)S(1)}, f32[25,768]{1,0:T(8,128)S(1)}, u32[]{:S(2)}, u32[]{:S(2)}) %collective-permute-start.40) | collective-permute-done | bytes 76832 | tf_op jit(solution)/shard_map/ppermute | solution.py:1033
  274.4 30.2 %reduce-scatter.8.cloned.1.call-done.refs_5_ = bf16[96,4608]{1,0:T(8,128)(2,1)} async-done(((bf16[384,4608]{1,0:T(8,128)(2,1)}), bf16[96,4608]{1,0:T(8,128)(2,1)}) %reduce-scatter.8.cloned.1.call-update) | async-done | bytes 884752 | tf_op jit(solution)/shard_map/reduce_scatter | solution.py:1361
  307.2 2.0 collective-permute-done.41.refs_6_
  310.3 3.7 %placed_gradients.1 = (f32[2,96,1536]{2,1,0:T(8,128)}, f32[2,96,1536]{2,1,0:T(8,128)}, f32[2,3,96,384]{3,2,1,0:T(8,128)}, f32[2,96,384]{2,1,0:T(8,128)}, f32[3,48,384]{2,1,0:T(8,128)}, /*index=5*/f32[48,384]{1,0:T(8,128)}) custom-call(s32[9]{0:T(128)S(1)} %pad_add_fusion.refs_0_, bf16[96,3072]{1,0:T(8,128)(2,1)S(1)} %copy-done.31, ...), custom_call_target="tpu_custom_call" | custom-call | flops 2300000000 | tf_op jit(solution)/shard_map/placed_gradients/pallas_call | solution.py:249
  (328 shorter events, 53.2 us)
Async XLA Ops:
  7.2 198.5 %reduce-scatter.4.cloned.1.call-start = ((), (), s32[]{:S(2)}) async-start(), calls=%async_computation.3 | async-start | bytes 5308416 | tf_op jit(solution)/shard_map/reduce_scatter | solution.py:1212
  7.3 8.4 %collective-permute-start.1 = (bf16[1,2,3,768,384]{4,3,2,1,0:T(8,128)(2,1)}, bf16[1,2,3,768,384]{4,3,2,1,0:T(8,128)(2,1)}, u32[]{:S(2)}, u32[]{:S(2)}) collective-permute-start(bf16[1,2,3,768,384]{4,3,2,1,0:T(8,128)(2,1)} %bitcast.82), channel_id=1, source_target_pairs={{0,16},{16,0},{1,17},{17,1},{2,18},{18,2},{3,19},{19,3},{4,20},{20... | collective-permute-start | bytes 10616840 | tf_op jit(solution)/shard_map/ppermute | solution.py:1033
  10.2 3.7 %collective-permute-start = (f32[2,16,768]{2,1,0:T(8,128)S(1)}, f32[2,16,768]{2,1,0:T(8,128)S(1)}, u32[]{:S(2)}, u32[]{:S(2)}) collective-permute-start(f32[2,16,768]{2,1,0:T(8,128)S(1)} %concatenate.31), channel_id=1, source_target_pairs={{0,16},{16,0},{1,17},{17,1},{2,18},{18,2},{3,19},{19,3},{4,20},{20... | collective-permute-start | bytes 294920 | tf_op jit(solution)/shard_map/ppermute | solution.py:1033
  10.4 5.3 %collective-permute-start.2 = (bf16[1,2,384,768]{3,2,1,0:T(8,128)(2,1)}, bf16[1,2,384,768]{3,2,1,0:T(8,128)(2,1)S(1)}, u32[]{:S(2)}, u32[]{:S(2)}) collective-permute-start(bf16[1,2,384,768]{3,2,1,0:T(8,128)(2,1)} %refs_17_.1), channel_id=1, source_target_pairs={{0,16},{16,0},{1,17},{17,1},{2,18},{18,2},{3,19},{19,3},{4,20},{20... | collective-permute-start | bytes 3538952 | tf_op jit(solution)/shard_map/ppermute | solution.py:1033
  11.4 147.1 %copy-start.4 = (bf16[768,768]{1,0:T(8,128)(2,1)}, bf16[768,768]{1,0:T(8,128)(2,1)S(1)}, u32[]{:S(2)}) copy-start(bf16[768,768]{1,0:T(8,128)(2,1)S(1)} %fusion.refs_3_.refs_5_.refs_6_.refs_7_.refs_10_) | copy-start | bytes 3538948
  15.7 13.4 %collective-permute-start.4 = (bf16[1,2,768,1536]{3,2,1,0:T(8,128)(2,1)}, bf16[1,2,768,1536]{3,2,1,0:T(8,128)(2,1)S(1)}, u32[]{:S(2)}, u32[]{:S(2)}) collective-permute-start(bf16[1,2,768,1536]{3,2,1,0:T(8,128)(2,1)} %refs_13_.1), channel_id=1, source_target_pairs={{0,16},{16,0},{1,17},{17,1},{2,18},{18,2},{3,19},{19,3},{4,20},{20... | collective-permute-start | bytes 14155784 | tf_op jit(solution)/shard_map/ppermute | solution.py:1033
  16.1 14.5 %collective-permute-start.5 = (bf16[1,2,1536,768]{3,2,1,0:T(8,128)(2,1)}, bf16[1,2,1536,768]{3,2,1,0:T(8,128)(2,1)S(1)}, u32[]{:S(2)}, u32[]{:S(2)}) collective-permute-start(bf16[1,2,1536,768]{3,2,1,0:T(8,128)(2,1)} %refs_15_.1), channel_id=1, source_target_pairs={{0,16},{16,0},{1,17},{17,1},{2,18},{18,2},{3,19},{19,3},{4,20},{20... | collective-permute-start | bytes 14155784 | tf_op jit(solution)/shard_map/ppermute | solution.py:1033
  16.3 142.2 %copy-start.10 = (f32[16,768]{1,0:T(8,128)}, f32[16,768]{1,0:T(8,128)S(1)}, u32[]{:S(2)}) copy-start(f32[16,768]{1,0:T(8,128)S(1)} %get-tuple-element.346.refs_2_.refs_4_.refs_8_) | copy-start | bytes 147460
  16.3 142.2 %copy-start.11 = (f32[16,768]{1,0:T(8,128)}, f32[16,768]{1,0:T(8,128)S(1)}, u32[]{:S(2)}) copy-start(f32[16,768]{1,0:T(8,128)S(1)} %get-tuple-element.347.refs_2_.refs_4_.refs_7_.refs_9_) | copy-start | bytes 147460
  20.3 8.7 %collective-permute-start.6 = (bf16[144,768]{1,0:T(8,128)(2,1)S(1)}, bf16[144,768]{1,0:T(8,128)(2,1)S(1)}, u32[]{:S(2)}, u32[]{:S(2)}) collective-permute-start(bf16[144,768]{1,0:T(8,128)(2,1)S(1)} %get-tuple-element.173.refs_2_), channel_id=1, source_target_pairs={{0,1},{1,0},{2,3},{3,2},{4,5},{5,4},{6,7},{7,6},{8,9},{9,8},{10,11... | collective-permute-start | bytes 663560 | tf_op jit(solution)/shard_map/ppermute | solution.py:1033
  26.8 12.3 %collective-permute-start.3 = (bf16[80,768]{1,0:T(8,128)(2,1)S(1)}, bf16[80,768]{1,0:T(8,128)(2,1)S(1)}, u32[]{:S(2)}, u32[]{:S(2)}) collective-permute-start(bf16[80,768]{1,0:T(8,128)(2,1)S(1)} %get-tuple-element.170.refs_2_), channel_id=1, source_target_pairs={{0,1},{1,0},{2,3},{3,2},{4,5},{5,4},{6,7},{7,6},{8,9},{9,8},{10,11... | collective-permute-start | bytes 368648 | tf_op jit(solution)/shard_map/ppermute | solution.py:1033
  36.4 11.8 %collective-permute-start.9 = (bf16[144,768]{1,0:T(8,128)(2,1)S(1)}, bf16[144,768]{1,0:T(8,128)(2,1)}, u32[]{:S(2)}, u32[]{:S(2)}) collective-permute-start(bf16[144,768]{1,0:T(8,128)(2,1)S(1)} %get-tuple-element.183.refs_5_), channel_id=1, source_target_pairs={{0,1},{1,0},{2,3},{3,2},{4,5},{5,4},{6,7},{7,6},{8,9},{9,8},{10,11... | collective-permute-start | bytes 663560 | tf_op jit(solution)/shard_map/ppermute | solution.py:1033
  43.0 5.2 %collective-permute-start.8 = (bf16[80,768]{1,0:T(8,128)(2,1)S(1)}, bf16[80,768]{1,0:T(8,128)(2,1)S(1)}, u32[]{:S(2)}, u32[]{:S(2)}) collective-permute-start(bf16[80,768]{1,0:T(8,128)(2,1)S(1)} %get-tuple-element.181.refs_2_), channel_id=1, source_target_pairs={{0,1},{1,0},{2,3},{3,2},{4,5},{5,4},{6,7},{7,6},{8,9},{9,8},{10,11... | collective-permute-start | bytes 368648 | tf_op jit(solution)/shard_map/ppermute | solution.py:1033
  45.6 15.0 %collective-permute-start.12 = (bf16[224,768]{1,0:T(8,128)(2,1)}, bf16[224,768]{1,0:T(8,128)(2,1)S(1)}, u32[]{:S(2)}, u32[]{:S(2)}) collective-permute-start(bf16[224,768]{1,0:T(8,128)(2,1)} %get-tuple-element.192.refs_10_), channel_id=1, source_target_pairs={{0,2},{2,0},{4,6},{6,4},{8,10},{10,8},{12,14},{14,12},{1,3},{3,1},... | collective-permute-start | bytes 1032200 | tf_op jit(solution)/shard_map/ppermute | solution.py:1033
  47.7 30.9 %collective-permute-start.7 = (bf16[224,1920]{1,0:T(8,128)(2,1)}, bf16[224,1920]{1,0:T(8,128)(2,1)}, u32[]{:S(2)}, u32[]{:S(2)}) collective-permute-start(bf16[224,1920]{1,0:T(8,128)(2,1)} %get-tuple-element.179.refs_3_), channel_id=1, source_target_pairs={{0,2},{2,0},{4,6},{6,4},{8,10},{10,8},{12,14},{14,12},{1,3},{3,1},... | collective-permute-start | bytes 2580488 | tf_op jit(solution)/shard_map/ppermute | solution.py:1033
  58.4 7.7 %collective-permute-start.11 = (bf16[144,768]{1,0:T(8,128)(2,1)S(1)}, bf16[144,768]{1,0:T(8,128)(2,1)S(1)}, u32[]{:S(2)}, u32[]{:S(2)}) collective-permute-start(bf16[144,768]{1,0:T(8,128)(2,1)S(1)} %get-tuple-element.191.refs_2_), channel_id=1, source_target_pairs={{0,1},{1,0},{2,3},{3,2},{4,5},{5,4},{6,7},{7,6},{8,9},{9,8},{10,11... | collective-permute-start | bytes 663560 | tf_op jit(solution)/shard_map/ppermute | solution.py:1033
  59.9 14.8 %collective-permute-start.10 = (bf16[80,768]{1,0:T(8,128)(2,1)S(1)}, bf16[80,768]{1,0:T(8,128)(2,1)S(1)}, u32[]{:S(2)}, u32[]{:S(2)}) collective-permute-start(bf16[80,768]{1,0:T(8,128)(2,1)S(1)} %get-tuple-element.189.refs_2_), channel_id=1, source_target_pairs={{0,1},{1,0},{2,3},{3,2},{4,5},{5,4},{6,7},{7,6},{8,9},{9,8},{10,11... | collective-permute-start | bytes 368648 | tf_op jit(solution)/shard_map/ppermute | solution.py:1033
  70.9 7.8 %collective-permute-start.14 = (bf16[144,768]{1,0:T(8,128)(2,1)S(1)}, bf16[144,768]{1,0:T(8,128)(2,1)S(1)}, u32[]{:S(2)}, u32[]{:S(2)}) collective-permute-start(bf16[144,768]{1,0:T(8,128)(2,1)S(1)} %get-tuple-element.201.refs_2_), channel_id=1, source_target_pairs={{0,1},{1,0},{2,3},{3,2},{4,5},{5,4},{6,7},{7,6},{8,9},{9,8},{10,11... | collective-permute-start | bytes 663560 | tf_op jit(solution)/shard_map/ppermute | solution.py:1033
  73.1 15.9 %collective-permute-start.15 = (bf16[224,768]{1,0:T(8,128)(2,1)}, bf16[224,768]{1,0:T(8,128)(2,1)S(1)}, u32[]{:S(2)}, u32[]{:S(2)}) collective-permute-start(bf16[224,768]{1,0:T(8,128)(2,1)} %get-tuple-element.204.refs_10_), channel_id=1, source_target_pairs={{0,2},{2,0},{4,6},{6,4},{8,10},{10,8},{12,14},{14,12},{1,3},{3,1},... | collective-permute-start | bytes 1032200 | tf_op jit(solution)/shard_map/ppermute | solution.py:1033
  83.5 13.1 %collective-permute-start.18 = (bf16[144,1920]{1,0:T(8,128)(2,1)}, bf16[144,1920]{1,0:T(8,128)(2,1)S(1)}, u32[]{:S(2)}, u32[]{:S(2)}) collective-permute-start(bf16[144,1920]{1,0:T(8,128)(2,1)} %get-tuple-element.213.refs_4_), channel_id=1, source_target_pairs={{0,2},{2,0},{4,6},{6,4},{8,10},{10,8},{12,14},{14,12},{1,3},{3,1},... | collective-permute-start | bytes 1658888 | tf_op jit(solution)/shard_map/ppermute | solution.py:1033
  84.1 4.9 %collective-permute-start.13 = (bf16[80,768]{1,0:T(8,128)(2,1)S(1)}, bf16[80,768]{1,0:T(8,128)(2,1)S(1)}, u32[]{:S(2)}, u32[]{:S(2)}) collective-permute-start(bf16[80,768]{1,0:T(8,128)(2,1)S(1)} %get-tuple-element.199.refs_2_), channel_id=1, source_target_pairs={{0,1},{1,0},{2,3},{3,2},{4,5},{5,4},{6,7},{7,6},{8,9},{9,8},{10,11... | collective-permute-start | bytes 368648 | tf_op jit(solution)/shard_map/ppermute | solution.py:1033
  84.8 10.8 %collective-permute-start.17 = (bf16[144,768]{1,0:T(8,128)(2,1)S(1)}, bf16[144,768]{1,0:T(8,128)(2,1)S(1)}, u32[]{:S(2)}, u32[]{:S(2)}) collective-permute-start(bf16[144,768]{1,0:T(8,128)(2,1)S(1)} %get-tuple-element.211.refs_2_), channel_id=1, source_target_pairs={{0,1},{1,0},{2,3},{3,2},{4,5},{5,4},{6,7},{7,6},{8,9},{9,8},{10,11... | collective-permute-start | bytes 663560 | tf_op jit(solution)/shard_map/ppermute | solution.py:1033
  93.4 9.9 %collective-permute-start.19 = (bf16[80,1920]{1,0:T(8,128)(2,1)}, bf16[80,1920]{1,0:T(8,128)(2,1)S(1)}, u32[]{:S(2)}, u32[]{:S(2)}) collective-permute-start(bf16[80,1920]{1,0:T(8,128)(2,1)} %get-tuple-element.218.refs_3_), channel_id=1, source_target_pairs={{0,2},{2,0},{4,6},{6,4},{8,10},{10,8},{12,14},{14,12},{1,3},{3,1},... | collective-permute-start | bytes 921608 | tf_op jit(solution)/shard_map/ppermute | solution.py:1033
  95.0 8.3 %collective-permute-start.16 = (bf16[80,768]{1,0:T(8,128)(2,1)S(1)}, bf16[80,768]{1,0:T(8,128)(2,1)S(1)}, u32[]{:S(2)}, u32[]{:S(2)}) collective-permute-start(bf16[80,768]{1,0:T(8,128)(2,1)S(1)} %get-tuple-element.208.refs_2_), channel_id=1, source_target_pairs={{0,1},{1,0},{2,3},{3,2},{4,5},{5,4},{6,7},{7,6},{8,9},{9,8},{10,11... | collective-permute-start | bytes 368648 | tf_op jit(solution)/shard_map/ppermute | solution.py:1033
  101.6 8.8 %collective-permute-start.21 = (bf16[144,768]{1,0:T(8,128)(2,1)S(1)}, bf16[144,768]{1,0:T(8,128)(2,1)S(1)}, u32[]{:S(2)}, u32[]{:S(2)}) collective-permute-start(bf16[144,768]{1,0:T(8,128)(2,1)S(1)} %get-tuple-element.226.refs_4_), channel_id=1, source_target_pairs={{0,1},{1,0},{2,3},{3,2},{4,5},{5,4},{6,7},{7,6},{8,9},{9,8},{10,11... | collective-permute-start | bytes 663560 | tf_op jit(solution)/shard_map/ppermute | solution.py:1033
  107.9 8.8 %collective-permute-start.20 = (bf16[80,768]{1,0:T(8,128)(2,1)S(1)}, bf16[80,768]{1,0:T(8,128)(2,1)S(1)}, u32[]{:S(2)}, u32[]{:S(2)}) collective-permute-start(bf16[80,768]{1,0:T(8,128)(2,1)S(1)} %get-tuple-element.220.refs_4_), channel_id=1, source_target_pairs={{0,1},{1,0},{2,3},{3,2},{4,5},{5,4},{6,7},{7,6},{8,9},{9,8},{10,11... | collective-permute-start | bytes 368648 | tf_op jit(solution)/shard_map/ppermute | solution.py:1033
  108.4 14.1 %collective-permute-start.24 = (bf16[80,1920]{1,0:T(8,128)(2,1)}, bf16[80,1920]{1,0:T(8,128)(2,1)S(1)}, u32[]{:S(2)}, u32[]{:S(2)}) collective-permute-start(bf16[80,1920]{1,0:T(8,128)(2,1)} %get-tuple-element.244.refs_8_), channel_id=1, source_target_pairs={{0,2},{2,0},{4,6},{6,4},{8,10},{10,8},{12,14},{14,12},{1,3},{3,1},... | collective-permute-start | bytes 921608 | tf_op jit(solution)/shard_map/ppermute | solution.py:1033
  110.0 13.7 %collective-permute-start.25 = (bf16[144,1920]{1,0:T(8,128)(2,1)S(1)}, bf16[144,1920]{1,0:T(8,128)(2,1)S(1)}, u32[]{:S(2)}, u32[]{:S(2)}) collective-permute-start(bf16[144,1920]{1,0:T(8,128)(2,1)S(1)} %copy-done.76), channel_id=1, source_target_pairs={{0,2},{2,0},{4,6},{6,4},{8,10},{10,8},{12,14},{14,12},{1,3},{3,1},... | collective-permute-start | bytes 1658888 | tf_op jit(solution)/shard_map/ppermute | solution.py:1033
  130.3 101.5 %reduce-scatter.6.cloned.1.call-start = ((), (), s32[]{:S(2)}) async-start(), calls=%async_computation.4 | async-start | bytes 3981312 | tf_op jit(solution)/shard_map/reduce_scatter | solution.py:1212
  131.2 10.5 %collective-permute-start.26 = (bf16[224,768]{1,0:T(8,128)(2,1)S(1)}, bf16[224,768]{1,0:T(8,128)(2,1)S(1)}, u32[]{:S(2)}, u32[]{:S(2)}) collective-permute-start(bf16[224,768]{1,0:T(8,128)(2,1)S(1)} %copy-done.46), channel_id=1, source_target_pairs={{0,2},{2,0},{4,6},{6,4},{8,10},{10,8},{12,14},{14,12},{1,3},{3,1},... | collective-permute-start | bytes 1032200 | tf_op jit(solution)/shard_map/ppermute | solution.py:1033
  132.3 9.5 %collective-permute-start.23 = (bf16[144,768]{1,0:T(8,128)(2,1)S(1)}, bf16[144,768]{1,0:T(8,128)(2,1)S(1)}, u32[]{:S(2)}, u32[]{:S(2)}) collective-permute-start(bf16[144,768]{1,0:T(8,128)(2,1)S(1)} %copy-done.80), channel_id=1, source_target_pairs={{0,1},{1,0},{2,3},{3,2},{4,5},{5,4},{6,7},{7,6},{8,9},{9,8},{10,11... | collective-permute-start | bytes 663560 | tf_op jit(solution)/shard_map/ppermute | solution.py:1033
  133.5 8.3 %collective-permute-start.22 = (bf16[80,768]{1,0:T(8,128)(2,1)S(1)}, bf16[80,768]{1,0:T(8,128)(2,1)S(1)}, u32[]{:S(2)}, u32[]{:S(2)}) collective-permute-start(bf16[80,768]{1,0:T(8,128)(2,1)S(1)} %copy-done.81), channel_id=1, source_target_pairs={{0,1},{1,0},{2,3},{3,2},{4,5},{5,4},{6,7},{7,6},{8,9},{9,8},{10,11... | collective-permute-start | bytes 368648 | tf_op jit(solution)/shard_map/ppermute | solution.py:1033
  134.3 24.2 %collective-permute-start.28 = (bf16[224,1536]{1,0:T(8,128)(2,1)S(1)}, bf16[224,1536]{1,0:T(8,128)(2,1)S(1)}, u32[]{:S(2)}, u32[]{:S(2)}) collective-permute-start(bf16[224,1536]{1,0:T(8,128)(2,1)S(1)} %copy-done.44), channel_id=1, source_target_pairs={{0,2},{2,0},{4,6},{6,4},{8,10},{10,8},{12,14},{14,12},{1,3},{3,1},... | collective-permute-start | bytes 2064392 | tf_op jit(solution)/shard_map/ppermute | solution.py:1033
  151.2 7.3 %collective-permute-start.27 = (bf16[224,768]{1,0:T(8,128)(2,1)S(1)}, bf16[224,768]{1,0:T(8,128)(2,1)S(1)}, u32[]{:S(2)}, u32[]{:S(2)}) collective-permute-start(bf16[224,768]{1,0:T(8,128)(2,1)S(1)} %get-tuple-element.249.refs_6_), channel_id=1, source_target_pairs={{0,1},{1,0},{2,3},{3,2},{4,5},{5,4},{6,7},{7,6},{8,9},{9,8},{10,11... | collective-permute-start | bytes 1032200 | tf_op jit(solution)/shard_map/ppermute | solution.py:1033
  151.3 15.7 %collective-permute-start.31 = (bf16[224,1536]{1,0:T(8,128)(2,1)}, bf16[224,1536]{1,0:T(8,128)(2,1)S(1)}, u32[]{:S(2)}, u32[]{:S(2)}) collective-permute-start(bf16[224,1536]{1,0:T(8,128)(2,1)} %get-tuple-element.273.refs_13_), channel_id=1, source_target_pairs={{0,2},{2,0},{4,6},{6,4},{8,10},{10,8},{12,14},{14,12},{1,3},{3,1},... | collective-permute-start | bytes 2064392 | tf_op jit(solution)/shard_map/ppermute | solution.py:1033
  173.8 130.8 %reduce-scatter.8.cloned.1.call-start = ((), (), s32[]{:S(2)}) async-start(), calls=%async_computation.5 | async-start | bytes 4423680 | tf_op jit(solution)/shard_map/reduce_scatter | solution.py:1361
  174.7 7.2 %collective-permute-start.30 = (bf16[224,768]{1,0:T(8,128)(2,1)S(1)}, bf16[224,768]{1,0:T(8,128)(2,1)S(1)}, u32[]{:S(2)}, u32[]{:S(2)}) collective-permute-start(bf16[224,768]{1,0:T(8,128)(2,1)S(1)} %copy-done.78), channel_id=1, source_target_pairs={{0,1},{1,0},{2,3},{3,2},{4,5},{5,4},{6,7},{7,6},{8,9},{9,8},{10,11... | collective-permute-start | bytes 1032200 | tf_op jit(solution)/shard_map/ppermute | solution.py:1033
  175.0 20.0 %collective-permute-start.29 = (bf16[224,1920]{1,0:T(8,128)(2,1)S(1)}, bf16[224,1920]{1,0:T(8,128)(2,1)S(1)}, u32[]{:S(2)}, u32[]{:S(2)}) collective-permute-start(bf16[224,1920]{1,0:T(8,128)(2,1)S(1)} %copy-done.72), channel_id=1, source_target_pairs={{0,2},{2,0},{4,6},{6,4},{8,10},{10,8},{12,14},{14,12},{1,3},{3,1},... | collective-permute-start | bytes 2580488 | tf_op jit(solution)/shard_map/ppermute | solution.py:1033
  194.6 11.2 %collective-permute-start.32 = (bf16[224,1536]{1,0:T(8,128)(2,1)}, bf16[224,1536]{1,0:T(8,128)(2,1)S(1)}, u32[]{:S(2)}, u32[]{:S(2)}) collective-permute-start(bf16[224,1536]{1,0:T(8,128)(2,1)} %get-tuple-element.276.refs_13_), channel_id=1, source_target_pairs={{0,2},{2,0},{4,6},{6,4},{8,10},{10,8},{12,14},{14,12},{1,3},{3,1},... | collective-permute-start | bytes 2064392 | tf_op jit(solution)/shard_map/ppermute | solution.py:1033
  213.9 6.5 %collective-permute-start.33 = (bf16[384,4608]{1,0:T(8,128)(2,1)}, bf16[384,4608]{1,0:T(8,128)(2,1)S(1)}, u32[]{:S(2)}, u32[]{:S(2)}) collective-permute-start(bf16[384,4608]{1,0:T(8,128)(2,1)} %get-tuple-element.279), channel_id=1, source_target_pairs={{0,16},{16,0},{1,17},{17,1},{2,18},{18,2},{3,19},{19,3},{4,20},{20... | collective-permute-start | bytes 10616840 | tf_op jit(solution)/shard_map/ppermute | solution.py:1033
  235.5 1.4 collective-permute-start.37
  236.9 4.9 %collective-permute-start.38 = (f32[25,768]{1,0:T(8,128)S(1)}, f32[25,768]{1,0:T(8,128)S(1)}, u32[]{:S(2)}, u32[]{:S(2)}) collective-permute-start(f32[25,768]{1,0:T(8,128)S(1)} %fusion.2), channel_id=1, source_target_pairs={{0,2},{2,0},{4,6},{6,4},{8,10},{10,8},{12,14},{14,12},{1,3},{3,1},... | collective-permute-start | bytes 230408 | tf_op jit(solution)/shard_map/ppermute | solution.py:1033
  241.8 9.0 %collective-permute-start.39 = (f32[25,768]{1,0:T(8,128)S(1)}, f32[25,768]{1,0:T(8,128)S(1)}, u32[]{:S(2)}, u32[]{:S(2)}) collective-permute-start(f32[25,768]{1,0:T(8,128)S(1)} %add.164), channel_id=1, source_target_pairs={{0,4},{2,6},{4,0},{6,2},{8,12},{10,14},{12,8},{14,10},{1,5},{3,7},... | collective-permute-start | bytes 230408 | tf_op jit(solution)/shard_map/ppermute | solution.py:1033
  250.9 14.2 %collective-permute-start.40 = (f32[25,768]{1,0:T(8,128)S(1)}, f32[25,768]{1,0:T(8,128)S(1)}, u32[]{:S(2)}, u32[]{:S(2)}) collective-permute-start(f32[25,768]{1,0:T(8,128)S(1)} %add.165), channel_id=1, source_target_pairs={{0,8},{2,10},{4,12},{6,14},{8,0},{10,2},{12,4},{14,6},{1,9},{3,11}... | collective-permute-start | bytes 230408 | tf_op jit(solution)/shard_map/ppermute | solution.py:1033
  252.7 19.0 %collective-permute-start.36 = (bf16[224,768]{1,0:T(8,128)(2,1)S(1)}, bf16[224,768]{1,0:T(8,128)(2,1)S(1)}, u32[]{:S(2)}, u32[]{:S(2)}) collective-permute-start(bf16[224,768]{1,0:T(8,128)(2,1)S(1)} %copy-done.47), channel_id=1, source_target_pairs={{0,1},{1,0},{2,3},{3,2},{4,5},{5,4},{6,7},{7,6},{8,9},{9,8},{10,11... | collective-permute-start | bytes 1032200 | tf_op jit(solution)/shard_map/ppermute | solution.py:1033
  265.4 9.0 %collective-permute-start.34 = (bf16[96,3072]{1,0:T(8,128)(2,1)S(1)}, bf16[96,3072]{1,0:T(8,128)(2,1)S(1)}, u32[]{:S(2)}, u32[]{:S(2)}) collective-permute-start(bf16[96,3072]{1,0:T(8,128)(2,1)S(1)} %copy-done.31), channel_id=1, source_target_pairs={{0,16},{1,17},{2,18},{3,19},{4,20},{5,21},{6,22},{7,23},{8,24},{9,... | collective-permute-start | bytes 1769480 | tf_op jit(solution)/shard_map/ppermute | solution.py:1442
  267.9 6.5 %collective-permute-start.35 = (bf16[96,1536]{1,0:T(8,128)(2,1)}, bf16[96,1536]{1,0:T(8,128)(2,1)S(1)}, u32[]{:S(2)}, u32[]{:S(2)}) collective-permute-start(bf16[96,1536]{1,0:T(8,128)(2,1)} %slice.94), channel_id=1, source_target_pairs={{0,16},{1,17},{2,18},{3,19},{4,20},{5,21},{6,22},{7,23},{8,24},{9,... | collective-permute-start | bytes 884744 | tf_op jit(solution)/shard_map/ppermute | solution.py:1442
  304.6 4.5 %collective-permute-start.41 = (bf16[96,4608]{1,0:T(8,128)(2,1)}, bf16[96,4608]{1,0:T(8,128)(2,1)S(1)}, u32[]{:S(2)}, u32[]{:S(2)}) collective-permute-start(bf16[96,4608]{1,0:T(8,128)(2,1)} %reduce-scatter.8.cloned.1.call-done.refs_5_), channel_id=1, source_target_pairs={{16,0},{17,1},{18,2},{19,3},{20,4},{21,5},{22,6},{23,7},{24,8},{25... | collective-permute-start | bytes 2654216 | tf_op jit(solution)/shard_map/ppermute | solution.py:1458
  (83 other events, 747.6 us)
Sparse Core Ops, SparseCore 0:
  130.4 55.6 reduce-scatter.3
  188.5 43.2 reduce-scatter.5
  234.2 70.3 reduce-scatter.7

commit v2 on v1

--- a/solution.py
+++ b/solution.py
@@ -16,6 +16,7 @@
 EPS = 1e-06
 SCALE = HEAD_DIM**-0.5
 COST_SCALE = 0.5
+ORDER = (1, 0)
 bf16 = jnp.bfloat16
 f32 = jnp.float32
 
@@ -123,6 +124,10 @@
             grads[2].append(mm_tn(probs, grad_context[:, lanes]))
         for kind in range(3):
             emit(kind, lanes, jnp.where(first, grads[kind][0], grads[kind][1]).astype(bf16))
+
+
+def small_of(meta, layer, side, own, other):
+    return jnp.where(meta[0] == layer, own[side], other[side])
 
 
 class Fetched:
@@ -166,6 +171,39 @@
         for copy in copies if piece is None else (copies[piece],):
             copy.wait()
         return copies[0].buffer
+
+
+class Held:
+    def __init__(self, *refs):
+        self.refs = refs
+
+    def get(self, slot, piece=None):
+        return self.refs[slot]
+
+
+def weight_inputs(entry, leave, kinds="wwww"):
+    if len(entry) == 1:
+        return [(entry[0], "v"), (leave[0], "v")]
+    return list(zip(entry + leave, kinds))
+
+
+def pass_on(meta, layer, offered, taken, sems):
+    copies = []
+    for i, target in enumerate(taken):
+        own = pltpu.make_async_copy(offered[2 * i].at[0], target, sems.at[i])
+        other = pltpu.make_async_copy(offered[2 * i + 1].at[0], target, sems.at[i])
+        pl.when(meta[0] == layer)(own.start)
+        pl.when(meta[0] != layer)(other.start)
+        copies.append(own)
+    return copies
+
+
+def items_of(meta, source, raw, rows_ref, sem, batch):
+    copy = pltpu.make_async_copy(source.at[meta[0]], raw, sem)
+    copy.start()
+    copy.wait()
+    for slot in range(raw.shape[0]):
+        rows_ref[slot * batch : (slot + 1) * batch] = raw[slot].astype(f32)
 
 
 def maps(own, other, side, pieces=((),)):
@@ -280,35 +318,49 @@
 
 
 def self_forward(
-    side, layer, batch, meta, state, prior, small, chooser, att_in, att_out, place, ties=()
+    side, layer, batch, meta, state, prior, small, chooser, att_in, att_out, place, ties=(), later=()
 ):
-    rows = state.shape[0]
+    rows = state.shape[1] * batch if prior is None else state.shape[0]
     width = att_in[0].shape[-1]
     first = prior is None
+    held, n_maps = len(att_in) == 1, len(att_in + att_out)
 
     def body(flush, meta, state, *refs):
         refs = list(refs)
         if not first:
             own, other, post = refs[:3]
             refs = refs[3:]
-        small, chooser, in_own, in_other, out_own, out_other = refs[:6]
-        qkv, probs, selected, pack, part, squares = refs[6:12]
-        refs = refs[12:]
+        small = small_of(meta, layer, side, refs[0], refs[1])
+        chooser, refs = refs[2], refs[3:]
+        given, refs = refs[:n_maps], refs[n_maps:]
+        offered, refs = refs[: 2 * len(later)], refs[2 * len(later) :]
+        qkv, probs, selected, pack, part, squares = refs[:6]
+        refs = refs[6:]
         if not first:
             mixed_ref, unit_ref, rstd_ref = refs[:3]
-            refs = refs[3:]
-        in_buffer, out_buffer, sems = refs
-        weights = Weights(
-            meta,
-            layer,
-            (maps(in_own, in_other, side, ENTRY), maps(out_own, out_other, side)),
-            (in_buffer, out_buffer),
-            sems,
-        )
+            taken, refs = refs[3 : 3 + len(later)], refs[3 + len(later) :]
+            passing = pass_on(meta, layer, offered, taken, refs[-1]) if later else []
+        else:
+            low_ref, refs = refs[0], refs[1:]
+            raw, rows_ref, raw_sem = refs[-3:]
+            refs = refs[:-3]
+        if held:
+            weights = Held(given[0].at[side], given[1].at[side])
+        else:
+            in_buffer, out_buffer, sems = refs
+            weights = Weights(
+                meta,
+                layer,
+                (maps(*given[:2], side, ENTRY), maps(*given[2:], side)),
+                (in_buffer, out_buffer),
+                sems,
+            )
         valid = row_valid(meta, side, batch, rows)
         if first:
-            low = state[...]
-            squares[...] = square_sum(low.astype(f32), valid)
+            items_of(meta, state, raw, rows_ref, raw_sem, batch)
+            squares[...] = square_sum(rows_ref[...], valid)
+            low = rows_ref[...].astype(bf16)
+            low_ref[...] = low
         else:
             branch = summed(own, other) + post[0:1]
             squares[...] = square_sum(branch, valid)
@@ -327,12 +379,16 @@
         )
         flush(qkv, probs, pack)
         part[...] = mm(context[...], weights.get(1)[...]).astype(bf16)
-
-    ins = [(meta, "s"), (state, "v")]
+        if not first:
+            for copy in passing:
+                copy.wait()
+
+    ins = [(meta, "s"), (state, "w" if first else "v")]
     if not first:
         ins += list(zip(prior, "vvv"))
-    ins += [(small, "v"), (chooser, "v")]
-    ins += list(zip(att_in + att_out, "wawa" if layer == 0 else "wwww"))
+    ins += [(item, "v") for item in (*small, chooser)]
+    ins += weight_inputs(att_in, att_out, "wawa")
+    ins += [(item, "w") for pair in later for item in pair]
     outs = [
         ((3, rows, width), bf16, "h"),
         ((width // HEAD_DIM, rows, rows), bf16, "h"),
@@ -343,12 +399,58 @@
     ]
     if not first:
         outs += [((rows, D), f32, "v"), ((rows, D), f32, "h"), ((rows, 1), f32, "h")]
+        outs += [(pair[0].shape[1:], bf16, "v") for pair in later]
+    else:
+        outs.append(((rows, D), bf16, "v"))
     scratch = [
         pltpu.VMEM((3, D, width), bf16),
         pltpu.VMEM((width, D), bf16),
         pltpu.SemaphoreType.DMA((6,)),
     ]
-    return call(body, ins, outs, scratch, 4.0, f"self_forward_{layer}_{side}", ties)
+    scratch = [] if held else scratch
+    if first:
+        scratch += [
+            pltpu.VMEM(state.shape[1:], bf16),
+            pltpu.VMEM((rows, D), f32),
+            pltpu.SemaphoreType.DMA,
+        ]
+    if later:
+        scratch.append(pltpu.SemaphoreType.DMA((len(later),)))
+    return call(body, ins, outs, scratch, 4.0, f"self_forward_{layer}_{side}", ties, 12)
+
+
+def hand_over(low_ref, kept, sent, sems):
+    copies = []
+    for slot, target in enumerate((kept, sent)):
+        copies.append(
+            pltpu.make_async_copy(low_ref, target.at[:, pl.ds(0, D)], sems.at[slot])
+        )
+        copies[-1].start()
+    return copies
+
+
+def hand_halves(meta, batch, wide_ref, kept, sent, sems):
+    count = wide_ref.shape[1] // 2
+    copies = []
+    for half in (0, 1):
+        source = wide_ref.at[:, pl.ds(half * count, count)]
+        to_kept, to_sent = (
+            pltpu.make_async_copy(source, target.at[:, pl.ds(D, count)], sems.at[2 + half])
+            for target in (kept, sent)
+        )
+        mine = meta[1 + 2 * batch] == half
+        pl.when(mine)(to_kept.start)
+        pl.when(jnp.logical_not(mine))(to_sent.start)
+        copies.append(to_kept)
+    return copies
+
+
+def hand_scratch(rows, units):
+    return [
+        pltpu.VMEM((rows, D), bf16),
+        pltpu.VMEM((rows, units), bf16),
+        pltpu.SemaphoreType.DMA((4,)),
+    ]
 
 
 def feed_forward(
@@ -358,21 +460,29 @@
     units = feed_in[0].shape[-1]
     step = units // 4
 
-    def body(
-        flush, meta, residual, own, other, small, chooser, in_own, in_other, out_own, out_other,
-        settled_ref, unit_ref, rstd_ref, selected, pack, slope, part, squares,
-        in_buffer, out_buffer, sems,
-    ):
-        weights = Weights(
-            meta,
-            layer,
-            (
-                maps(in_own, in_other, side, column_pieces(units, 4)),
-                maps(out_own, out_other, side, row_pieces(units, 2)),
-            ),
-            (in_buffer, out_buffer),
-            sems,
-        )
+    held, n_maps = len(feed_in) == 1, len(feed_in + feed_out)
+
+    def body(flush, meta, residual, own, other, small_own, small_other, *refs):
+        small = small_of(meta, layer, side, small_own, small_other)
+        if not held:
+            chooser, refs = refs[0], refs[1:]
+        given, refs = refs[:n_maps], refs[n_maps:]
+        settled_ref, unit_ref, rstd_ref, selected, pack, slope, part, squares = refs[:8]
+        if held:
+            weights = Held(given[0].at[side], given[1].at[side])
+            low_ref, active_ref, sems = refs[8:]
+        else:
+            in_buffer, out_buffer, sems = refs[8:]
+            weights = Weights(
+                meta,
+                layer,
+                (
+                    maps(*given[:2], side, column_pieces(units, 4)),
+                    maps(*given[2:], side, row_pieces(units, 2)),
+                ),
+                (in_buffer, out_buffer),
+                sems,
+            )
         post = small[ROW_ATT_POST : ROW_ATT_POST + 3]
         branch = summed(own, other) + post[0:1]
         squares[...] = square_sum(branch, row_valid(meta, side, batch, rows))
@@ -381,8 +491,14 @@
         rstd_ref[...] = rstd
         settled_ref[...] = settled
         low = settled.astype(bf16)
-        select_rows(low, chooser, selected, pack)
-        flush(unit_ref, rstd_ref, selected)
+        if held:
+            low_ref[...] = low
+            copies = hand_over(low_ref, selected, pack, sems)
+            flush(unit_ref, rstd_ref)
+        else:
+            select_rows(low, chooser, selected, pack)
+            active_ref = pack.at[:, HALF:]
+            flush(unit_ref, rstd_ref, selected)
         for i in range(units // step):
             first = weights.get(0, i)
             columns = slice(i * step, (i + 1) * step)
@@ -391,20 +507,28 @@
             hidden = mm(low, first[:, columns]) + small[row : row + 1, place : place + step]
             below = 0.5 + 0.5 * lax.erf(hidden * (0.5**0.5))
             density = jnp.exp(hidden * hidden * -0.5) * 0.3989422804014327
-            pack[:, HALF + i * step : HALF + (i + 1) * step] = (hidden * below).astype(bf16)
+            active_ref[:, columns] = (hidden * below).astype(bf16)
             slope[:, columns] = (below + hidden * density).astype(bf16)
         flush(pack, slope)
-        part[...] = mm(pack[:, HALF:], weights.get(1)[...]).astype(bf16)
+        if held:
+            copies += hand_halves(meta, batch, active_ref, selected, pack, sems)
+        part[...] = mm(active_ref[...], weights.get(1)[...]).astype(bf16)
+        if held:
+            for copy in copies:
+                copy.wait()
 
     ins = [(meta, "s"), (residual, "v"), (own, "v"), (other, "v")]
-    ins += [(small, "v"), (chooser, "v")]
-    ins += list(zip(feed_in + feed_out, "wawa" if layer == 0 else "wwww"))
+    ins += [(item, "v") for item in ((*small,) if held else (*small, chooser))]
+    ins += weight_inputs(feed_in, feed_out, "wawa")
     outs = [
         ((rows, D), f32, "v"),
         ((rows, D), f32, "h"),
         ((rows, 1), f32, "h"),
-        ((rows, HALF), bf16, "h"),
-        ((rows, HALF + units), bf16, "h", *place),
+        *(
+            [((rows, D + units // 2), bf16, "w")] * 2
+            if held
+            else [((rows, HALF), bf16, "h"), ((rows, HALF + units), bf16, "h", *place)]
+        ),
         ((rows, units), bf16, "h"),
         ((rows, D), bf16, "v"),
         ((1, 128), f32, "h"),
@@ -414,11 +538,13 @@
         pltpu.VMEM((units, D), bf16),
         pltpu.SemaphoreType.DMA((6,)),
     ]
-    return call(body, ins, outs, scratch, 4.3, f"feed_forward_{layer}_{side}", ties)
+    if held:
+        scratch = hand_scratch(rows, units)
+    return call(body, ins, outs, scratch, 4.3, f"feed_forward_{layer}_{side}", ties, 12 if held else 14)
 
 
 def cross_forward(
-    batch, meta, streams, smalls, chooser, cross_in, cross_bias, cross_out, ties=()
+    batch, meta, streams, smalls, chooser, cross_in, cross_bias, cross_out, later, ties=()
 ):
     rows = [stream[0].shape[0] for stream in streams]
     spans = spans_of(rows)
@@ -427,12 +553,15 @@
 
     def body(flush, meta, *refs):
         given = (refs[0:3], refs[3:6])
-        small, chooser, in_ref, bias, out_ref = (refs[6:8], *refs[8:12])
+        small = [small_of(meta, 0, side, refs[6], refs[7]) for side in (0, 1)]
+        chooser, in_ref, bias, out_ref = refs[8:12]
+        offered, refs = refs[12 : 12 + 2 * len(later)], refs[:12] + refs[12 + 2 * len(later) :]
+        taken, refs = refs[29 : 29 + len(later)], refs[:29] + refs[29 + len(later) :]
         all_pack = refs[28]
         outs = [refs[12:20], refs[20:28]]
         for side in (0, 1):
             outs[side] = outs[side][:5] + (all_pack.at[spans[side]],) + outs[side][5:]
-        in_buffer, out_buffer, sems = refs[29:]
+        in_buffer, out_buffer, sems, later_sems = refs[29:]
         weights = Weights(
             meta,
             0,
@@ -440,6 +569,7 @@
             (in_buffer, out_buffer),
             sems,
         )
+        passing = pass_on(meta, 1, offered, taken, later_sems)
         lows = []
         for side in (0, 1):
             settled, own, other = given[side]
@@ -468,10 +598,13 @@
             attend(qkv[0], there[1], there[2], valid, probs, context)
             flush(qkv, probs)
             part[...] = mm(context[...], leave[...]).astype(bf16)
+        for copy in passing:
+            copy.wait()
 
     ins = [(meta, "s")] + [pair for stream in streams for pair in zip(stream, "vvv")]
     ins += [(item, "v") for item in smalls]
     ins += [(chooser, "v"), (cross_in, "w"), (cross_bias, "v"), (cross_out, "w")]
+    ins += [(item, "w") for pair in later for item in pair]
     outs = []
     for side in (0, 1):
         here, there = rows[side], rows[1 - side]
@@ -486,13 +619,15 @@
             ((here, D), bf16, "v"),
         ]
     outs.append(((sum(rows), HALF + width), bf16, "h"))
+    outs += [(pair[0].shape[1:], bf16, "v") for pair in later]
     scratch = [
         pltpu.VMEM((3, D, width), bf16),
         pltpu.VMEM((width, D), bf16),
         pltpu.SemaphoreType.DMA((6,)),
+        pltpu.SemaphoreType.DMA((len(later),)),
     ]
     result = call(body, ins, outs, scratch, 6.8, "cross_forward", ties)
-    return result[:8], result[8:16], result[16]
+    return result[:8], result[8:16], result[16], result[17:]
 
 
 class Layout:
@@ -532,6 +667,7 @@
     step = units // 4
     n_top = len(tops[0])
     n = len(sides)
+    held, n_maps = len(feed_in) == 1, len(feed_in + feed_out)
 
     def body(flush, meta, *refs):
         tops = {}
@@ -539,21 +675,28 @@
             tops[side], refs = refs[:n_top], refs[n_top:]
         if not last:
             joint, refs = refs[:3], refs[3:]
-        small, refs = dict(zip(sides, refs[:n])), refs[n:]
-        chooser, slopes, refs = refs[0], dict(zip(sides, refs[1 : 1 + n])), refs[1 + n :]
-        in_own, in_other, out_own, out_other = refs[:4]
-        grad_all, selected_all, pack_all, part_all, post_all, bias_all = refs[4:10]
+        small = {side: small_of(meta, layer, side, refs[0], refs[1]) for side in sides}
+        refs = refs[2:]
+        if not held:
+            chooser, refs = refs[0], refs[1:]
+        slopes, refs = dict(zip(sides, refs[:n])), refs[n:]
+        given, refs = refs[:n_maps], refs[n_maps:]
+        grad_all, selected_all, pack_all, part_all, post_all, bias_all = refs[:6]
         if last:
-            squares_all, results = refs[10], dict(zip(sides, refs[11 : 11 + n]))
-        in_buffer, out_buffer, sems = refs[-3:]
+            squares_all, results = refs[6], dict(zip(sides, refs[7 : 7 + n]))
+            low_ref, hidden_ref, hand_sems, raw, rows_ref, raw_sem = refs[-6:]
         weights = {}
         for i, side in enumerate(sides):
+            if held:
+                weights[side] = Held(given[1].at[side], given[0].at[side])
+                continue
+            in_buffer, out_buffer, sems = refs[-3:]
             weights[side] = Weights(
                 meta,
                 layer,
                 (
-                    maps(out_own, out_other, side, row_pieces(units, 4)),
-                    maps(in_own, in_other, side, column_pieces(units, 2)),
+                    maps(*given[2:], side, row_pieces(units, 4)),
+                    maps(*given[:2], side, column_pieces(units, 2)),
                 ),
                 (out_buffer.at[i], in_buffer.at[i]),
                 sems.at[i],
@@ -571,7 +714,8 @@
                 valid = row_valid(meta, side, batch, rows[side])
                 squares_all[at, 0:1] = square_sum(branch, valid)
                 squares_all[at, 1:2] = square_sum(low.astype(f32), valid)
-                incoming = cotangent[...].astype(f32) * valid
+                items_of(meta, cotangent, raw, rows_ref, raw_sem, batch)
+                incoming = rows_ref[...] * valid
             else:
                 unit_ref, rstd_ref = tops[side]
                 unit, rstd = unit_ref[...], rstd_ref[...]
@@ -585,30 +729,44 @@
             post_all[at, 2:3] = column_sum(incoming)
             lows[side] = low
         flush(grad_all, post_all)
+        if held:
+            low_ref[...] = lows[sides[0]]
+            copies = hand_over(low_ref, selected_all, pack_all, hand_sems)
+        else:
+            hidden_ref = pack_all.at[:, HALF:]
         for side in sides:
             here, at = layout.here(side), layout.index(side)
             for i in range(units // step):
                 columns = slice(i * step, (i + 1) * step)
                 active = mm_nt(lows[side], weights[side].get(0, i)[columns, :])
                 hidden = (active * slopes[side][:, columns].astype(f32)).astype(bf16)
-                pack_all[here, HALF + i * step : HALF + (i + 1) * step] = hidden
+                hidden_ref[here, columns] = hidden
                 bias_all[at, :, columns] = column_sum(hidden.astype(f32))
-            select_rows(lows[side], chooser, selected_all.at[here], pack_all.at[here])
+            if not held:
+                select_rows(lows[side], chooser, selected_all.at[here], pack_all.at[here])
         flush(pack_all, selected_all)
+        if held:
+            copies += hand_halves(meta, batch, hidden_ref, selected_all, pack_all, hand_sems)
         for side in sides:
             here = layout.here(side)
-            part_all[here] = mm_nt(pack_all[here, HALF:], weights[side].get(1)[...]).astype(bf16)
-
-    ins = [(meta, "s")] + [pair for top in tops for pair in zip(top, "vvvv" if last else "vv")]
+            part_all[here] = mm_nt(hidden_ref[here], weights[side].get(1)[...]).astype(bf16)
+        if held:
+            for copy in copies:
+                copy.wait()
+
+    ins = [(meta, "s")] + [pair for top in tops for pair in zip(top, "vvvw" if last else "vv")]
     if not last:
         ins += [(item, "v") for item in joint]
-    ins += [(item, "v") for item in (*small, chooser, *slopes)]
-    ins += list(zip(feed_in + feed_out, "wwww"))
+    ins += [(item, "v") for item in ((*small, *slopes) if held else (*small, chooser, *slopes))]
+    ins += weight_inputs(feed_in, feed_out)
     count = layout.count
     outs = [
         ((count, D), f32, "v" if last else "h"),
-        layout.rows(HALF, bf16, 1),
-        ((count, HALF + units), bf16, "h"),
+        *(
+            [((count, D + units // 2), bf16, "w")] * 2
+            if held
+            else [layout.rows(HALF, bf16, 1), ((count, HALF + units), bf16, "h")]
+        ),
         ((count, D), bf16, "v" if last else "h"),
         layout.each((3, D), 4),
         layout.each((1, units), 5),
@@ -620,8 +778,15 @@
         pltpu.VMEM((n, units, D), bf16),
         pltpu.SemaphoreType.DMA((n, 6)),
     ]
+    if last:
+        side = sides[0]
+        scratch = hand_scratch(rows[side], units) + [
+            pltpu.VMEM(tops[0][3].shape[1:], bf16),
+            pltpu.VMEM((rows[side], D), f32),
+            pltpu.SemaphoreType.DMA,
+        ]
     name = f"feed_backward_{layer}_" + "".join(map(str, sides))
-    return call(body, ins, outs, scratch, 11.0 * count / layout.total, name, ties, 24)
+    return call(body, ins, outs, scratch, 11.0 * count / layout.total, name, ties, 12 if held else 24)
 
 
 def summed_rows(own, other, here):
@@ -664,21 +829,26 @@
     layout = Layout(sides, rows, given)
     width = qkvs[0].shape[2]
     n = len(sides)
+    held, n_maps = len(att_in) == 1, len(att_in + att_out)
 
     def body(flush, meta, *refs):
         tops = {side: refs[2 * i : 2 * i + 2] for i, side in enumerate(sides)}
         joint, refs = refs[2 * n : 2 * n + 3], refs[2 * n + 3 :]
-        small, chooser, refs = dict(zip(sides, refs[:n])), refs[n], refs[n + 1 :]
+        small = {side: small_of(meta, layer, side, refs[0], refs[1]) for side in sides}
+        chooser, refs = refs[2], refs[3:]
         qkvs, probs, refs = dict(zip(sides, refs[:n])), dict(zip(sides, refs[n : 2 * n])), refs[2 * n :]
-        in_own, in_other, out_own, out_other = refs[:4]
-        grad_all, selected_all, pack_all, part_all, post_all, bias_all = refs[4:10]
-        in_buffer, out_buffer, sems = refs[10:]
+        given, refs = refs[:n_maps], refs[n_maps:]
+        grad_all, selected_all, pack_all, part_all, post_all, bias_all = refs[:6]
         weights = {}
         for i, side in enumerate(sides):
+            if held:
+                weights[side] = Held(given[1].at[side], given[0].at[side])
+                continue
+            in_buffer, out_buffer, sems = refs[6:]
             weights[side] = Weights(
                 meta,
                 layer,
-                (maps(out_own, out_other, side), maps(in_own, in_other, side, ENTRY)),
+                (maps(*given[2:], side), maps(*given[:2], side, ENTRY)),
                 (out_buffer.at[i], in_buffer.at[i]),
                 sems.at[i],
             )
@@ -709,7 +879,7 @@
     ins = [(meta, "s")] + [(item, near) for top in tops for item in top]
     ins += [*zip(joint, "vvv" if layer == 1 else "hhf")] + [(item, near) for item in small]
     ins += [(item, near) for item in (chooser, *qkvs, *probs)]
-    ins += list(zip(att_in + att_out, "wwww"))
+    ins += weight_inputs(att_in, att_out)
     outs = [
         ((layout.count, D), f32, "h"),
         layout.rows(HALF, bf16, 1),
@@ -723,8 +893,9 @@
         pltpu.VMEM((n, width, D), bf16),
         pltpu.SemaphoreType.DMA((n, 6)),
     ]
+    scratch = [] if held else scratch
     name = f"self_backward_{layer}_" + "".join(map(str, sides))
-    return call(body, ins, outs, scratch, 12.0 * layout.count / layout.total, name, ties, 18)
+    return call(body, ins, outs, scratch, 12.0 * layout.count / layout.total, name, ties, 12 if held else 18)
 
 
 def cross_backward(meta, tops, grads, owns, others, post, chooser, qkvs, probs, cross_in, cross_out, ties=()):
@@ -802,6 +973,7 @@
     def __init__(self, in_selected, in_packs, in_gots, out_selected, out_packs, out_gots):
         self.parts = [*in_selected, *in_packs, *in_gots, out_selected, *out_packs, *out_gots]
         self.counts = (len(in_packs), len(out_packs))
+        self.lead = HALF
         self.kinds = "w" * len(self.parts)
         self.sizes = (out_packs[0].shape[1] - HALF, in_packs[0].shape[1] - HALF)
         self.rows = [array.shape[0] for array in in_selected]
@@ -855,12 +1027,47 @@
         return result, at
 
 
+class Halves:
+    def __init__(self, in_kept, in_gots, out_kept, out_gots):
+        self.parts = [*in_kept, *in_gots, *out_kept, *out_gots]
+        self.kinds = "w" * len(self.parts)
+        self.lead = D
+        self.sizes = (out_kept[0].shape[1] - D, in_kept[0].shape[1] - D)
+        self.rows = [array.shape[0] for array in in_kept]
+
+    def buffers(self):
+        return [
+            pltpu.VMEM((2 * rows, D + size), bf16)
+            for rows in self.rows
+            for size in (self.sizes[1], self.sizes[0])
+        ]
+
+    def fetch(self, refs, buffers, sems, at):
+        result = []
+        for side in (0, 1):
+            count = self.rows[side]
+            per_side = []
+            for kind in (0, 1):
+                buffer = buffers[2 * side + kind]
+                copies = []
+                for part in (0, 1):
+                    target = buffer.at[slice(part * count, (part + 1) * count)]
+                    source = refs[4 * kind + 2 * part + side]
+                    copies.append(pltpu.make_async_copy(source, target, sems.at[at]))
+                    copies[-1].start()
+                    at += 1
+                per_side.append((buffer, copies))
+            result.append(per_side)
+        return result, at
+
+
 def chunk_order(groups):
     return [(s, z) for z in range(groups) for s in ((0, 1) if z % 2 == 0 else (1, 0))]
 
 
 def gradients(meta, blocks, cross, groups, name, ties=(), split=False):
-    chunk = HALF // groups
+    lead = blocks[0].lead
+    chunk = lead // groups
     half = chunk // 2
     size = chunk + half if cross else chunk
     order = chunk_order(groups)
@@ -928,10 +1135,10 @@
                 start = base
                 for left, right in ((0, 1), (1, 0)):
                     left, right = ready(copies[side][left]), ready(copies[side][right])
-                    turned = left[:, :HALF].T
-                    span = right.shape[1] - HALF
+                    turned = left[:, :lead].T
+                    span = right.shape[1] - lead
                     for step in range(0, span, HALF):
-                        value = mm(turned, right[:, HALF + step : HALF + step + HALF])
+                        value = mm(turned, right[:, lead + step : lead + step + HALF])
                         stage[side, :, start + step : start + step + HALF] = value.astype(bf16)
                     columns = pl.ds(start, span)
                     leave(stage.at[side, :, columns], side, columns, at)
@@ -960,16 +1167,16 @@
     if aligned and not split:
         outs = [((2 * groups * size, width), bf16, "w")]
     else:
-        outs = [((HALF, width), bf16, "w")] * n_out
+        outs = [((lead, width), bf16, "w")] * n_out
     scratch = [buffer for block in every for buffer in block.buffers()]
     if cross:
         scratch += [
             pltpu.SemaphoreType.DMA((n_sems,)),
-            pltpu.VMEM((2, HALF, width), bf16),
+            pltpu.VMEM((2, lead, width), bf16),
             pltpu.VMEM((HALF, sum(cross.sizes)), bf16),
         ]
     else:
-        scratch += [pltpu.SemaphoreType.DMA((n_sems,)), pltpu.VMEM((2, HALF, width), bf16)]
+        scratch += [pltpu.SemaphoreType.DMA((n_sems,)), pltpu.VMEM((2, lead, width), bf16)]
     result = call(body, ins, outs, scratch, 6.0, name, ties, 20)
     if split:
         return result
@@ -1015,7 +1222,7 @@
         cross_out[...] = late1[chunk:, 3 * width :].astype(f32)
 
     ins = [(meta, "s")]
-    ins += [(item, "f") for item in (feed1, late1, *late_words, layer0, late_regions)]
+    ins += [(item, "h") for item in (feed1, late1, *late_words, layer0, late_regions)]
     half = chunk // 2
     outs = [
         ((2, chunk, units), f32, "h"),
@@ -1026,6 +1233,36 @@
         ((half, width), f32, "h"),
     ]
     return call(body, ins, outs, (), 4.0, "placed_gradients")
+
+
+def prepared(ids, lengths, att_bias, att_post, feed_bias, feed_post):
+    batch = lengths[0].shape[1]
+    n_feed = feed_bias.shape[2] // D
+
+    def body(flush, ids, words, regions, att_bias, att_post, feed_bias, feed_post, small, meta):
+        meta[0] = ids[0]
+        meta[1 + 2 * batch] = ids[1]
+        for side, counts in enumerate((words, regions)):
+            for i in range(batch):
+                meta[1 + side * batch + i] = counts[ids[0], i]
+        half = att_bias.shape[3]
+        for side in (0, 1):
+            for j in (0, 1):
+                small[side, ROW_ATT_BIAS : ROW_ATT_BIAS + 1, j * half : (j + 1) * half] = att_bias[
+                    0, side, j : j + 1
+                ]
+            small[side, ROW_ATT_POST : ROW_ATT_POST + 3] = att_post[0, side]
+            for j in range(n_feed):
+                row = ROW_FEED_BIAS + j
+                small[side, row : row + 1] = feed_bias[0, side : side + 1, j * D : (j + 1) * D]
+            small[side, ROW_FEED_POST : ROW_FEED_POST + 3] = feed_post[0, side]
+            end = ROW_FEED_POST + 3
+            small[side, end:] = jnp.zeros((SMALL_ROWS - end, D), f32)
+
+    ins = [(ids, "s"), (lengths[0], "s"), (lengths[1], "s")]
+    ins += [(item, "f") for item in (att_bias, att_post, feed_bias, feed_post)]
+    outs = [((2, SMALL_ROWS, D), f32, "h"), ((2 + 2 * batch,), jnp.int32, "s")]
+    return call(body, ins, outs, (), 1.0, "prepared")
 
 
 def swap(value, axis, distance=1):
@@ -1063,10 +1300,6 @@
     both = (0, 1)
     chains = [[s * dp_count + 2 * z + y for s, z in chunk_order(groups)] for y in both]
 
-    def flat(value):
-        own = lax.dynamic_index_in_dim(value, section, 0, keepdims=False)
-        return own.transpose(1, 0, 2).reshape(-1, D)
-
     def unflat(value):
         return value.reshape(-1, batch, D).transpose(1, 0, 2)[None]
 
@@ -1087,47 +1320,39 @@
     chooser = chooser_of(dp_count, False)
     cross_chooser = chooser_of(2 * dp_count, True)
 
-    small_own = jnp.concatenate(
-        [
-            attention_bias[0].reshape(2, 1, D),
-            attention_post[0],
-            feed_bias[0].reshape(2, -1, D),
-            feed_post[0],
-            jnp.zeros((2, SMALL_ROWS - 9, D), f32),
-        ],
-        axis=1,
-    )
-    small_other = swap(small_own, "section")
-    smalls = [jnp.where(section == layer, small_own, small_other) for layer in both]
-    small = [[smalls[layer][side] for side in both] for layer in both]
+    ids = jnp.stack([section, place]).astype(jnp.int32)
+    small_own, meta = prepared(
+        ids,
+        (word_lengths, region_counts),
+        attention_bias,
+        attention_post,
+        feed_bias,
+        feed_post,
+    )
+    small = (small_own, swap(small_own, "section"))
     att_in_own = attention_in.transpose(0, 1, 3, 2, 4)
     att_in = (att_in_own, swap(att_in_own, "section"))
     att_out = (attention_out, swap(attention_out, "section"))
-    states = [flat(word_state), flat(region_state)]
+    states = [value.transpose(0, 2, 1, 3) for value in (word_state, region_state)]
     feed_in_later, feed_out_later, *_ = lax.optimization_barrier(
-        (feed_in, feed_out, att_in[1], att_out[1], smalls[0], chooser, cross_chooser, *states)
+        (feed_in, feed_out, att_in[1], att_out[1], small[1], chooser, cross_chooser)
     )
     ff_in = (feed_in, swap(feed_in_later, "section"))
     ff_out = (feed_out, swap(feed_out_later, "section"))
     cross_entry = cross_in.transpose(1, 0, 2)
 
-    lengths = [
-        lax.dynamic_index_in_dim(value, section, 0, keepdims=False)
-        for value in (word_lengths, region_counts)
-    ]
-    meta = jnp.concatenate([section[None].astype(jnp.int32), *lengths])
-    cotangents = [flat(word_cotangent), flat(region_cotangent)]
-    rows = [state.shape[0] for state in states]
+    cotangents = [value.transpose(0, 2, 1, 3) for value in (word_cotangent, region_cotangent)]
+    rows = [state.shape[1] * batch for state in states]
     total_rows = sum(rows)
 
-    def in_order(step, pack_index, tie=None, joined=True):
+    def in_order(step, pack_index, tie=None, joined=True, order=(1, 0)):
         results = [None, None]
         given = None
-        for side in (1, 0):
+        for side in order:
             ties = () if tie is None else (tie,)
             place = (total_rows, rows[0] * side, given) if joined else ()
             results[side] = step(side, place, ties)
-            tie, given = results[side][-1], results[side][pack_index]
+            tie, given = results[side][pack_index + 2], results[side][pack_index]
         return results
 
     def over_mp(results, index):
@@ -1135,7 +1360,7 @@
 
     self0 = in_order(
         lambda side, place, ties: self_forward(
-            side, 0, batch, meta, states[side], None, small[0][side], chooser, att_in, att_out,
+            side, 0, batch, meta, states[side], None, small, chooser, att_in, att_out,
             place, ties,
         ),
         3,
@@ -1143,7 +1368,7 @@
     got = over_mp(self0, 4)
     feed0 = in_order(
         lambda side, place, ties: feed_forward(
-            side, 0, batch, meta, states[side], self0[side][4], got[side], small[0][side], chooser,
+            side, 0, batch, meta, self0[side][6], self0[side][4], got[side], small, chooser,
             ff_in, ff_out, place, ties,
         ),
         4,
@@ -1151,43 +1376,51 @@
     )
     got = over_mp(feed0, 6)
     self0_there = swap(self0[0][3], "dp")
-    cross_w, cross_r, cross_pack = cross_forward(
+    cross_w, cross_r, cross_pack, held = cross_forward(
         batch,
         meta,
         [(feed0[side][0], feed0[side][6], got[side]) for side in both],
-        small[0],
+        small,
         cross_chooser,
         cross_entry,
         cross_bias,
         cross_out,
-    )
+        (att_in, att_out),
+    )
+    att_in1, att_out1 = [(item,) for item in held]
     cross = (cross_w, cross_r)
     got = over_mp(cross, 7)
     feed0_there = swap(feed0[0][4], "dp")
     self1 = in_order(
         lambda side, place, ties: self_forward(
             side, 1, batch, meta, cross[side][0], (cross[side][7], got[side], cross_post),
-            small[1][side], chooser, att_in, att_out, place, ties + ((self0_there, "a"), (cotangents[side], "w")),
+            small, chooser, att_in1, att_out1, place, ties + ((self0_there, "a"),),
+            (ff_in if side == ORDER[0] else ff_out,),
         ),
         3,
-    )
+        None,
+        True,
+        ORDER,
+    )
+    ff_in1, ff_out1 = [(self1[side][9],) for side in ORDER]
     got = over_mp(self1, 4)
     cross_there = swap(cross_pack, "dp")
     feed1 = in_order(
         lambda side, place, ties: feed_forward(
-            side, 1, batch, meta, self1[side][6], self1[side][4], got[side], small[1][side], chooser,
-            ff_in, ff_out, place, ties + ((cross_there if side == 0 else feed0_there, "a"),),
+            side, 1, batch, meta, self1[side][6], self1[side][4], got[side], small, chooser,
+            ff_in1, ff_out1, place, ties + ((cross_there if side == ORDER[-1] else feed0_there, "a"),),
         ),
         4,
-        self1[0][5],
+        self1[ORDER[-1]][5],
         False,
+        ORDER,
     )
     got = over_mp(feed1, 6)
     self1_there = swap(self1[0][3], "dp")
     feed1_there = [swap(feed1[side][4], "dp") for side in both]
 
     given, back_feed1 = None, [None, None]
-    for side in (1, 0):
+    for side in ORDER:
         given = feed_backward(
             1,
             (side,),
@@ -1196,11 +1429,11 @@
             meta,
             [(feed1[side][0], feed1[side][6], got[side], cotangents[side])],
             None,
-            [small[1][side]],
+            small,
             chooser,
             [feed1[side][5]],
-            ff_in,
-            ff_out,
+            ff_in1,
+            ff_out1,
             ((feed1_there[side], "a"),),
             given,
         )
@@ -1214,7 +1447,7 @@
         )
 
     given, back_self1 = None, [None, None]
-    for side in (1, 0):
+    for side in ORDER:
         given = self_backward(
             1,
             (side,),
@@ -1222,12 +1455,12 @@
             meta,
             [feed1[side][1:3]],
             (back_feed1[side][0], back_feed1[side][3], got[side]),
-            [small[1][side]],
+            small,
             chooser,
             [self1[side][0]],
             [self1[side][1]],
-            att_in,
-            att_out,
+            att_in1,
+            att_out1,
             (),
             given,
         )
@@ -1236,21 +1469,19 @@
     feed1_grads = gradients(
         meta,
         [
-            Block(
+            Halves(
                 [feed1[side][3] for side in both],
-                [feed1[side][4] for side in both],
                 feed1_there,
-                back_feed1[0][1],
-                [back_feed1[side][2] for side in both],
+                [back_feed1[side][1] for side in both],
                 back_feed1_there,
             )
         ],
         None,
         groups,
         "feed_gradients_1",
-        (back_self1[0][5],),
-    )
-    back_self1_there = swap(back_self1[0][2], "dp")
+        (back_self1[ORDER[-1]][5],),
+    )
+    back_self1_there = swap(back_self1[ORDER[-1]][2], "dp")
     back_cross = cross_backward(
         meta,
         [self1[side][7:9] for side in both],
@@ -1268,7 +1499,17 @@
     cross_post_grad, cross_bias_grad = back_cross[4:6]
     got = swap(back_cross[3], "mp")
     back_cross_there = swap(back_cross[2], "dp")
-    feed1_share = scatter(feed1_grads)
+    feed1_pair = scatter(feed1_grads).reshape(2, D // dp_count, -1)
+    feed1_own = lax.dynamic_index_in_dim(feed1_pair, place, 0, keepdims=False)
+    feed1_other = swap(lax.dynamic_index_in_dim(feed1_pair, 1 - place, 0, keepdims=False), "dp")
+    halves = (
+        jnp.where(place == 0, feed1_own, feed1_other),
+        jnp.where(place == 0, feed1_other, feed1_own),
+    )
+    count = units // 2
+    feed1_share = jnp.concatenate(
+        [half[:, j * count : (j + 1) * count] for j in both for half in halves], axis=1
+    )
 
     back_feed0 = feed_backward(
         0,
@@ -1278,7 +1519,7 @@
         meta,
         [cross[side][1:3] for side in (1, 0)],
         (back_cross[0], back_cross[3], got),
-        small[0][::-1],
+        small,
         chooser,
         [feed0[side][5] for side in (1, 0)],
         ff_in,
@@ -1294,8 +1535,8 @@
                 [self1[side][2] for side in both],
                 [self1[0][3]],
                 [self1_there],
-                back_self1[0][1],
-                [back_self1[0][2]],
+                back_self1[ORDER[-1]][1],
+                [back_self1[ORDER[-1]][2]],
                 [back_self1_there],
             )
         ],
@@ -1318,7 +1559,7 @@
         meta,
         [feed0[side][1:3] for side in (1, 0)],
         (back_feed0[0], back_feed0[3], got),
-        small[0][::-1],
+        small,
         chooser,
         [self0[side][0] for side in (1, 0)],
         [self0[side][1] for side in (1, 0)],
@@ -1352,7 +1593,7 @@
         None,
         groups,
         "gradients_0",
-        (back_self0[5], feed1_share),
+        (back_self0[5], feed1_pair),
         True,
     )
     layer0_kept, layer0_sent = layer0_grads
@@ -1399,12 +1640,12 @@
             ),
         ),
         packed(
-            back_self1[0],
-            back_feed1[0],
+            back_self1[ORDER[-1]],
+            back_feed1[ORDER[-1]],
             squares_of(
                 [self1[side][5] for side in both],
                 [feed1[side][7] for side in both],
-                [back_feed1[0][6][side] for side in both],
+                [back_feed1[ORDER[-1]][6][side] for side in both],
             ),
         ),
     ]

time: 327 us -> 317 us (0.969)
  starting transfers between devices: 38.9 us -> 51.3 us
  waiting for transfers between devices: 116 us -> 107 us
  Pallas kernels: 116 us -> 108 us
  local copies, waits for them, and re-layouts: 23.1 us -> 19.7 us
    ppermute x39 -> x40, starting transfers between devices: 34.4 us -> 46 us  [swap(): return lax.ppermute(value, axis, [(i, i ^ distance) for i in range(count)])]
    pallas_call x20 -> x21, Pallas kernels: 116 us -> 108 us  [call(): pl.pallas_call(whole, out_shape=[spaces[out[2]]((out[3], *out[0][1:]) if...]
    ppermute x39 -> x40, waiting for transfers between devices: 76.9 us -> 70.4 us  [swap(): return lax.ppermute(value, axis, [(i, i ^ distance) for i in range(count)])]
    reduce_scatter x1, waiting for transfers between devices: 30.2 us -> 25 us  [on_device(): lax.psum_scatter(layer0_total, 'dp', scatter_dimension=0, axis_index_grou...]
    unnamed x188 -> x191, local copies, waits for them, and re-layouts: 10.6 us -> 13.6 us
  transfers between devices with their start and end apart: 45 -> 46, of which waited for: 21 -> 21; matrix products, arithmetic and copies ran while one was open for 8% -> 6% of each run, Pallas kernels for 33% -> 32%
where the time goes in v2:
time: 317 us; the launch traced here: 311 us
  Pallas kernels  108 us (34%)
  waiting for transfers between devices  107 us (34%)
  starting transfers between devices  51.3 us (16%)
  local copies, waits for them, and re-layouts  19.7 us (6%)
  between operations  15.6 us (5%)
  other arithmetic  9.28 us (3%)
    pallas_call x21, Pallas kernels, call(): pl.pallas_call(whole, out_shape=[spaces[out[2]]((out[3], *out[0][1:]) if...  108 us
    ppermute x40, waiting for transfers between devices, swap(): return lax.ppermute(value, axis, [(i, i ^ distance) for i in range(count)])  70.4 us
    ppermute x40, starting transfers between devices, swap(): return lax.ppermute(value, axis, [(i, i ^ distance) for i in range(count)])  46 us
    reduce_scatter x1, waiting for transfers between devices, on_device(): lax.psum_scatter(layer0_total, 'dp', scatter_dimension=0, axis_index_grou...  25 us
    unnamed x191, local copies, waits for them, and re-layouts  13.6 us
    reduce_scatter x2, waiting for transfers between devices, scatter(): lax.psum_scatter(value, ('section', 'dp'), scatter_dimension=0, axis_inde...  9.69 us
  transfers between devices with their start and end apart: 46, of which 21 were waited for; matrix products, arithmetic and copies ran while one was open for 6% of the time, Pallas kernels for 32%

profile of v2, /device:TPU:0, one launch (start us, length us, event | category | flops | bytes accessed | tf_op | source)
XLA Modules:
  0.0 311.2 jit_solution(8483104052251997865)
XLA Ops:
  17.1 4.5 %self_forward_0_1.1 = (bf16[3,144,384]{2,1,0:T(8,128)(2,1)}, bf16[6,144,144]{2,1,0:T(8,128)(2,1)}, bf16[144,384]{1,0:T(8,128)(2,1)}, bf16[224,768]{1,0:T(8,128)(...) custom-call(s32[10]{0:T(128)S(4)} %get-tuple-element.176.refs_0_, ...), custom_call_target="tpu_custom_call" | custom-call | flops 2300000000 | tf_op jit(solution)/shard_map/self_forward_0_1/pallas_call | solution.py:287
  21.6 2.9 collective-permute-start.6
  24.5 4.0 %self_forward_0_0.1 = (bf16[3,80,384]{2,1,0:T(8,128)(2,1)}, bf16[6,80,80]{2,1,0:T(8,128)(2,1)}, bf16[80,384]{1,0:T(8,128)(2,1)}, bf16[224,768]{1,0:T(8,128)(2,1)...) custom-call(s32[10]{0:T(128)S(4)} %get-tuple-element.176.refs_0_, ...), custom_call_target="tpu_custom_call", output_to_operand_aliasing={{3}: (9, {})} | custom-call | flops 2300000000 | tf_op jit(solution)/shard_map/self_forward_0_0/pallas_call | solution.py:287
  30.6 6.4 %feed_forward_0_1.1 = (f32[144,768]{1,0:T(8,128)S(1)}, f32[144,768]{1,0:T(8,128)}, f32[144,1]{1,0:T(8,128)}, bf16[144,384]{1,0:T(8,128)(2,1)}, bf16[224,1920]{1,...) custom-call(s32[10]{0:T(128)S(4)} %get-tuple-element.176.refs_0_, ...), custom_call_target="tpu_custom_call" | custom-call | flops 2472499968 | tf_op jit(solution)/shard_map/feed_forward_0_1/pallas_call | solution.py:287
  37.1 2.5 collective-permute-start.9
  39.6 3.3 %feed_forward_0_0.1 = (f32[80,768]{1,0:T(8,128)S(1)}, f32[80,768]{1,0:T(8,128)}, f32[80,1]{1,0:T(8,128)}, bf16[80,384]{1,0:T(8,128)(2,1)}, bf16[224,1920]{1,0:T(...) custom-call(s32[10]{0:T(128)S(4)} %get-tuple-element.176.refs_0_, ...), custom_call_target="tpu_custom_call", output_to_operand_aliasing={{4}: (11, {})} | custom-call | flops 2472499968 | tf_op jit(solution)/shard_map/feed_forward_0_0/pallas_call | solution.py:287
  45.5 2.3 collective-permute-done.8.refs_3_
  48.8 7.4 %cross_forward.1 = (bf16[80,768]{1,0:T(8,128)(2,1)S(1)}, f32[80,768]{1,0:T(8,128)}, f32[80,1]{1,0:T(8,128)}, f32[2,128]{1,0:T(2,128)}, bf16[80,384]{1,0:T(8,128)...) custom-call(s32[10]{0:T(128)S(4)} %get-tuple-element.176.refs_0_, ...), custom_call_target="tpu_custom_call" | custom-call | flops 3910000128 | tf_op jit(solution)/shard_map/cross_forward/pallas_call | solution.py:287
  58.3 4.1 %collective-permute-done.11.refs_3_ = bf16[144,768]{1,0:T(8,128)(2,1)S(1)} collective-permute-done((bf16[144,768]{1,0:T(8,128)(2,1)S(1)}, bf16[144,768]{1,0:T(8,128)(2,1)S(1)}, u32[]{:S(2)}, u32[]{:S(2)}) %collective-permute-start.11) | collective-permute-done | bytes 221216 | tf_op jit(solution)/shard_map/ppermute | solution.py:1270
  62.3 5.0 %self_forward_1_1.1 = (bf16[3,144,384]{2,1,0:T(8,128)(2,1)}, bf16[6,144,144]{2,1,0:T(8,128)(2,1)}, bf16[144,384]{1,0:T(8,128)(2,1)}, bf16[224,768]{1,0:T(8,128)(...) custom-call(s32[10]{0:T(128)S(4)} %get-tuple-element.176.refs_0_, ...), custom_call_target="tpu_custom_call" | custom-call | flops 2300000000 | tf_op jit(solution)/shard_map/self_forward_1_1/pallas_call | solution.py:287
  67.3 1.8 collective-permute-start.14
  70.0 4.1 %self_forward_1_0.1 = (bf16[3,80,384]{2,1,0:T(8,128)(2,1)}, bf16[6,80,80]{2,1,0:T(8,128)(2,1)}, bf16[80,384]{1,0:T(8,128)(2,1)}, bf16[224,768]{1,0:T(8,128)(2,1)...) custom-call(s32[10]{0:T(128)S(4)} %get-tuple-element.176.refs_0_, ...), custom_call_target="tpu_custom_call", output_to_operand_aliasing={{3}: (12, {})} | custom-call | flops 2300000000 | tf_op jit(solution)/shard_map/self_forward_1_0/pallas_call | solution.py:287
  74.2 2.9 feed_forward_1_1.1
  80.2 4.1 %collective-permute-done.13.refs_3_ = bf16[80,768]{1,0:T(8,128)(2,1)S(1)} collective-permute-done((bf16[80,768]{1,0:T(8,128)(2,1)S(1)}, bf16[80,768]{1,0:T(8,128)(2,1)S(1)}, u32[]{:S(2)}, u32[]{:S(2)}) %collective-permute-start.13) | collective-permute-done | bytes 122912 | tf_op jit(solution)/shard_map/ppermute | solution.py:1270
  84.3 2.6 feed_forward_1_0.1
  90.7 4.7 %feed_backward_1_1.1 = (f32[144,768]{1,0:T(8,128)S(1)}, bf16[144,1536]{1,0:T(8,128)(2,1)}, bf16[144,1536]{1,0:T(8,128)(2,1)}, bf16[144,768]{1,0:T(8,128)(2,1)S(1...) custom-call(s32[10]{0:T(128)S(4)} %get-tuple-element.176.refs_0_, ...), custom_call_target="tpu_custom_call" | custom-call | flops 4066071552 | tf_op jit(solution)/shard_map/feed_backward_1_1/pallas_call | solution.py:287
  96.7 4.1 %feed_backward_1_0.1 = (f32[80,768]{1,0:T(8,128)S(1)}, bf16[80,1536]{1,0:T(8,128)(2,1)}, bf16[80,1536]{1,0:T(8,128)(2,1)}, bf16[80,768]{1,0:T(8,128)(2,1)S(1)}, ...) custom-call(s32[10]{0:T(128)S(4)} %get-tuple-element.176.refs_0_, ...), custom_call_target="tpu_custom_call", output_to_operand_aliasing={{4}: (10, {}), {5}: (11, {}), {6}: (12, {})} | custom-call | flops 2258928640 | tf_op jit(solution)/shard_map/feed_backward_1_0/pallas_call | solution.py:287
  103.9 4.1 %self_backward_1_1.1 = (f32[144,768]{1,0:T(8,128)}, bf16[224,384]{1,0:T(8,128)(2,1)}, bf16[224,1536]{1,0:T(8,128)(2,1)}, bf16[144,768]{1,0:T(8,128)(2,1)}, f32[2,3,768]{2,1,0:T(4,128)}, /*index=5*/f32[2,2,384]{2,1,0:T(2,128)}) custom-call(s32[10]{0:T(128)S(4)} %get-tuple-element.176.refs_0_, f32[144,768]{1,0:T(8,128)S(1)} %copy-done.32, ...), custom_call_target="tpu_custom_call" | custom-call | flops 4435714048 | tf_op jit(solution)/shard_map/self_backward_1_1/pallas_call | solution.py:287
  108.0 3.7 %self_backward_1_0.1 = (f32[80,768]{1,0:T(8,128)}, bf16[224,384]{1,0:T(8,128)(2,1)}, bf16[224,1536]{1,0:T(8,128)(2,1)}, bf16[80,768]{1,0:T(8,128)(2,1)}, f32[2,3,768]{2,1,0:T(4,128)}, /*index=5*/f32[2,2,384]{2,1,0:T(2,128)}) custom-call(s32[10]{0:T(128)S(4)} %get-tuple-element.176.refs_0_, ...), custom_call_target="tpu_custom_call", output_to_operand_aliasing={{1}: (13, {}), {2}: (14, {}), {4}: (15, {}), {5}: (16, {})} | custom-call | flops 2464285696 | tf_op jit(solution)/shard_map/self_backward_1_0/pallas_call | solution.py:287
  113.8 5.1 %feed_gradients_1.1.refs_19_ = bf16[1536,1536]{1,0:T(8,128)(2,1)} custom-call(s32[10]{0:T(128)S(4)} %get-tuple-element.176.refs_0_, bf16[80,1536]{1,0:T(8,128)(2,1)} %get-tuple-element.255.refs_1_, bf16[144,1536]{1,0:T(8,128)(2,1)} %get-tuple-element.256.refs_2_, bf16[80,1536]{1,0:T(8,128)(2,1)} %copy-done.16, bf16[144,1536]{1,0:T(8,128)(2,1)} %copy-done.31, ...), custom_call_target="tpu_custom_call" | custom-call | flops 3449999872 | tf_op jit(solution)/shard_map/feed_gradients_1/pallas_call | solution.py:287
  120.0 1.7 collective-permute-start.26
  124.0 6.3 %collective-permute-done.26.refs_20_.refs_4_ = bf16[224,768]{1,0:T(8,128)(2,1)S(1)} collective-permute-done((bf16[224,768]{1,0:T(8,128)(2,1)S(1)}, bf16[224,768]{1,0:T(8,128)(2,1)S(1)}, u32[]{:S(2)}, u32[]{:S(2)}) %collective-permute-start.26) | collective-permute-done | bytes 344096 | tf_op jit(solution)/shard_map/ppermute | solution.py:1270
  130.4 9.2 %cross_backward.1 = (f32[224,768]{1,0:T(8,128)S(1)}, bf16[224,384]{1,0:T(8,128)(2,1)}, bf16[224,1536]{1,0:T(8,128)(2,1)}, bf16[224,768]{1,0:T(8,128)(2,1)S(1)}, f32[3,768]{1,0:T(4,128)}, /*index=5*/f32[2,384]{1,0:T(2,128)}) custom-call(s32[10]{0:T(128)S(4)} %get-tuple-element.176.refs_0_, f32[80,768]{1,0:T(8,128)} %get-tuple-element.208.refs_1_, ...), custom_call_target="tpu_custom_call" | custom-call | flops 5750000128 | tf_op jit(solution)/shard_map/cross_backward/pallas_call | solution.py:287
  139.7 2.3 collective-permute-start.27
  142.0 1.7 collective-permute-start.31
  143.7 3.5 %collective-permute-done.27.refs_7_ = bf16[224,768]{1,0:T(8,128)(2,1)S(1)} collective-permute-done((bf16[224,768]{1,0:T(8,128)(2,1)S(1)}, bf16[224,768]{1,0:T(8,128)(2,1)S(1)}, u32[]{:S(2)}, u32[]{:S(2)}) %collective-permute-start.27) | collective-permute-done | bytes 344096 | tf_op jit(solution)/shard_map/ppermute | solution.py:1270
  147.3 7.8 %feed_backward_0_10.1 = (f32[224,768]{1,0:T(8,128)}, bf16[224,384]{1,0:T(8,128)(2,1)}, bf16[224,1920]{1,0:T(8,128)(2,1)}, bf16[224,768]{1,0:T(8,128)(2,1)}, f32[2,3,768]{2,1,0:T(4,128)}, /*index=5*/f32[2,1,1536]{2,1,0:T(1,128)}) custom-call(s32[10]{0:T(128)S(4)} %get-tuple-element.176.refs_0_, f32[144,768]{1,0:T(8,128)S(1)} %copy-done.14, ...), custom_call_target="tpu_custom_call" | custom-call | flops 6325000192 | tf_op jit(solution)/shard_map/feed_backward_0_10/pallas_call | solution.py:287
  156.1 5.3 %late_gradients_1.1.refs_19_ = bf16[1152,1536]{1,0:T(8,128)(2,1)} custom-call(s32[10]{0:T(128)S(4)} %get-tuple-element.176.refs_0_, bf16[80,384]{1,0:T(8,128)(2,1)} %get-tuple-element.282.refs_1_, bf16[144,384]{1,0:T(8,128)(2,1)} %get-tuple-element.283.refs_2_, bf16[224,768]{1,0:T(8,128)(2,1)} %get-tuple-element.262.refs_3_, bf16[224,768]{1,0:T(8,128)(2,1)} %copy-done.34, ...), custom_call_target="tpu_custom_call" | custom-call | flops 3449999872 | tf_op jit(solution)/shard_map/late_gradients_1/pallas_call | solution.py:287
  162.4 2.0 collective-permute-start.30
  166.2 3.5 %collective-permute-done.30.refs_7_ = bf16[224,768]{1,0:T(8,128)(2,1)S(1)} collective-permute-done((bf16[224,768]{1,0:T(8,128)(2,1)S(1)}, bf16[224,768]{1,0:T(8,128)(2,1)S(1)}, u32[]{:S(2)}, u32[]{:S(2)}) %collective-permute-start.30) | collective-permute-done | bytes 344096 | tf_op jit(solution)/shard_map/ppermute | solution.py:1270
  169.7 11.6 %self_backward_0_10.1 = (f32[224,768]{1,0:T(8,128)}, bf16[224,384]{1,0:T(8,128)(2,1)}, bf16[224,1536]{1,0:T(8,128)(2,1)}, bf16[224,768]{1,0:T(8,128)(2,1)}, f32[2,3,768]{2,1,0:T(4,128)}, /*index=5*/f32[2,2,384]{2,1,0:T(2,128)}) custom-call(s32[10]{0:T(128)S(4)} %get-tuple-element.176.refs_0_, f32[144,768]{1,0:T(8,128)} %get-tuple-element.272.refs_1_, ...), custom_call_target="tpu_custom_call" | custom-call | flops 6899999744 | tf_op jit(solution)/shard_map/self_backward_0_10/pallas_call | solution.py:287
  181.3 1.8 collective-permute-start.32
  183.1 9.4 %collective-permute-done.32.refs_14_ = bf16[224,1536]{1,0:T(8,128)(2,1)S(1)} collective-permute-done((bf16[224,1536]{1,0:T(8,128)(2,1)}, bf16[224,1536]{1,0:T(8,128)(2,1)S(1)}, u32[]{:S(2)}, u32[]{:S(2)}) %collective-permute-start.32) | collective-permute-done | bytes 688160 | tf_op jit(solution)/shard_map/ppermute | solution.py:1270
  193.4 6.7 %gradients_0.1 = (bf16[384,4608]{1,0:T(8,128)(2,1)}, bf16[384,4608]{1,0:T(8,128)(2,1)}) custom-call(s32[10]{0:T(128)S(4)} %get-tuple-element.176.refs_0_, bf16[80,384]{1,0:T(8,128)(2,1)} %get-tuple-element.189.refs_1_, bf16[144,384]{1,0:T(8,128)(2,1)} %get-tuple-element.190.refs_2_, bf16[224,1920]{1,0:T(8,128)(2,1)} %get-tuple-element.191.refs_3_, ...), custom_call_target="tpu_custom_call" | custom-call | flops 3449999872 | tf_op jit(solution)/shard_map/gradients_0/pallas_call | solution.py:287
  200.2 6.4 %collective-permute-done.33 = bf16[384,4608]{1,0:T(8,128)(2,1)S(1)} collective-permute-done((bf16[384,4608]{1,0:T(8,128)(2,1)}, bf16[384,4608]{1,0:T(8,128)(2,1)S(1)}, u32[]{:S(2)}, u32[]{:S(2)}) %collective-permute-start.33) | collective-permute-done | bytes 3538976 | tf_op jit(solution)/shard_map/ppermute | solution.py:1270
  206.6 4.8 %add_convert_fusion = bf16[384,4608]{1,0:T(8,128)(2,1)} fusion(bf16[384,4608]{1,0:T(8,128)(2,1)S(1)} %collective-permute-done.33, bf16[384,4608]{1,0:T(8,128)(2,1)} %get-tuple-element.293), kind=kLoop, calls=%fused_computation | loop fusion | flops 7077888 | bytes 10616832 | tf_op jit(solution)/shard_map/convert_element_type | solution.py:1601
  211.6 9.7 %reduce-scatter.6.cloned.1.call-done.refs_2_ = bf16[144,1536]{1,0:T(8,128)(2,1)} async-done(((bf16[1152,1536]{1,0:T(8,128)(2,1)}), bf16[144,1536]{1,0:T(8,128)(2,1)}) %reduce-scatter.6.cloned.1.call-update) | async-done | bytes 442384 | tf_op jit(solution)/shard_map/reduce_scatter | solution.py:1445
  226.5 1.8 collective-permute-start.39
  228.2 3.1 %collective-permute-done.39 = f32[25,768]{1,0:T(8,128)S(1)} collective-permute-done((f32[25,768]{1,0:T(8,128)S(1)}, f32[25,768]{1,0:T(8,128)S(1)}, u32[]{:S(2)}, u32[]{:S(2)}) %collective-permute-start.39) | collective-permute-done | bytes 76832 | tf_op jit(solution)/shard_map/ppermute | solution.py:1270
  231.5 9.0 %collective-permute-done.40 = f32[25,768]{1,0:T(8,128)S(1)} collective-permute-done((f32[25,768]{1,0:T(8,128)S(1)}, f32[25,768]{1,0:T(8,128)S(1)}, u32[]{:S(2)}, u32[]{:S(2)}) %collective-permute-start.40) | collective-permute-done | bytes 76832 | tf_op jit(solution)/shard_map/ppermute | solution.py:1270
  242.5 2.0 collective-permute-start.37
  244.5 7.8 %collective-permute-done.41 = f32[25,768]{1,0:T(8,128)S(1)} collective-permute-done((f32[25,768]{1,0:T(8,128)S(1)}, f32[25,768]{1,0:T(8,128)S(1)}, u32[]{:S(2)}, u32[]{:S(2)}) %collective-permute-start.41) | collective-permute-done | bytes 76832 | tf_op jit(solution)/shard_map/ppermute | solution.py:1270
  252.4 4.2 %collective-permute-start.34 = (bf16[96,1536]{1,0:T(8,128)(2,1)S(1)}, bf16[96,1536]{1,0:T(8,128)(2,1)S(1)}, u32[]{:S(2)}, u32[]{:S(2)}) collective-permute-start(bf16[96,1536]{1,0:T(8,128)(2,1)S(1)} %dynamic-slice_bitcast_fusion), channel_id=1, source_target_pairs={{0,2},{2,0},{4,6},{6,4},{8,10},{10,8},{12,14},{14,12},{1,3},{3,1},... | collective-permute-start | bytes 884744 | tf_op jit(solution)/shard_map/ppermute | solution.py:1270
  256.8 4.4 %collective-permute-done.34 = bf16[96,1536]{1,0:T(8,128)(2,1)S(1)} collective-permute-done((bf16[96,1536]{1,0:T(8,128)(2,1)S(1)}, bf16[96,1536]{1,0:T(8,128)(2,1)S(1)}, u32[]{:S(2)}, u32[]{:S(2)}) %collective-permute-start.34) | collective-permute-done | bytes 294944 | tf_op jit(solution)/shard_map/ppermute | solution.py:1270
  261.4 2.2 collective-permute-start.35
  269.5 25.0 %reduce-scatter.8.cloned.1.call-done.refs_5_ = bf16[96,4608]{1,0:T(8,128)(2,1)} async-done(((bf16[384,4608]{1,0:T(8,128)(2,1)}), bf16[96,4608]{1,0:T(8,128)(2,1)}) %reduce-scatter.8.cloned.1.call-update) | async-done | bytes 884752 | tf_op jit(solution)/shard_map/reduce_scatter | solution.py:1602
  297.1 2.0 collective-permute-done.42.refs_6_
  300.0 4.2 %placed_gradients.1 = (f32[2,96,1536]{2,1,0:T(8,128)}, f32[2,96,1536]{2,1,0:T(8,128)}, f32[2,3,96,384]{3,2,1,0:T(8,128)}, f32[2,96,384]{2,1,0:T(8,128)}, f32[3,48,384]{2,1,0:T(8,128)}, /*index=5*/f32[48,384]{1,0:T(8,128)}) custom-call(s32[10]{0:T(128)S(4)} %get-tuple-element.176.refs_0_, bf16[96,3072]{1,0:T(8,128)(2,1)} %copy-done.44, ...), custom_call_target="tpu_custom_call" | custom-call | flops 2300000000 | tf_op jit(solution)/shard_map/placed_gradients/pallas_call | solution.py:287
  (321 shorter events, 56.4 us)
Async XLA Ops:
  7.2 185.3 %reduce-scatter.4.cloned.1.call-start = ((), (), s32[]{:S(2)}) async-start(), calls=%async_computation.3 | async-start | bytes 5308416 | tf_op jit(solution)/shard_map/reduce_scatter | solution.py:1445
  7.2 8.4 %collective-permute-start.1 = (bf16[1,2,3,768,384]{4,3,2,1,0:T(8,128)(2,1)}, bf16[1,2,3,768,384]{4,3,2,1,0:T(8,128)(2,1)}, u32[]{:S(2)}, u32[]{:S(2)}) collective-permute-start(bf16[1,2,3,768,384]{4,3,2,1,0:T(8,128)(2,1)} %bitcast.61), channel_id=1, source_target_pairs={{0,16},{16,0},{1,17},{17,1},{2,18},{18,2},{3,19},{19,3},{4,20},{20... | collective-permute-start | bytes 10616840 | tf_op jit(solution)/shard_map/ppermute | solution.py:1270
  7.8 7.9 %collective-permute-start.2 = (bf16[1,2,384,768]{3,2,1,0:T(8,128)(2,1)}, bf16[1,2,384,768]{3,2,1,0:T(8,128)(2,1)S(1)}, u32[]{:S(2)}, u32[]{:S(2)}) collective-permute-start(bf16[1,2,384,768]{3,2,1,0:T(8,128)(2,1)} %refs_17_.1), channel_id=1, source_target_pairs={{0,16},{16,0},{1,17},{17,1},{2,18},{18,2},{3,19},{19,3},{4,20},{20... | collective-permute-start | bytes 3538952 | tf_op jit(solution)/shard_map/ppermute | solution.py:1270
  13.5 2.1 collective-permute-start
  14.5 132.8 %copy-start = (bf16[768,768]{1,0:T(8,128)(2,1)}, bf16[768,768]{1,0:T(8,128)(2,1)S(1)}, u32[]{:S(2)}) copy-start(bf16[768,768]{1,0:T(8,128)(2,1)S(1)} %fusion.refs_4_.refs_6_.refs_7_.refs_8_.refs_10_) | copy-start | bytes 3538948
  15.6 131.6 %copy-start.5 = (f32[2,16,768]{2,1,0:T(8,128)}, f32[2,16,768]{2,1,0:T(8,128)S(1)}, u32[]{:S(2)}) copy-start(f32[2,16,768]{2,1,0:T(8,128)S(1)} %collective-permute-done.refs_3_.refs_5_.refs_8_.refs_6_.refs_7_.refs_9_) | copy-start | bytes 294916
  15.7 14.5 %collective-permute-start.4 = (bf16[1,2,768,1536]{3,2,1,0:T(8,128)(2,1)}, bf16[1,2,768,1536]{3,2,1,0:T(8,128)(2,1)S(1)}, u32[]{:S(2)}, u32[]{:S(2)}) collective-permute-start(bf16[1,2,768,1536]{3,2,1,0:T(8,128)(2,1)} %refs_13_.1), channel_id=1, source_target_pairs={{0,16},{16,0},{1,17},{17,1},{2,18},{18,2},{3,19},{19,3},{4,20},{20... | collective-permute-start | bytes 14155784 | tf_op jit(solution)/shard_map/ppermute | solution.py:1270
  16.1 14.5 %collective-permute-start.5 = (bf16[1,2,1536,768]{3,2,1,0:T(8,128)(2,1)}, bf16[1,2,1536,768]{3,2,1,0:T(8,128)(2,1)S(1)}, u32[]{:S(2)}, u32[]{:S(2)}) collective-permute-start(bf16[1,2,1536,768]{3,2,1,0:T(8,128)(2,1)} %refs_15_.3), channel_id=1, source_target_pairs={{0,16},{16,0},{1,17},{17,1},{2,18},{18,2},{3,19},{19,3},{4,20},{20... | collective-permute-start | bytes 14155784 | tf_op jit(solution)/shard_map/ppermute | solution.py:1270
  21.6 8.5 %collective-permute-start.6 = (bf16[144,768]{1,0:T(8,128)(2,1)S(1)}, bf16[144,768]{1,0:T(8,128)(2,1)S(1)}, u32[]{:S(2)}, u32[]{:S(2)}) collective-permute-start(bf16[144,768]{1,0:T(8,128)(2,1)S(1)} %get-tuple-element.185.refs_2_), channel_id=1, source_target_pairs={{0,1},{1,0},{2,3},{3,2},{4,5},{5,4},{6,7},{7,6},{8,9},{9,8},{10,11... | collective-permute-start | bytes 663560 | tf_op jit(solution)/shard_map/ppermute | solution.py:1270
  28.5 11.0 %collective-permute-start.3 = (bf16[80,768]{1,0:T(8,128)(2,1)S(1)}, bf16[80,768]{1,0:T(8,128)(2,1)S(1)}, u32[]{:S(2)}, u32[]{:S(2)}) collective-permute-start(bf16[80,768]{1,0:T(8,128)(2,1)S(1)} %get-tuple-element.181.refs_2_), channel_id=1, source_target_pairs={{0,1},{1,0},{2,3},{3,2},{4,5},{5,4},{6,7},{7,6},{8,9},{9,8},{10,11... | collective-permute-start | bytes 368648 | tf_op jit(solution)/shard_map/ppermute | solution.py:1270
  37.1 10.8 %collective-permute-start.9 = (bf16[144,768]{1,0:T(8,128)(2,1)S(1)}, bf16[144,768]{1,0:T(8,128)(2,1)S(1)}, u32[]{:S(2)}, u32[]{:S(2)}) collective-permute-start(bf16[144,768]{1,0:T(8,128)(2,1)S(1)} %get-tuple-element.188.refs_12_.refs_5_), channel_id=1, source_target_pairs={{0,1},{1,0},{2,3},{3,2},{4,5},{5,4},{6,7},{7,6},{8,9},{9,8},{10,11... | collective-permute-start | bytes 663560 | tf_op jit(solution)/shard_map/ppermute | solution.py:1270
  42.9 4.9 %collective-permute-start.8 = (bf16[80,768]{1,0:T(8,128)(2,1)S(1)}, bf16[80,768]{1,0:T(8,128)(2,1)S(1)}, u32[]{:S(2)}, u32[]{:S(2)}) collective-permute-start(bf16[80,768]{1,0:T(8,128)(2,1)S(1)} %get-tuple-element.193.refs_2_), channel_id=1, source_target_pairs={{0,1},{1,0},{2,3},{3,2},{4,5},{5,4},{6,7},{7,6},{8,9},{9,8},{10,11... | collective-permute-start | bytes 368648 | tf_op jit(solution)/shard_map/ppermute | solution.py:1270
  43.5 14.8 %collective-permute-start.12 = (bf16[224,768]{1,0:T(8,128)(2,1)S(1)}, bf16[224,768]{1,0:T(8,128)(2,1)S(1)}, u32[]{:S(2)}, u32[]{:S(2)}) collective-permute-start(bf16[224,768]{1,0:T(8,128)(2,1)S(1)} %copy-done.46), channel_id=1, source_target_pairs={{0,2},{2,0},{4,6},{6,4},{8,10},{10,8},{12,14},{14,12},{1,3},{3,1},... | collective-permute-start | bytes 1032200 | tf_op jit(solution)/shard_map/ppermute | solution.py:1270
  44.4 29.8 %collective-permute-start.7 = (bf16[224,1920]{1,0:T(8,128)(2,1)}, bf16[224,1920]{1,0:T(8,128)(2,1)S(1)}, u32[]{:S(2)}, u32[]{:S(2)}) collective-permute-start(bf16[224,1920]{1,0:T(8,128)(2,1)} %get-tuple-element.191.refs_3_), channel_id=1, source_target_pairs={{0,2},{2,0},{4,6},{6,4},{8,10},{10,8},{12,14},{14,12},{1,3},{3,1},... | collective-permute-start | bytes 2580488 | tf_op jit(solution)/shard_map/ppermute | solution.py:1270
  56.2 6.2 %collective-permute-start.11 = (bf16[144,768]{1,0:T(8,128)(2,1)S(1)}, bf16[144,768]{1,0:T(8,128)(2,1)S(1)}, u32[]{:S(2)}, u32[]{:S(2)}) collective-permute-start(bf16[144,768]{1,0:T(8,128)(2,1)S(1)} %get-tuple-element.204.refs_2_), channel_id=1, source_target_pairs={{0,1},{1,0},{2,3},{3,2},{4,5},{5,4},{6,7},{7,6},{8,9},{9,8},{10,11... | collective-permute-start | bytes 663560 | tf_op jit(solution)/shard_map/ppermute | solution.py:1270
  56.8 13.2 %collective-permute-start.10 = (bf16[80,768]{1,0:T(8,128)(2,1)S(1)}, bf16[80,768]{1,0:T(8,128)(2,1)S(1)}, u32[]{:S(2)}, u32[]{:S(2)}) collective-permute-start(bf16[80,768]{1,0:T(8,128)(2,1)S(1)} %get-tuple-element.200.refs_2_), channel_id=1, source_target_pairs={{0,1},{1,0},{2,3},{3,2},{4,5},{5,4},{6,7},{7,6},{8,9},{9,8},{10,11... | collective-permute-start | bytes 368648 | tf_op jit(solution)/shard_map/ppermute | solution.py:1270
  67.3 6.9 %collective-permute-start.14 = (bf16[144,768]{1,0:T(8,128)(2,1)S(1)}, bf16[144,768]{1,0:T(8,128)(2,1)S(1)}, u32[]{:S(2)}, u32[]{:S(2)}) collective-permute-start(bf16[144,768]{1,0:T(8,128)(2,1)S(1)} %get-tuple-element.217.refs_2_), channel_id=1, source_target_pairs={{0,1},{1,0},{2,3},{3,2},{4,5},{5,4},{6,7},{7,6},{8,9},{9,8},{10,11... | collective-permute-start | bytes 663560 | tf_op jit(solution)/shard_map/ppermute | solution.py:1270
  69.1 15.2 %collective-permute-start.15 = (bf16[224,768]{1,0:T(8,128)(2,1)S(1)}, bf16[224,768]{1,0:T(8,128)(2,1)S(1)}, u32[]{:S(2)}, u32[]{:S(2)}) collective-permute-start(bf16[224,768]{1,0:T(8,128)(2,1)S(1)} %copy-done.77), channel_id=1, source_target_pairs={{0,2},{2,0},{4,6},{6,4},{8,10},{10,8},{12,14},{14,12},{1,3},{3,1},... | collective-permute-start | bytes 1032200 | tf_op jit(solution)/shard_map/ppermute | solution.py:1270
  77.2 12.4 %collective-permute-start.18 = (bf16[144,1536]{1,0:T(8,128)(2,1)}, bf16[144,1536]{1,0:T(8,128)(2,1)S(1)}, u32[]{:S(2)}, u32[]{:S(2)}) collective-permute-start(bf16[144,1536]{1,0:T(8,128)(2,1)} %get-tuple-element.228), channel_id=1, source_target_pairs={{0,2},{2,0},{4,6},{6,4},{8,10},{10,8},{12,14},{14,12},{1,3},{3,1},... | collective-permute-start | bytes 1327112 | tf_op jit(solution)/shard_map/ppermute | solution.py:1270
  78.2 6.1 %collective-permute-start.13 = (bf16[80,768]{1,0:T(8,128)(2,1)S(1)}, bf16[80,768]{1,0:T(8,128)(2,1)S(1)}, u32[]{:S(2)}, u32[]{:S(2)}) collective-permute-start(bf16[80,768]{1,0:T(8,128)(2,1)S(1)} %get-tuple-element.213.refs_2_), channel_id=1, source_target_pairs={{0,1},{1,0},{2,3},{3,2},{4,5},{5,4},{6,7},{7,6},{8,9},{9,8},{10,11... | collective-permute-start | bytes 368648 | tf_op jit(solution)/shard_map/ppermute | solution.py:1270
  78.8 9.8 %collective-permute-start.17 = (bf16[144,768]{1,0:T(8,128)(2,1)S(1)}, bf16[144,768]{1,0:T(8,128)(2,1)S(1)}, u32[]{:S(2)}, u32[]{:S(2)}) collective-permute-start(bf16[144,768]{1,0:T(8,128)(2,1)S(1)} %get-tuple-element.219.refs_8_.refs_2_), channel_id=1, source_target_pairs={{0,1},{1,0},{2,3},{3,2},{4,5},{5,4},{6,7},{7,6},{8,9},{9,8},{10,11... | collective-permute-start | bytes 663560 | tf_op jit(solution)/shard_map/ppermute | solution.py:1270
  86.9 9.7 %collective-permute-start.19 = (bf16[80,1536]{1,0:T(8,128)(2,1)}, bf16[80,1536]{1,0:T(8,128)(2,1)S(1)}, u32[]{:S(2)}, u32[]{:S(2)}) collective-permute-start(bf16[80,1536]{1,0:T(8,128)(2,1)} %get-tuple-element.232), channel_id=1, source_target_pairs={{0,2},{2,0},{4,6},{6,4},{8,10},{10,8},{12,14},{14,12},{1,3},{3,1},... | collective-permute-start | bytes 737288 | tf_op jit(solution)/shard_map/ppermute | solution.py:1270
  87.8 8.9 %collective-permute-start.16 = (bf16[80,768]{1,0:T(8,128)(2,1)S(1)}, bf16[80,768]{1,0:T(8,128)(2,1)S(1)}, u32[]{:S(2)}, u32[]{:S(2)}) collective-permute-start(bf16[80,768]{1,0:T(8,128)(2,1)S(1)} %get-tuple-element.224.refs_2_), channel_id=1, source_target_pairs={{0,1},{1,0},{2,3},{3,2},{4,5},{5,4},{6,7},{7,6},{8,9},{9,8},{10,11... | collective-permute-start | bytes 368648 | tf_op jit(solution)/shard_map/ppermute | solution.py:1270
  95.4 8.4 %collective-permute-start.21 = (bf16[144,768]{1,0:T(8,128)(2,1)S(1)}, bf16[144,768]{1,0:T(8,128)(2,1)S(1)}, u32[]{:S(2)}, u32[]{:S(2)}) collective-permute-start(bf16[144,768]{1,0:T(8,128)(2,1)S(1)} %get-tuple-element.240.refs_4_), channel_id=1, source_target_pairs={{0,1},{1,0},{2,3},{3,2},{4,5},{5,4},{6,7},{7,6},{8,9},{9,8},{10,11... | collective-permute-start | bytes 663560 | tf_op jit(solution)/shard_map/ppermute | solution.py:1270
  100.9 7.1 %collective-permute-start.20 = (bf16[80,768]{1,0:T(8,128)(2,1)S(1)}, bf16[80,768]{1,0:T(8,128)(2,1)S(1)}, u32[]{:S(2)}, u32[]{:S(2)}) collective-permute-start(bf16[80,768]{1,0:T(8,128)(2,1)S(1)} %get-tuple-element.234.refs_4_), channel_id=1, source_target_pairs={{0,1},{1,0},{2,3},{3,2},{4,5},{5,4},{6,7},{7,6},{8,9},{9,8},{10,11... | collective-permute-start | bytes 368648 | tf_op jit(solution)/shard_map/ppermute | solution.py:1270
  101.8 9.9 %collective-permute-start.24 = (bf16[80,1536]{1,0:T(8,128)(2,1)}, bf16[80,1536]{1,0:T(8,128)(2,1)S(1)}, u32[]{:S(2)}, u32[]{:S(2)}) collective-permute-start(bf16[80,1536]{1,0:T(8,128)(2,1)} %get-tuple-element.259), channel_id=1, source_target_pairs={{0,2},{2,0},{4,6},{6,4},{8,10},{10,8},{12,14},{14,12},{1,3},{3,1},... | collective-permute-start | bytes 737288 | tf_op jit(solution)/shard_map/ppermute | solution.py:1270
  103.3 9.8 %collective-permute-start.25 = (bf16[144,1536]{1,0:T(8,128)(2,1)S(1)}, bf16[144,1536]{1,0:T(8,128)(2,1)S(1)}, u32[]{:S(2)}, u32[]{:S(2)}) collective-permute-start(bf16[144,1536]{1,0:T(8,128)(2,1)S(1)} %copy-done.75), channel_id=1, source_target_pairs={{0,2},{2,0},{4,6},{6,4},{8,10},{10,8},{12,14},{14,12},{1,3},{3,1},... | collective-permute-start | bytes 1327112 | tf_op jit(solution)/shard_map/ppermute | solution.py:1270
  119.1 102.3 %reduce-scatter.6.cloned.1.call-start = ((), (), s32[]{:S(2)}) async-start(), calls=%async_computation.4 | async-start | bytes 3981312 | tf_op jit(solution)/shard_map/reduce_scatter | solution.py:1445
  120.0 10.4 %collective-permute-start.26 = (bf16[224,768]{1,0:T(8,128)(2,1)S(1)}, bf16[224,768]{1,0:T(8,128)(2,1)S(1)}, u32[]{:S(2)}, u32[]{:S(2)}) collective-permute-start(bf16[224,768]{1,0:T(8,128)(2,1)S(1)} %copy-done.48), channel_id=1, source_target_pairs={{0,2},{2,0},{4,6},{6,4},{8,10},{10,8},{12,14},{14,12},{1,3},{3,1},... | collective-permute-start | bytes 1032200 | tf_op jit(solution)/shard_map/ppermute | solution.py:1270
  121.7 8.7 %collective-permute-start.23 = (bf16[144,768]{1,0:T(8,128)(2,1)S(1)}, bf16[144,768]{1,0:T(8,128)(2,1)S(1)}, u32[]{:S(2)}, u32[]{:S(2)}) collective-permute-start(bf16[144,768]{1,0:T(8,128)(2,1)S(1)} %copy-done.81), channel_id=1, source_target_pairs={{0,1},{1,0},{2,3},{3,2},{4,5},{5,4},{6,7},{7,6},{8,9},{9,8},{10,11... | collective-permute-start | bytes 663560 | tf_op jit(solution)/shard_map/ppermute | solution.py:1270
  123.4 7.0 %collective-permute-start.22 = (bf16[80,768]{1,0:T(8,128)(2,1)S(1)}, bf16[80,768]{1,0:T(8,128)(2,1)S(1)}, u32[]{:S(2)}, u32[]{:S(2)}) collective-permute-start(bf16[80,768]{1,0:T(8,128)(2,1)S(1)} %copy-done.82), channel_id=1, source_target_pairs={{0,1},{1,0},{2,3},{3,2},{4,5},{5,4},{6,7},{7,6},{8,9},{9,8},{10,11... | collective-permute-start | bytes 368648 | tf_op jit(solution)/shard_map/ppermute | solution.py:1270
  123.7 23.5 %collective-permute-start.28 = (bf16[224,1536]{1,0:T(8,128)(2,1)S(1)}, bf16[224,1536]{1,0:T(8,128)(2,1)S(1)}, u32[]{:S(2)}, u32[]{:S(2)}) collective-permute-start(bf16[224,1536]{1,0:T(8,128)(2,1)S(1)} %copy-done.73), channel_id=1, source_target_pairs={{0,2},{2,0},{4,6},{6,4},{8,10},{10,8},{12,14},{14,12},{1,3},{3,1},... | collective-permute-start | bytes 2064392 | tf_op jit(solution)/shard_map/ppermute | solution.py:1270
  139.7 7.6 %collective-permute-start.27 = (bf16[224,768]{1,0:T(8,128)(2,1)S(1)}, bf16[224,768]{1,0:T(8,128)(2,1)S(1)}, u32[]{:S(2)}, u32[]{:S(2)}) collective-permute-start(bf16[224,768]{1,0:T(8,128)(2,1)S(1)} %get-tuple-element.264.refs_6_), channel_id=1, source_target_pairs={{0,1},{1,0},{2,3},{3,2},{4,5},{5,4},{6,7},{7,6},{8,9},{9,8},{10,11... | collective-permute-start | bytes 1032200 | tf_op jit(solution)/shard_map/ppermute | solution.py:1270
  142.0 13.2 %collective-permute-start.31 = (bf16[224,1536]{1,0:T(8,128)(2,1)}, bf16[224,1536]{1,0:T(8,128)(2,1)S(1)}, u32[]{:S(2)}, u32[]{:S(2)}) collective-permute-start(bf16[224,1536]{1,0:T(8,128)(2,1)} %get-tuple-element.288.refs_13_), channel_id=1, source_target_pairs={{0,2},{2,0},{4,6},{6,4},{8,10},{10,8},{12,14},{14,12},{1,3},{3,1},... | collective-permute-start | bytes 2064392 | tf_op jit(solution)/shard_map/ppermute | solution.py:1270
  161.5 133.1 %reduce-scatter.8.cloned.1.call-start = ((), (), s32[]{:S(2)}) async-start(), calls=%async_computation.5 | async-start | bytes 4423680 | tf_op jit(solution)/shard_map/reduce_scatter | solution.py:1602
  162.4 7.3 %collective-permute-start.30 = (bf16[224,768]{1,0:T(8,128)(2,1)S(1)}, bf16[224,768]{1,0:T(8,128)(2,1)S(1)}, u32[]{:S(2)}, u32[]{:S(2)}) collective-permute-start(bf16[224,768]{1,0:T(8,128)(2,1)S(1)} %copy-done.78), channel_id=1, source_target_pairs={{0,1},{1,0},{2,3},{3,2},{4,5},{5,4},{6,7},{7,6},{8,9},{9,8},{10,11... | collective-permute-start | bytes 1032200 | tf_op jit(solution)/shard_map/ppermute | solution.py:1270
  164.4 18.7 %collective-permute-start.29 = (bf16[224,1920]{1,0:T(8,128)(2,1)S(1)}, bf16[224,1920]{1,0:T(8,128)(2,1)S(1)}, u32[]{:S(2)}, u32[]{:S(2)}) collective-permute-start(bf16[224,1920]{1,0:T(8,128)(2,1)S(1)} %copy-done.70), channel_id=1, source_target_pairs={{0,2},{2,0},{4,6},{6,4},{8,10},{10,8},{12,14},{14,12},{1,3},{3,1},... | collective-permute-start | bytes 2580488 | tf_op jit(solution)/shard_map/ppermute | solution.py:1270
  181.3 11.2 %collective-permute-start.32 = (bf16[224,1536]{1,0:T(8,128)(2,1)}, bf16[224,1536]{1,0:T(8,128)(2,1)S(1)}, u32[]{:S(2)}, u32[]{:S(2)}) collective-permute-start(bf16[224,1536]{1,0:T(8,128)(2,1)} %get-tuple-element.291.refs_13_), channel_id=1, source_target_pairs={{0,2},{2,0},{4,6},{6,4},{8,10},{10,8},{12,14},{14,12},{1,3},{3,1},... | collective-permute-start | bytes 2064392 | tf_op jit(solution)/shard_map/ppermute | solution.py:1270
  200.1 6.5 %collective-permute-start.33 = (bf16[384,4608]{1,0:T(8,128)(2,1)}, bf16[384,4608]{1,0:T(8,128)(2,1)S(1)}, u32[]{:S(2)}, u32[]{:S(2)}) collective-permute-start(bf16[384,4608]{1,0:T(8,128)(2,1)} %get-tuple-element.294), channel_id=1, source_target_pairs={{0,16},{16,0},{1,17},{17,1},{2,18},{18,2},{3,19},{19,3},{4,20},{20... | collective-permute-start | bytes 10616840 | tf_op jit(solution)/shard_map/ppermute | solution.py:1270
  225.1 1.4 collective-permute-start.38
  226.5 4.9 %collective-permute-start.39 = (f32[25,768]{1,0:T(8,128)S(1)}, f32[25,768]{1,0:T(8,128)S(1)}, u32[]{:S(2)}, u32[]{:S(2)}) collective-permute-start(f32[25,768]{1,0:T(8,128)S(1)} %fusion.2), channel_id=1, source_target_pairs={{0,2},{2,0},{4,6},{6,4},{8,10},{10,8},{12,14},{14,12},{1,3},{3,1},... | collective-permute-start | bytes 230408 | tf_op jit(solution)/shard_map/ppermute | solution.py:1270
  231.4 9.1 %collective-permute-start.40 = (f32[25,768]{1,0:T(8,128)S(1)}, f32[25,768]{1,0:T(8,128)S(1)}, u32[]{:S(2)}, u32[]{:S(2)}) collective-permute-start(f32[25,768]{1,0:T(8,128)S(1)} %add.162), channel_id=1, source_target_pairs={{0,4},{2,6},{4,0},{6,2},{8,12},{10,14},{12,8},{14,10},{1,5},{3,7},... | collective-permute-start | bytes 230408 | tf_op jit(solution)/shard_map/ppermute | solution.py:1270
  240.5 11.8 %collective-permute-start.41 = (f32[25,768]{1,0:T(8,128)S(1)}, f32[25,768]{1,0:T(8,128)S(1)}, u32[]{:S(2)}, u32[]{:S(2)}) collective-permute-start(f32[25,768]{1,0:T(8,128)S(1)} %add.163), channel_id=1, source_target_pairs={{0,8},{2,10},{4,12},{6,14},{8,0},{10,2},{12,4},{14,6},{1,9},{3,11}... | collective-permute-start | bytes 230408 | tf_op jit(solution)/shard_map/ppermute | solution.py:1270
  242.5 25.4 %collective-permute-start.37 = (bf16[224,768]{1,0:T(8,128)(2,1)S(1)}, bf16[224,768]{1,0:T(8,128)(2,1)S(1)}, u32[]{:S(2)}, u32[]{:S(2)}) collective-permute-start(bf16[224,768]{1,0:T(8,128)(2,1)S(1)} %copy-done.47), channel_id=1, source_target_pairs={{0,1},{1,0},{2,3},{3,2},{4,5},{5,4},{6,7},{7,6},{8,9},{9,8},{10,11... | collective-permute-start | bytes 1032200 | tf_op jit(solution)/shard_map/ppermute | solution.py:1270
  252.4 8.9 %collective-permute-start.34 = (bf16[96,1536]{1,0:T(8,128)(2,1)S(1)}, bf16[96,1536]{1,0:T(8,128)(2,1)S(1)}, u32[]{:S(2)}, u32[]{:S(2)}) collective-permute-start(bf16[96,1536]{1,0:T(8,128)(2,1)S(1)} %dynamic-slice_bitcast_fusion), channel_id=1, source_target_pairs={{0,2},{2,0},{4,6},{6,4},{8,10},{10,8},{12,14},{14,12},{1,3},{3,1},... | collective-permute-start | bytes 884744 | tf_op jit(solution)/shard_map/ppermute | solution.py:1270
  261.4 8.1 %collective-permute-start.35 = (bf16[96,3072]{1,0:T(8,128)(2,1)S(1)}, bf16[96,3072]{1,0:T(8,128)(2,1)}, u32[]{:S(2)}, u32[]{:S(2)}) collective-permute-start(bf16[96,3072]{1,0:T(8,128)(2,1)S(1)} %pad_maximum_fusion.refs_1_), channel_id=1, source_target_pairs={{0,16},{1,17},{2,18},{3,19},{4,20},{5,21},{6,22},{7,23},{8,24},{9,... | collective-permute-start | bytes 1769480 | tf_op jit(solution)/shard_map/ppermute | solution.py:1683
  264.1 5.4 %collective-permute-start.36 = (bf16[96,1536]{1,0:T(8,128)(2,1)S(1)}, bf16[96,1536]{1,0:T(8,128)(2,1)S(1)}, u32[]{:S(2)}, u32[]{:S(2)}) collective-permute-start(bf16[96,1536]{1,0:T(8,128)(2,1)S(1)} %slice.94), channel_id=1, source_target_pairs={{0,16},{1,17},{2,18},{3,19},{4,20},{5,21},{6,22},{7,23},{8,24},{9,... | collective-permute-start | bytes 884744 | tf_op jit(solution)/shard_map/ppermute | solution.py:1683
  294.5 4.5 %collective-permute-start.42 = (bf16[96,4608]{1,0:T(8,128)(2,1)}, bf16[96,4608]{1,0:T(8,128)(2,1)S(1)}, u32[]{:S(2)}, u32[]{:S(2)}) collective-permute-start(bf16[96,4608]{1,0:T(8,128)(2,1)} %reduce-scatter.8.cloned.1.call-done.refs_5_), channel_id=1, source_target_pairs={{16,0},{17,1},{18,2},{19,3},{20,4},{21,5},{22,6},{23,7},{24,8},{25... | collective-permute-start | bytes 2654216 | tf_op jit(solution)/shard_map/ppermute | solution.py:1699
  (85 other events, 926.5 us)
Sparse Core Ops, SparseCore 0:
  119.2 56.8 reduce-scatter.3
  178.4 42.8 reduce-scatter.5
  223.8 70.7 reduce-scatter.7
